TPU v7x, 512 devices: a whole 4x8x8 slice. The times are simulated.
512 devices in a mesh: pb: 64 (over y, z), row: 4 (over x), col: 2 (over core).
Axes of the slice: x: 4, y: 8, z: 8, core: 2. Of those that a mesh axis runs over, the one named last changes fastest.
Arguments:
- amplitudes: bfloat16 [64, 20, 4, 9216], P('pb'), may hold values from -6 to 6
- pairs: int32 [64, 4, 2], P('pb'), may hold values from 0 to 63
- stored_k: int32 [64], replicated, may hold values from 0 to 63, each once
- orbitals: bfloat16 [64, 192, 2048], P('pb', None, ('row', 'col')), may hold values from -1.078125 to 1.078125
- valence_energy: float32 [64, 96], replicated, may hold values from -1 to 0
- conduction_energy: float32 [64, 96], replicated, may hold values from 2.5 to 3.5
- screened: bfloat16 [64, 2048, 2048], P('pb', 'row', 'col'), may hold values from -0.125 to 0.125
Outputs:
- filtered: bfloat16 [64, 20, 4, 9216], P('pb')
Inputs may be any that keep to these rules, and one draw needn't show every extreme that they name: stored_k holds every k-point exactly once; row s of orbitals belongs to k-point stored_k[s]. `pairs`: each entry is a k-point.
All inputs are finite; a program needn't handle non-finite values.
Results may differ from a plain program's by a relative error of at most 0.024.
Values may be sent and summed in bfloat16 or wider, within the bound.
No kernel may reach another device: no remote copies, remote signals or barrier semaphores. Data moves between devices by JAX's collectives and lax.ppermute only.
A program may use at most 64 MiB of HBM per device.

v0:
```python
import jax
import jax.numpy as jnp
from jax import lax
from jax.sharding import PartitionSpec as P

CENTER = 3.0
HALF = 2.5


def on_device(amplitudes, pairs, stored_k, orbitals, valence_energy, conduction_energy, screened):
    amplitude = amplitudes[0]
    pair_list = pairs[0]
    w_tile = screened[0]
    count_v = valence_energy.shape[1]
    count_c = conduction_energy.shape[1]
    vectors, pair_count, flat_size = amplitude.shape
    points = orbitals.shape[2]
    col_width = w_tile.shape[1]
    column = lax.axis_index("col")

    def pick(shard_piece):
        pick_low = (stored_k[None, :] == pair_list[:, 0:1]).astype(jnp.bfloat16)
        pick_high = (stored_k[None, :] == pair_list[:, 1:2]).astype(jnp.bfloat16)
        low_bands = jnp.einsum(
            "pl,lbr->pbr", pick_low, shard_piece[:, :count_v], preferred_element_type=jnp.float32
        )
        high_bands = jnp.einsum(
            "pl,lbr->pbr", pick_high, shard_piece[:, count_v:], preferred_element_type=jnp.float32
        )
        return (low_bands, high_bands)

    def fetch_each():
        found = pick(lax.all_gather(orbitals, "pb", axis=0, tiled=True))
        return (found[0].astype(jnp.bfloat16), found[1].astype(jnp.bfloat16))

    low_energy = jnp.take(valence_energy, pair_list[:, 0], axis=0)
    high_energy = jnp.take(conduction_energy, pair_list[:, 1], axis=0)
    gap_grid = (high_energy[:, None, :] - low_energy[:, :, None]).reshape(pair_count, flat_size)
    gap_rows = jnp.tile(gap_grid, (vectors, 1))

    def kernel_term(current, bands):
        valence, conduction_orbital = bands
        amplitude_lattice = current.reshape(vectors, pair_count, count_v, count_c)
        inner_total_sum = jnp.einsum(
            "iomx,oxj->iomj",
            amplitude_lattice,
            conduction_orbital,
            preferred_element_type=jnp.float32,
        )
        values = jnp.sum(valence.astype(jnp.float32)[None] * inner_total_sum, axis=2)
        values = values.astype(jnp.bfloat16).reshape(vectors * pair_count, points)
        everywhere = lax.all_gather(values, ("row", "col"), axis=1, tiled=True)
        needed = lax.dynamic_slice_in_dim(everywhere, column * col_width, col_width, 1)
        partial_value = lax.dot_general(
            needed, w_tile, (((1,), (1,)), ((), ())), preferred_element_type=jnp.float32
        )
        own_sums = (
            lax.psum_scatter(
                partial_value.astype(jnp.bfloat16), "col", scatter_dimension=1, tiled=True
            )
            .astype(jnp.float32)
            .reshape(vectors, pair_count, points)
        )
        weighted_product = (valence.astype(jnp.float32)[None] * own_sums[:, :, None, :]).astype(
            jnp.bfloat16
        )
        projected = jnp.einsum(
            "kyqz,yhz->kyqh",
            weighted_product,
            conduction_orbital,
            preferred_element_type=jnp.float32,
        )
        return projected.reshape(vectors * pair_count, flat_size)

    def advance(current_rows, summed, gap_part, previous_rows, factor):
        value = (gap_part * current_rows + summed - CENTER * current_rows) / HALF
        if previous_rows is None:
            return value.astype(jnp.bfloat16)
        return (factor * value - previous_rows).astype(jnp.bfloat16)

    def finish(partial_term, current, previous, factor):
        summed = lax.psum(partial_term.astype(jnp.bfloat16), ("row", "col")).astype(jnp.float32)
        previous_full = None
        if previous is not None:
            previous_full = previous.astype(jnp.float32)
        return advance(current.astype(jnp.float32), summed, gap_rows, previous_full, factor)

    initial = amplitude.reshape(vectors * pair_count, flat_size)
    first_bands = fetch_each()
    first_term = finish(kernel_term(initial, first_bands), initial, None, 1.0)
    second_bands = fetch_each()
    second_term = finish(kernel_term(first_term, second_bands), first_term, initial, 2.0)
    return second_term.reshape(1, vectors, pair_count, flat_size)


def solution(mesh):
    return jax.shard_map(
        on_device,
        mesh=mesh,
        in_specs=(
            P("pb", None, None, None),
            P("pb", None, None),
            P(),
            P("pb", None, ("row", "col")),
            P(),
            P(),
            P("pb", "row", "col"),
        ),
        out_specs=P("pb", None, None, None),
        check_vma=False,
    )
```

profile of v0, /device:TPU:1, one launch (start us, length us, event | category | flops | bytes accessed | tf_op | source)
XLA Modules:
  0.0 364.3 jit_solution(16499442433685016366)
XLA Ops:
  6.5 0.0 copy-start
  6.5 0.0 copy-start.1
  6.5 0.0 all-gather.2.cloned.1.call-start
  6.5 0.7 all-gather.2.cloned.1.call-update
  7.3 0.0 reduce-scatter.3.cloned.1.call-start
  7.3 4.4 %reshape_reshape_squeeze.3 = bf16[20,4,96,96]{3,2,1,0:T(8,128)(2,1)} reshape(bf16[1,20,4,9216]{3,2,1,0:T(4,128)(2,1)} %param.9) | data formatting | bytes 2949120 | tf_op jit(solution)/shard_map/reshape;reshape;squeeze | solution.py:43
  11.8 0.0 copy-done.1
  11.8 0.0 copy-start.7
  11.8 1.7 reshape.48
  13.5 0.0 copy-done.7
  13.5 0.0 copy-start.8
  13.5 92.5 %all-gather.2.cloned.1.call-done = bf16[64,192,256]{2,1,0:T(8,128)(2,1)} async-done(((bf16[1,192,256]{2,1,0:T(8,128)(2,1)}), bf16[64,192,256]{2,1,0:T(8,128)(2,1)}) %all-gather.2.cloned.1.call-update) | async-done | bytes 6291472 | tf_op jit(solution)/shard_map/all_gather | solution.py:33
  106.0 3.3 fusion.49
  109.4 0.0 copy-done.8
  109.4 1.8 fusion.25
  111.2 0.0 copy-start.2
  111.2 0.1 copy.59
  111.2 1.8 fusion.28
  113.0 0.0 copy-done.2
  113.0 1.2 fusion.1
  114.3 14.4 %all_gather.11 = bf16[80,2048]{1,0:T(8,128)(2,1)S(1)} all-gather(bf16[80,256]{1,0:T(8,128)(2,1)S(1)} %convert_element_type.92), channel_id=1, replica_groups=mesh['pb'=64,'row'=4,'col'=2] {'row','col'}, dimensions={1}, use_global_device_ids=true | all-gather | bytes 368640 | tf_op jit(solution)/shard_map/all_gather | solution.py:52
  128.7 0.0 copy-done
  128.7 1.1 convolution_convert_fusion.1
  129.8 0.0 reduce-scatter.3.cloned.1.call-update
  129.8 0.0 all-reduce.3.cloned.1.call-start
  129.9 12.7 %reduce-scatter.3.cloned.1.call-done = bf16[80,256]{1,0:T(8,128)(2,1)} async-done(((bf16[80,512]{1,0:T(8,128)(2,1)}), bf16[80,256]{1,0:T(8,128)(2,1)}) %reduce-scatter.3.cloned.1.call-update) | async-done | bytes 40976 | tf_op jit(solution)/shard_map/reduce_scatter | solution.py:58
  142.6 0.8 reshape.49
  143.4 0.0 copy-done.3
  143.4 2.9 convert_bitcast_fusion.1
  146.3 3.2 copy.65
  149.5 0.0 copy-start.5
  149.5 0.0 copy-start.6
  149.5 3.6 convert_element_type.97
  153.1 0.0 all-reduce.3.cloned.1.call-update
  153.1 0.2 reduce-scatter.5.cloned.1.call-start
  153.3 0.0 copy-done.5
  153.3 0.6 gather_fusion.1
  153.9 0.0 copy-done.6
  153.9 0.6 gather_fusion
  154.5 0.1 broadcast_select_fusion
  154.5 0.1 broadcast_select_fusion.1
  154.6 0.1 broadcast_subtract_fusion
  154.7 0.2 sub.32
  154.9 2.2 tile.8
  157.2 4.3 %tile.9 = f32[80,9216]{1,0:T(8,128)} reshape(f32[20,4,9216]{2,1,0:T(4,128)} %tile.8) | data formatting | bytes 5898240 | tf_op jit(solution)/shard_map/tile | solution.py:39
  161.4 64.5 %all-reduce.3.cloned.1.call-done = bf16[80,9216]{1,0:T(8,128)(2,1)} async-done(((bf16[80,9216]{1,0:T(8,128)(2,1)}), bf16[80,9216]{1,0:T(8,128)(2,1)}) %all-reduce.3.cloned.1.call-update) | async-done | bytes 1474576 | tf_op jit(solution)/shard_map/psum | solution.py:82
  226.0 3.8 %multiply_convert_fusion.4 = bf16[80,9216]{1,0:T(8,128)(2,1)S(1)} fusion(f32[80,9216]{1,0:T(8,128)} %reshape.48, bf16[80,9216]{1,0:T(8,128)(2,1)} %all-reduce.3.cloned.1.call-done, f32[80,9216]{1,0:T(8,128)} %tile.9), kind=kLoop, calls=%fused_computation.25 | loop fusion | flops 5160960 | bytes 8847360 | tf_op jit(solution)/shard_map/convert_element_type | solution.py:78
  229.8 0.0 copy-start.4
  229.8 2.9 reshape.46
  232.7 0.0 copy-done.4
  232.7 2.7 fusion
  235.5 15.1 %all_gather.12 = bf16[80,2048]{1,0:T(8,128)(2,1)S(1)} all-gather(bf16[80,256]{1,0:T(8,128)(2,1)S(1)} %convert_element_type.102), channel_id=1, replica_groups=mesh['pb'=64,'row'=4,'col'=2] {'row','col'}, dimensions={1}, use_global_device_ids=true | all-gather | bytes 368640 | tf_op jit(solution)/shard_map/all_gather | solution.py:52
  250.6 1.1 convolution_convert_fusion
  251.6 0.0 reduce-scatter.5.cloned.1.call-update
  251.7 0.0 all-reduce.5.cloned.1.call-start
  251.7 16.5 %reduce-scatter.5.cloned.1.call-done = bf16[80,256]{1,0:T(8,128)(2,1)} async-done(((bf16[80,512]{1,0:T(8,128)(2,1)}), bf16[80,256]{1,0:T(8,128)(2,1)}) %reduce-scatter.5.cloned.1.call-update) | async-done | bytes 40976 | tf_op jit(solution)/shard_map/reduce_scatter | solution.py:58
  268.2 0.8 reshape.50
  269.0 2.9 convert_bitcast_fusion
  271.9 3.2 copy.71
  275.1 3.6 convert_element_type.107
  278.7 0.0 all-reduce.5.cloned.1.call-update
  278.7 72.8 %all-reduce.5.cloned.1.call-done = bf16[80,9216]{1,0:T(8,128)(2,1)} async-done(((bf16[80,9216]{1,0:T(8,128)(2,1)}), bf16[80,9216]{1,0:T(8,128)(2,1)}) %all-reduce.5.cloned.1.call-update) | async-done | bytes 1474576 | tf_op jit(solution)/shard_map/psum | solution.py:82
  351.5 4.8 %fusion.16 = bf16[80,9216]{1,0:T(8,128)(2,1)S(1)} fusion(f32[80,9216]{1,0:T(8,128)} %reshape.48, f32[80,9216]{1,0:T(8,128)} %tile.9, bf16[80,9216]{1,0:T(8,128)(2,1)} %all-reduce.5.cloned.1.call-done, bf16[80,9216]{1,0:T(8,128)(2,1)} %all-reduce.3.cloned.1.call-done), kind=kLoop, calls=%fused_computation.24 | loop fusion | flops 11796480 | bytes 10321920 | tf_op jit(solution)/shard_map/convert_element_type | solution.py:79
  356.4 1.4 reshape.47
  (10 shorter events, 0.1 us)
Async XLA Ops:
  6.5 122.2 %copy-start = (bf16[1,512,1024]{2,1,0:T(8,128)(2,1)S(1)}, bf16[1,512,1024]{2,1,0:T(8,128)(2,1)}, u32[]{:S(2)}) copy-start(bf16[1,512,1024]{2,1,0:T(8,128)(2,1)} %param.15) | copy-start | bytes 3145732
  6.5 5.2 %copy-start.1 = (bf16[1,20,4,9216]{3,2,1,0:T(4,128)(2,1)S(1)}, bf16[1,20,4,9216]{3,2,1,0:T(4,128)(2,1)}, u32[]{:S(2)}) copy-start(bf16[1,20,4,9216]{3,2,1,0:T(4,128)(2,1)} %param.9) | copy-start | bytes 4423684
  6.5 99.5 %all-gather.2.cloned.1.call-start = ((), (), s32[]{:S(2)}) async-start(), calls=%async_computation.2 | async-start | bytes 6389760 | tf_op jit(solution)/shard_map/all_gather | solution.py:33
  7.3 135.3 %reduce-scatter.3.cloned.1.call-start = ((), (), s32[]{:S(2)}) async-start(), calls=%async_computation.3 | async-start | bytes 122880 | tf_op jit(solution)/shard_map/reduce_scatter | solution.py:58
  11.8 1.7 copy-start.7
  13.5 95.8 %copy-start.8 = (s32[64]{0:T(128)S(1)}, s32[64]{0:T(128)}, u32[]{:S(2)}) copy-start(s32[64]{0:T(128)} %param.11) | copy-start | bytes 772
  111.2 1.9 copy-start.2
  113.0 30.4 %copy-start.3 = (bf16[4,96,256,1]{2,0,1,3:T(4,128)(2,1)}, bf16[4,96,256,1]{2,0,1,3:T(4,128)(2,1)S(1)}, u32[]{:S(2)}) copy-start(bf16[4,96,256,1]{2,0,1,3:T(4,128)(2,1)S(1)} %fusion.28) | copy-start | bytes 589828
  129.8 96.1 %all-reduce.3.cloned.1.call-start = ((), (), s32[]{:S(2)}) async-start(), calls=%async_computation.4 | async-start | bytes 2949120 | tf_op jit(solution)/shard_map/psum | solution.py:82
  149.5 3.8 %copy-start.5 = (f32[64,96]{1,0:T(8,128)S(1)}, f32[64,96]{1,0:T(8,128)}, u32[]{:S(2)}) copy-start(f32[64,96]{1,0:T(8,128)} %param.13) | copy-start | bytes 73732
  149.5 4.4 %copy-start.6 = (f32[64,96]{1,0:T(8,128)S(1)}, f32[64,96]{1,0:T(8,128)}, u32[]{:S(2)}) copy-start(f32[64,96]{1,0:T(8,128)} %param.14) | copy-start | bytes 73732
  153.1 115.1 %reduce-scatter.5.cloned.1.call-start = ((), (), s32[]{:S(2)}) async-start(), calls=%async_computation.5 | async-start | bytes 122880 | tf_op jit(solution)/shard_map/reduce_scatter | solution.py:58
  229.8 2.9 copy-start.4
  251.7 99.9 %all-reduce.5.cloned.1.call-start = ((), (), s32[]{:S(2)}) async-start(), calls=%async_computation.6 | async-start | bytes 2949120 | tf_op jit(solution)/shard_map/psum | solution.py:82
Sparse Core Ops, SparseCore 0:
  10.4 95.5 all-gather.1
  129.9 12.5 reduce-scatter.2
  153.2 72.7 all-reduce.2
  251.8 16.3 reduce-scatter.4
  278.8 72.6 all-reduce.4
where the time goes:
time: 366 us; the launch traced here: 364 us
  waiting for transfers between devices  260 us (71%)
  local copies, waits for them, and re-layouts  37 us (10%)
  blocking collectives  29.5 us (8%)
  matrix products  15.5 us (4%)
  between operations  13.3 us (4%)
  other arithmetic  8.91 us (2%)
    psum x2, waiting for transfers between devices, finish(): lax.psum(partial_term.astype(jnp.bfloat16), ('row', 'col'))  137 us
    all_gather x1, waiting for transfers between devices, fetch_each(): found = pick(lax.all_gather(orbitals, 'pb', axis=0, tiled=True))  92.5 us
    all_gather x2, blocking collectives, kernel_term(): everywhere = lax.all_gather(values, ('row', 'col'), axis=1, tiled=True)  29.5 us
    reduce_scatter x2, waiting for transfers between devices, kernel_term(): lax.psum_scatter(partial_value.astype(jnp.bfloat16), 'col', scatter_dimen...  29.1 us
    convert_element_type x4, local copies, waits for them, and re-layouts, finish(): partial_term.astype(jnp.bfloat16)  13.5 us
  transfers between devices with their start and end apart: 5, of which 5 were waited for; matrix products, arithmetic and copies ran while one was open for 4% of the time, Pallas kernels for 0%

commit v1 on v0

v1 whole, which is shorter than its diff:
```python
import jax
import jax.numpy as jnp
from jax import lax
from jax.experimental import pallas as pl
from jax.experimental.pallas import tpu as pltpu
from jax.sharding import PartitionSpec as P

CENTER = 3.0
HALF = 2.5
LANES = 128
ROWS = 8
VMEM_LIMIT = 56 * 1024 * 1024


def pack_kernel(pairs_ref, stored_ref, orbitals_ref, out_ref):
    targets = out_ref.shape[0]
    count = pairs_ref.shape[1]
    stored = stored_ref[...]
    place = lax.broadcasted_iota(jnp.int32, stored.shape, 1).astype(jnp.float32)
    lane = lax.broadcasted_iota(jnp.int32, (ROWS, LANES), 1)
    wanted = jnp.zeros((ROWS, LANES), jnp.float32)
    for half in range(2):
        for pair in range(count):
            hit = stored == pairs_ref[0, pair, half]
            row = jnp.sum(jnp.where(hit, place, 0.0), axis=1, keepdims=True)
            wanted = jnp.where(lane == half * count + pair, row, wanted)
    bands = orbitals_ref.shape[1]
    wide = orbitals_ref.shape[2] // LANES
    tiles = bands // ROWS * wide
    for target in range(targets):
        if target < tiles:
            group, side = target // wide, target % wide
            tile = orbitals_ref[0, group * ROWS : (group + 1) * ROWS, side * LANES : (side + 1) * LANES]
            tile = tile.astype(jnp.float32)
        else:
            tile = jnp.zeros((ROWS, LANES), jnp.float32)
        out_ref[target] = jnp.concatenate([tile, wanted], axis=0).astype(jnp.bfloat16)


def select_kernel(rows_ref, table_ref, out_ref):
    transfers, count = rows_ref.shape

    def one(transfer, carry):
        for pair in range(count):
            out_ref[transfer * count + pair] = table_ref[rows_ref[transfer, pair], :ROWS, :]
        return carry

    lax.fori_loop(0, transfers, one, 0, unroll=8)


def steps_kernel(column_ref, gap_ref, own_ref, other_ref, start_ref, w_ref, out_ref,
                 valence, conduction, w_all, screened_in, screened_out, total, first, sems):
    count_v = valence.shape[0]
    count_c = conduction.shape[0]
    points = valence.shape[1]
    tiles_w = w_ref.shape[0]
    rows_w, cols_w = w_ref.shape[1], w_ref.shape[2]
    wide_w = points // cols_w
    flat_rows = start_ref.shape[0]
    vectors = flat_rows // count_v
    padded = screened_in.shape[0]
    copies = [pltpu.make_async_copy(w_ref.at[t], w_all.at[t], sems.at[t]) for t in range(tiles_w)]
    for copy in copies:
        copy.start()

    even = column_ref[0] == 0
    wide = 2
    row_count = points // (2 * wide * LANES)

    def fetch(tile, block):
        row, core = block // 2, block % 2
        mine = own_ref[tile * row_count + row].astype(jnp.float32)
        theirs = other_ref[tile * row_count + row].astype(jnp.float32)
        return jnp.where(even, mine, theirs) if core == 0 else jnp.where(even, theirs, mine)

    for block in range(2 * row_count):
        for side in range(wide):
            lanes = slice((block * wide + side) * LANES, (block * wide + side + 1) * LANES)
            for pack in range(count_v // (2 * ROWS)):
                tile = [fetch((2 * pack + k) * wide + side, block) for k in range(2)]
                valence[2 * pack * ROWS : 2 * (pack + 1) * ROWS, lanes] = jnp.concatenate(tile, axis=0)
            base = count_v // ROWS
            for pack in range(count_c // (2 * ROWS)):
                tile = [fetch((base + 2 * pack + k) * wide + side, block) for k in range(2)]
                conduction[2 * pack * ROWS : 2 * (pack + 1) * ROWS, lanes] = jnp.concatenate(
                    tile, axis=0
                ).astype(jnp.bfloat16)

    screened_in[...] = jnp.zeros_like(screened_in)
    chunk = 256
    chunks = points // chunk

    def kernel_term(current_ref):
        def expand(step, carry):
            lanes = pl.ds(pl.multiple_of(step * chunk, chunk), chunk)
            inner = jnp.dot(current_ref[...], conduction[:, lanes], preferred_element_type=jnp.float32)
            inner = inner.reshape(vectors, count_v, chunk) * valence[:, lanes][None]
            screened_in[:vectors, lanes] = jnp.sum(inner, axis=1).astype(jnp.bfloat16).astype(jnp.float32)
            return carry

        lax.fori_loop(0, chunks, expand, 0)
        values = screened_in[...].astype(jnp.bfloat16)
        if current_ref is start_ref:
            for copy in copies:
                copy.wait()
        for row in range(tiles_w // wide_w):
            summed = jnp.zeros((padded, rows_w), jnp.float32)
            for col in range(wide_w):
                summed += lax.dot_general(
                    values[:, col * cols_w : (col + 1) * cols_w],
                    w_all[row * wide_w + col],
                    (((1,), (1,)), ((), ())),
                    preferred_element_type=jnp.float32,
                )
            screened_out[:, row * rows_w : (row + 1) * rows_w] = summed
        total[...] = jnp.zeros_like(total)

        def project(step, carry):
            lanes = pl.ds(pl.multiple_of(step * chunk, chunk), chunk)
            weighted = screened_out[:vectors, lanes][:, None, :] * valence[:, lanes][None]
            weighted = weighted.reshape(flat_rows, chunk).astype(jnp.bfloat16)
            total[...] += lax.dot_general(
                weighted,
                conduction[:, lanes],
                (((1,), (1,)), ((), ())),
                preferred_element_type=jnp.float32,
            )
            return carry

        lax.fori_loop(0, chunks, project, 0)

    gap = gap_ref[...][None]

    def scaled(current):
        parts = current.astype(jnp.float32).reshape(vectors, count_v, count_c)
        term = total[...].reshape(vectors, count_v, count_c)
        return ((gap * parts + term - CENTER * parts) / HALF).reshape(flat_rows, count_c)

    kernel_term(start_ref)
    first[...] = scaled(start_ref[...]).astype(jnp.bfloat16)
    kernel_term(first)
    out_ref[...] = (2.0 * scaled(first[...]) - start_ref[...].astype(jnp.float32)).astype(jnp.bfloat16)


def on_device(amplitudes, pairs, stored_k, orbitals, valence_energy, conduction_energy, screened):
    transfers = stored_k.shape[0]
    count_v = valence_energy.shape[1]
    count_c = conduction_energy.shape[1]
    vectors, pair_count, flat_size = amplitudes.shape[1:]
    member = lax.axis_index("pb")
    pair = lax.axis_index("row")
    column = lax.axis_index("col")
    cols = lax.axis_size("col")
    devices = lax.axis_size("row") * cols
    points = orbitals.shape[2] * devices
    share = vectors // cols
    smem = pl.BlockSpec(memory_space=pltpu.SMEM)
    vmem = pl.BlockSpec(memory_space=pltpu.VMEM)
    limit = pltpu.CompilerParams(vmem_limit_bytes=VMEM_LIMIT)

    w_tiles = lax.all_gather(screened[0], ("row", "col"))

    message = pl.pallas_call(
        pack_kernel,
        out_shape=jax.ShapeDtypeStruct((transfers, 2 * ROWS, LANES), jnp.bfloat16),
        in_specs=[smem, vmem, vmem],
        out_specs=vmem,
        compiler_params=limit,
    )(pairs, stored_k.reshape(1, transfers), orbitals)
    table = lax.all_to_all(message, "pb", 0, 0, tiled=True)
    wanted = table[:, ROWS, : 2 * pair_count].astype(jnp.int32)
    valence_tiles = count_v // ROWS * (orbitals.shape[2] // LANES)
    rows = jnp.where(member < valence_tiles, wanted[:, :pair_count], wanted[:, pair_count:])
    chosen = pl.pallas_call(
        select_kernel,
        out_shape=jax.ShapeDtypeStruct((transfers * pair_count, ROWS, LANES), jnp.bfloat16),
        in_specs=[smem, vmem],
        out_specs=vmem,
        compiler_params=limit,
    )(rows, table)
    own = lax.all_to_all(chosen, ("pb", "row"), 0, 0, tiled=True)
    other = lax.ppermute(own, "col", [(0, 1), (1, 0)])

    start = lax.dynamic_slice(
        amplitudes[0], (column * share, pair, 0), (share, 1, flat_size)
    ).reshape(share * count_v, count_c)
    listed = lax.dynamic_slice_in_dim(pairs[0], pair, 1, 0)
    low = lax.dynamic_slice_in_dim(valence_energy, listed[0, 0], 1, 0)
    high = lax.dynamic_slice_in_dim(conduction_energy, listed[0, 1], 1, 0)
    gap = high - low.reshape(count_v, 1)

    padded = 16
    flat_rows = share * count_v
    result = pl.pallas_call(
        steps_kernel,
        out_shape=jax.ShapeDtypeStruct((flat_rows, count_c), jnp.bfloat16),
        in_specs=[smem, vmem, vmem, vmem, vmem, pl.BlockSpec(memory_space=pl.ANY)],
        out_specs=vmem,
        scratch_shapes=[
            pltpu.VMEM((count_v, points), jnp.float32),
            pltpu.VMEM((count_c, points), jnp.bfloat16),
            pltpu.VMEM(w_tiles.shape, jnp.bfloat16),
            pltpu.VMEM((padded, points), jnp.float32),
            pltpu.VMEM((padded, points), jnp.float32),
            pltpu.VMEM((flat_rows, count_c), jnp.float32),
            pltpu.VMEM((flat_rows, count_c), jnp.bfloat16),
            pltpu.SemaphoreType.DMA((devices,)),
        ],
        compiler_params=limit,
    )(column.reshape(1), gap, own, other, start, w_tiles)

    mine = result.reshape(share, flat_size // LANES, LANES)
    across = lax.all_gather(mine, "row")
    theirs = lax.ppermute(across, "col", [(0, 1), (1, 0)])
    both = jnp.where(
        column == 0, jnp.stack([across, theirs]), jnp.stack([theirs, across])
    )
    return both.transpose(0, 2, 1, 3, 4).reshape(1, vectors, pair_count, flat_size)


def solution(mesh):
    return jax.shard_map(
        on_device,
        mesh=mesh,
        in_specs=(
            P("pb", None, None, None),
            P("pb", None, None),
            P(),
            P("pb", None, ("row", "col")),
            P(),
            P(),
            P("pb", "row", "col"),
        ),
        out_specs=P("pb", None, None, None),
        check_vma=False,
    )
```

time: 366 us -> 132 us (0.36)
  waiting for transfers between devices: 260 us -> 15.1 us
  local copies, waits for them, and re-layouts: 37 us -> 8.66 us
  starting transfers between devices: 0.35 us -> 27.6 us
  Pallas kernels: 0 us -> 21.3 us
  matrix products: 15.5 us -> 0 us
  blocking collectives: 29.5 us -> 40 us
  other arithmetic: 8.91 us -> 1.68 us
  between operations: 13.3 us -> 17.4 us
    psum x2 -> x0, waiting for transfers between devices: 137 us -> none  [finish(): lax.psum(partial_term.astype(jnp.bfloat16), ('row', 'col'))]
    all_gather x1, waiting for transfers between devices: 92.5 us -> 0.01 us  [on_device(): w_tiles = lax.all_gather(screened[0], ('row', 'col'))]
    reduce_scatter x2 -> x0, waiting for transfers between devices: 29.1 us -> none  [kernel_term(): lax.psum_scatter(partial_value.astype(jnp.bfloat16), 'col', scatter_dimen...]
    all_to_all x0 -> x1, blocking collectives: none -> 28.5 us  [on_device(): own = lax.all_to_all(chosen, ('pb', 'row'), 0, 0, tiled=True)]
    pallas_call x0 -> x3, Pallas kernels: none -> 21.3 us  [the longest x1 17.3 us: on_device(): pl.pallas_call(steps_kernel, out_shape=jax.ShapeDtypeStruct((flat_rows, c...]
    all_gather x2 -> x1, blocking collectives: 29.5 us -> 11.5 us  [on_device(): across = lax.all_gather(mine, 'row')]
    all_to_all x0 -> x1, starting transfers between devices: none -> 17.1 us  [on_device(): table = lax.all_to_all(message, 'pb', 0, 0, tiled=True)]
    dot_general x8 -> x0, matrix products: 15.5 us -> none  [the longest x2 5.8 us: kernel_term(): jnp.einsum('kyqz,yhz->kyqh', weighted_product, conduction_orbital, prefer...]
  transfers between devices with their start and end apart: 5 -> 4, of which waited for: 5 -> 2; matrix products, arithmetic and copies ran while one was open for 4% -> 5% of each run, Pallas kernels for 0% -> 3%
where the time goes in v1:
time: 132 us
  blocking collectives  40 us (30%)
  starting transfers between devices  27.6 us (21%)
  Pallas kernels  21.3 us (16%)
  between operations  17.4 us (13%)
  waiting for transfers between devices  15.1 us (11%)
  local copies, waits for them, and re-layouts  8.66 us (7%)
  other arithmetic  1.68 us (1%)
    all_to_all x1, blocking collectives, on_device(): own = lax.all_to_all(chosen, ('pb', 'row'), 0, 0, tiled=True)  28.5 us
    pallas_call x1, Pallas kernels, on_device(): pl.pallas_call(steps_kernel, out_shape=jax.ShapeDtypeStruct((flat_rows, c...  17.3 us
    all_to_all x1, starting transfers between devices, on_device(): table = lax.all_to_all(message, 'pb', 0, 0, tiled=True)  17.1 us
    all_to_all x1, waiting for transfers between devices, on_device(): table = lax.all_to_all(message, 'pb', 0, 0, tiled=True)  12.5 us
    all_gather x1, blocking collectives, on_device(): across = lax.all_gather(mine, 'row')  11.5 us
    ppermute x1, starting transfers between devices, on_device(): other = lax.ppermute(own, 'col', [(0, 1), (1, 0)])  5.92 us
    ppermute x1, starting transfers between devices, on_device(): theirs = lax.ppermute(across, 'col', [(0, 1), (1, 0)])  4.49 us
  transfers between devices with their start and end apart: 4, of which 2 were waited for; matrix products, arithmetic and copies ran while one was open for 5% of the time, Pallas kernels for 3%

profile of v1, /device:TPU:1, one launch (start us, length us, event | category | flops | bytes accessed | tf_op | source)
XLA Modules:
  0.0 131.7 jit_solution(32131175145504038)
XLA Ops:
  6.5 0.0 copy-start
  6.5 0.0 all-gather.2.cloned.1.call-start
  6.5 0.7 all-gather.2.cloned.1.call-update
  7.3 0.0 copy-start.4
  7.3 1.4 %copy.13.pairs_ref = s32[1,4,2]{2,1,0:T(4,128)} copy(s32[1,4,2]{1,2,0:T(2,128)} %param.8) | data formatting | bytes 64 | tf_op args[1]
  8.7 1.7 %shard_map.73 = bf16[64,16,128]{2,1,0:T(8,128)(2,1)} custom-call(s32[1,4,2]{2,1,0:T(4,128)} %copy.13.pairs_ref, s32[1,64]{1,0:T(1,128)} %bitcast.20, bf16[1,192,256]{2,1,0:T(8,128)(2,1)} %orbitals_ref.1), custom_call_target="tpu_custom_call" | custom-call | tf_op jit(solution)/shard_map/pallas_call | solution.py:163
  10.4 17.1 %all-to-all-start = ((bf16[64,16,128]{2,1,0:T(8,128)(2,1)}), bf16[64,16,128]{2,1,0:T(8,128)(2,1)S(1)}, u32[]{:S(2)}, u32[]{:S(2)}) async-start(bf16[64,16,128]{2,1,0:T(8,128)(2,1)} %shard_map.73), calls=%async_computation | async-start | bytes 524288 | tf_op jit(solution)/shard_map/all_to_all | solution.py:170
  27.5 12.5 %all-to-all-done.table_ref = bf16[64,16,128]{2,1,0:T(8,128)(2,1)S(1)} async-done(((bf16[64,16,128]{2,1,0:T(8,128)(2,1)}), bf16[64,16,128]{2,1,0:T(8,128)(2,1)S(1)}, u32[]{:S(2)}, u32[]{:S(2)}) %all-to-all-start) | async-done | bytes 262176 | tf_op jit(solution)/shard_map/all_to_all | solution.py:170
  40.1 0.0 copy-start.2
  40.1 0.7 slice_select_fusion.rows_ref
  40.8 0.0 copy-done.2
  40.9 2.3 %shard_map.74 = bf16[256,8,128]{2,1,0:T(8,128)(2,1)} custom-call(s32[64,4]{1,0:T(8,128)} %slice_select_fusion.rows_ref, bf16[64,16,128]{2,1,0:T(8,128)(2,1)} %copy-done.2), custom_call_target="tpu_custom_call" | custom-call | tf_op jit(solution)/shard_map/pallas_call | solution.py:174
  43.1 28.5 %all_to_all.10.own_ref = bf16[256,8,128]{2,1,0:T(8,128)(2,1)S(1)} all-to-all(bf16[256,8,128]{2,1,0:T(8,128)(2,1)} %shard_map.74), channel_id=1, replica_groups=mesh['pb'=64,'row'=4,'col'=2] {'pb','row'}, dimensions={0} | all-to-all | bytes 1048576 | tf_op jit(solution)/shard_map/all_to_all | solution.py:181
  71.7 0.0 copy-start.1
  71.7 5.9 %collective-permute-start = (bf16[256,8,128]{2,1,0:T(8,128)(2,1)S(1)}, bf16[256,8,128]{2,1,0:T(8,128)(2,1)S(1)}, u32[]{:S(2)}, u32[]{:S(2)}) collective-permute-start(bf16[256,8,128]{2,1,0:T(8,128)(2,1)S(1)} %all_to_all.10.own_ref), channel_id=1, source_target_pairs={{0,1},{1,0},{2,3},{3,2},{4,5},{5,4},{6,7},{7,6},{8,9},{9,8},{10,11... | collective-permute-start | bytes 1572872 | tf_op jit(solution)/shard_map/ppermute | solution.py:182
  77.6 0.0 copy-done.4
  77.6 0.2 dynamic-slice_reduce_fusion.1
  77.8 0.7 fusion.3
  81.0 0.0 copy-done
  81.0 1.1 dynamic-slice_reduce_fusion
  82.2 1.0 reshape.21.start_ref
  84.5 0.7 fusion.1
  85.2 0.7 broadcast_subtract_fusion.gap_ref
  85.9 0.0 collective-permute-done.other_ref
  85.9 0.0 copy-start.3
  85.9 0.0 all-gather.2.cloned.1.call-done.w_ref
  85.9 0.0 copy-done.1
  85.9 0.8 copy-done.3
  86.7 17.3 %shard_map.75 = bf16[960,96]{1,0:T(8,128)(2,1)} custom-call(s32[1]{0:T(128)} %bitcast.column_ref, f32[96,96]{1,0:T(8,128)} %broadcast_subtract_fusion.gap_ref, bf16[256,8,128]{2,1,0:T(8,128)(2,1)} %copy-done.1, bf16[256,8,128]{2,1,0:T(8,128)(2,1)} %copy-done.3, bf16[960,96]{1,0:T(8,128)(2,1)} %reshape.21.start_ref, ...), custom_call_target="tpu_custom_call" | custom-call | tf_op jit(solution)/shard_map/pallas_call | solution.py:194
  104.0 1.3 %all_gather_reshape.3 = bf16[1,10,72,128]{3,2,1,0:T(8,128)(2,1)S(1)} reshape(bf16[960,96]{1,0:T(8,128)(2,1)} %shard_map.75) | data formatting | bytes 368640 | tf_op jit(solution)/shard_map/all_gather;reshape | solution.py:213
  105.3 11.5 %all_gather.7 = bf16[4,10,72,128]{3,2,1,0:T(8,128)(2,1)S(1)} all-gather(bf16[1,10,72,128]{3,2,1,0:T(8,128)(2,1)S(1)} %all_gather_reshape.3), channel_id=1, replica_groups=mesh['pb'=64,'row'=4,'col'=2] {'row'}, dimensions={0}, use_global_device_ids=true | all-gather | bytes 921600 | tf_op jit(solution)/shard_map/all_gather | solution.py:213
  116.9 4.5 %collective-permute-start.1 = (bf16[4,10,72,128]{3,2,1,0:T(8,128)(2,1)S(1)}, bf16[4,10,72,128]{3,2,1,0:T(8,128)(2,1)S(1)}, u32[]{:S(2)}, u32[]{:S(2)}) collective-permute-start(bf16[4,10,72,128]{3,2,1,0:T(8,128)(2,1)S(1)} %all_gather.7), channel_id=1, source_target_pairs={{0,1},{1,0},{2,3},{3,2},{4,5},{5,4},{6,7},{7,6},{8,9},{9,8},{10,11... | collective-permute-start | bytes 2211848 | tf_op jit(solution)/shard_map/ppermute | solution.py:214
  121.4 1.8 %collective-permute-done.1 = bf16[4,10,72,128]{3,2,1,0:T(8,128)(2,1)S(1)} collective-permute-done((bf16[4,10,72,128]{3,2,1,0:T(8,128)(2,1)S(1)}, bf16[4,10,72,128]{3,2,1,0:T(8,128)(2,1)S(1)}, u32[]{:S(2)}, u32[]{:S(2)}) %collective-permute-start.1) | collective-permute-done | bytes 737312 | tf_op jit(solution)/shard_map/ppermute | solution.py:214
  123.2 0.2 fusion
  123.4 0.1 copy.14
  123.6 1.3 reshape.22
  (1 shorter events, 0.0 us)
Async XLA Ops:
  6.5 74.5 %copy-start = (bf16[1,20,4,9216]{3,2,1,0:T(4,128)(2,1)S(1)}, bf16[1,20,4,9216]{3,2,1,0:T(4,128)(2,1)}, u32[]{:S(2)}) copy-start(bf16[1,20,4,9216]{3,2,1,0:T(4,128)(2,1)} %param.7) | copy-start | bytes 4423684
  6.5 79.3 %all-gather.2.cloned.1.call-start = ((), (), s32[]{:S(2)}) async-start(), calls=%async_computation.2 | async-start | bytes 9437184 | tf_op jit(solution)/shard_map/all_gather | solution.py:161
  7.3 70.3 %copy-start.4 = (s32[1,4,2]{1,2,0:T(2,128)S(1)}, s32[1,4,2]{1,2,0:T(2,128)}, u32[]{:S(2)}) copy-start(s32[1,4,2]{1,2,0:T(2,128)} %param.8) | copy-start | bytes 100
  10.4 29.7 %all-to-all-start = ((bf16[64,16,128]{2,1,0:T(8,128)(2,1)}), bf16[64,16,128]{2,1,0:T(8,128)(2,1)S(1)}, u32[]{:S(2)}, u32[]{:S(2)}) async-start(bf16[64,16,128]{2,1,0:T(8,128)(2,1)} %shard_map.73), calls=%async_computation | async-start | bytes 524288 | tf_op jit(solution)/shard_map/all_to_all | solution.py:170
  40.1 0.8 copy-start.2
  71.7 14.2 %copy-start.1 = (bf16[256,8,128]{2,1,0:T(8,128)(2,1)}, bf16[256,8,128]{2,1,0:T(8,128)(2,1)S(1)}, u32[]{:S(2)}) copy-start(bf16[256,8,128]{2,1,0:T(8,128)(2,1)S(1)} %all_to_all.10.own_ref) | copy-start | bytes 1572868
  71.7 14.2 %collective-permute-start = (bf16[256,8,128]{2,1,0:T(8,128)(2,1)S(1)}, bf16[256,8,128]{2,1,0:T(8,128)(2,1)S(1)}, u32[]{:S(2)}, u32[]{:S(2)}) collective-permute-start(bf16[256,8,128]{2,1,0:T(8,128)(2,1)S(1)} %all_to_all.10.own_ref), channel_id=1, source_target_pairs={{0,1},{1,0},{2,3},{3,2},{4,5},{5,4},{6,7},{7,6},{8,9},{9,8},{10,11... | collective-permute-start | bytes 1572872 | tf_op jit(solution)/shard_map/ppermute | solution.py:182
  85.9 0.8 copy-start.3
  116.9 6.3 %collective-permute-start.1 = (bf16[4,10,72,128]{3,2,1,0:T(8,128)(2,1)S(1)}, bf16[4,10,72,128]{3,2,1,0:T(8,128)(2,1)S(1)}, u32[]{:S(2)}, u32[]{:S(2)}) collective-permute-start(bf16[4,10,72,128]{3,2,1,0:T(8,128)(2,1)S(1)} %all_gather.7), channel_id=1, source_target_pairs={{0,1},{1,0},{2,3},{3,2},{4,5},{5,4},{6,7},{7,6},{8,9},{9,8},{10,11... | collective-permute-start | bytes 2211848 | tf_op jit(solution)/shard_map/ppermute | solution.py:214
Sparse Core Ops, SparseCore 0:
  9.5 66.4 all-gather.1

commit v2 on v1

--- a/solution.py
+++ b/solution.py
@@ -21,7 +21,7 @@
     wanted = jnp.zeros((ROWS, LANES), jnp.float32)
     for half in range(2):
         for pair in range(count):
-            hit = stored == pairs_ref[0, pair, half]
+            hit = stored == pairs_ref[half, pair]
             row = jnp.sum(jnp.where(hit, place, 0.0), axis=1, keepdims=True)
             wanted = jnp.where(lane == half * count + pair, row, wanted)
     bands = orbitals_ref.shape[1]
@@ -48,22 +48,25 @@
     lax.fori_loop(0, transfers, one, 0, unroll=8)
 
 
-def steps_kernel(column_ref, gap_ref, own_ref, other_ref, start_ref, w_ref, out_ref,
-                 valence, conduction, w_all, screened_in, screened_out, total, first, sems):
+def steps_kernel(place_ref, gap_ref, own_ref, other_ref, start_ref, *refs):
+    tiles_w = len(refs) - 10
+    w_refs, out_ref = refs[:tiles_w], refs[tiles_w]
+    valence, conduction, w_all, screened_in, screened_out, total, first, flat, sems = refs[tiles_w + 1 :]
     count_v = valence.shape[0]
     count_c = conduction.shape[0]
     points = valence.shape[1]
-    tiles_w = w_ref.shape[0]
-    rows_w, cols_w = w_ref.shape[1], w_ref.shape[2]
+    rows_w, cols_w = w_refs[0].shape
     wide_w = points // cols_w
     flat_rows = start_ref.shape[0]
     vectors = flat_rows // count_v
     padded = screened_in.shape[0]
-    copies = [pltpu.make_async_copy(w_ref.at[t], w_all.at[t], sems.at[t]) for t in range(tiles_w)]
+    copies = [
+        pltpu.make_async_copy(w_refs[t], w_all.at[place_ref[1 + t]], sems.at[t]) for t in range(tiles_w)
+    ]
     for copy in copies:
         copy.start()
 
-    even = column_ref[0] == 0
+    even = place_ref[0] == 0
     wide = 2
     row_count = points // (2 * wide * LANES)
 
@@ -139,7 +142,15 @@
     kernel_term(start_ref)
     first[...] = scaled(start_ref[...]).astype(jnp.bfloat16)
     kernel_term(first)
-    out_ref[...] = (2.0 * scaled(first[...]) - start_ref[...].astype(jnp.float32)).astype(jnp.bfloat16)
+    total[...] = 2.0 * scaled(first[...]) - start_ref[...].astype(jnp.float32)
+
+    quads = flat_rows // 4
+    part = [total[pl.ds(k, quads, stride=4), :] for k in range(4)]
+    third = LANES - count_c
+    flat[pl.ds(0, quads, stride=3), :] = jnp.concatenate([part[0], part[1][:, :third]], axis=1)
+    flat[pl.ds(1, quads, stride=3), :] = jnp.concatenate([part[1][:, third:], part[2][:, : 2 * third]], axis=1)
+    flat[pl.ds(2, quads, stride=3), :] = jnp.concatenate([part[2][:, 2 * third :], part[3]], axis=1)
+    out_ref[...] = flat[...].astype(jnp.bfloat16)
 
 
 def on_device(amplitudes, pairs, stored_k, orbitals, valence_energy, conduction_energy, screened):
@@ -158,16 +169,42 @@
     vmem = pl.BlockSpec(memory_space=pltpu.VMEM)
     limit = pltpu.CompilerParams(vmem_limit_bytes=VMEM_LIMIT)
 
-    w_tiles = lax.all_gather(screened[0], ("row", "col"))
-
     message = pl.pallas_call(
         pack_kernel,
         out_shape=jax.ShapeDtypeStruct((transfers, 2 * ROWS, LANES), jnp.bfloat16),
         in_specs=[smem, vmem, vmem],
         out_specs=vmem,
         compiler_params=limit,
-    )(pairs, stored_k.reshape(1, transfers), orbitals)
+    )(pairs[0].T, stored_k.reshape(1, transfers), orbitals)
     table = lax.all_to_all(message, "pb", 0, 0, tiled=True)
+
+    swap = [(0, 1), (1, 0)]
+    rows_axis = lax.axis_size("row")
+    ring = [(r, c) for r in range(rows_axis) for c in range(cols)]
+    there = [(r * cols + c, (r + 1 - 2 * c) % rows_axis * cols + c) for r, c in ring]
+    back = [(target, source) for source, target in there]
+    w_own, _ = lax.optimization_barrier((screened[0], message))
+    w_there = lax.ppermute(w_own, ("row", "col"), there)
+    w_back = lax.ppermute(w_own, ("row", "col"), back)
+    w_far = lax.ppermute(w_there, ("row", "col"), there)
+    w_mine = [w_own, w_there, w_back, w_far]
+    w_tiles = w_mine + [lax.ppermute(tile, "col", swap) for tile in w_mine]
+    turn = 1 - 2 * column
+    rows_mine = jnp.stack([pair, pair - turn, pair + turn, pair + 2]) % rows_axis
+    rows_theirs = jnp.stack([pair, pair + turn, pair - turn, pair + 2]) % rows_axis
+    place = jnp.concatenate(
+        [column.reshape(1), rows_mine * cols + column, rows_theirs * cols + 1 - column]
+    ).astype(jnp.int32)
+    start = lax.dynamic_slice(
+        amplitudes[0], (column * share, pair, 0), (share, 1, flat_size)
+    ).reshape(share * count_v, count_c)
+    listed = lax.dynamic_slice_in_dim(pairs[0], pair, 1, 0)
+    low = lax.dynamic_slice_in_dim(valence_energy, listed[0, 0], 1, 0)
+    high = lax.dynamic_slice_in_dim(conduction_energy, listed[0, 1], 1, 0)
+    gap = high - low.reshape(count_v, 1)
+
+    table, start, gap, place = lax.optimization_barrier((table, start, gap, place))
+
     wanted = table[:, ROWS, : 2 * pair_count].astype(jnp.int32)
     valence_tiles = count_v // ROWS * (orbitals.shape[2] // LANES)
     rows = jnp.where(member < valence_tiles, wanted[:, :pair_count], wanted[:, pair_count:])
@@ -181,33 +218,26 @@
     own = lax.all_to_all(chosen, ("pb", "row"), 0, 0, tiled=True)
     other = lax.ppermute(own, "col", [(0, 1), (1, 0)])
 
-    start = lax.dynamic_slice(
-        amplitudes[0], (column * share, pair, 0), (share, 1, flat_size)
-    ).reshape(share * count_v, count_c)
-    listed = lax.dynamic_slice_in_dim(pairs[0], pair, 1, 0)
-    low = lax.dynamic_slice_in_dim(valence_energy, listed[0, 0], 1, 0)
-    high = lax.dynamic_slice_in_dim(conduction_energy, listed[0, 1], 1, 0)
-    gap = high - low.reshape(count_v, 1)
-
     padded = 16
     flat_rows = share * count_v
     result = pl.pallas_call(
         steps_kernel,
-        out_shape=jax.ShapeDtypeStruct((flat_rows, count_c), jnp.bfloat16),
-        in_specs=[smem, vmem, vmem, vmem, vmem, pl.BlockSpec(memory_space=pl.ANY)],
+        out_shape=jax.ShapeDtypeStruct((flat_rows * count_c // LANES, LANES), jnp.bfloat16),
+        in_specs=[smem, vmem, vmem, vmem, vmem] + [pl.BlockSpec(memory_space=pl.ANY)] * devices,
         out_specs=vmem,
         scratch_shapes=[
             pltpu.VMEM((count_v, points), jnp.float32),
             pltpu.VMEM((count_c, points), jnp.bfloat16),
-            pltpu.VMEM(w_tiles.shape, jnp.bfloat16),
+            pltpu.VMEM((devices,) + screened.shape[1:], jnp.bfloat16),
             pltpu.VMEM((padded, points), jnp.float32),
             pltpu.VMEM((padded, points), jnp.float32),
             pltpu.VMEM((flat_rows, count_c), jnp.float32),
             pltpu.VMEM((flat_rows, count_c), jnp.bfloat16),
+            pltpu.VMEM((flat_rows * count_c // LANES, LANES), jnp.float32),
             pltpu.SemaphoreType.DMA((devices,)),
         ],
         compiler_params=limit,
-    )(column.reshape(1), gap, own, other, start, w_tiles)
+    )(place, gap, own, other, start, *w_tiles)
 
     mine = result.reshape(share, flat_size // LANES, LANES)
     across = lax.all_gather(mine, "row")

time: 132 us -> 121 us (0.917)
  starting transfers between devices: 27.6 us -> 66.2 us
  blocking collectives: 40 us -> 11 us
  between operations: 17.4 us -> 3.72 us
  waiting for transfers between devices: 15.1 us -> 8.83 us
  local copies, waits for them, and re-layouts: 8.66 us -> 6.52 us
    all_to_all x1 -> x0, blocking collectives: 28.5 us -> none  [on_device(): own = lax.all_to_all(chosen, ('pb', 'row'), 0, 0, tiled=True)]
    ppermute x0 -> x7, starting transfers between devices: none -> 22.1 us  [the longest x4 10.4 us: on_device(): w_tiles = w_mine + [lax.ppermute(tile, 'col', swap) for tile in w_mine]]
    all_to_all x0 -> x1, starting transfers between devices: none -> 15.7 us  [on_device(): own = lax.all_to_all(chosen, ('pb', 'row'), 0, 0, tiled=True)]
    all_to_all x1, waiting for transfers between devices: 12.5 us -> 0.01 us  [on_device(): table = lax.all_to_all(message, 'pb', 0, 0, tiled=True)]
    all_to_all x0 -> x1, waiting for transfers between devices: none -> 5.49 us  [on_device(): own = lax.all_to_all(chosen, ('pb', 'row'), 0, 0, tiled=True)]
    ppermute x1, waiting for transfers between devices: 0.01 us -> 1.5 us  [on_device(): other = lax.ppermute(own, 'col', [(0, 1), (1, 0)])]
    unnamed x11 -> x10, local copies, waits for them, and re-layouts: 2.24 us -> 0.79 us
    another operation x1 -> x0, local copies, waits for them, and re-layouts: 1.32 us -> none  [on_device(): across = lax.all_gather(mine, 'row')]
  transfers between devices with their start and end apart: 4 -> 11, of which waited for: 2 -> 3; matrix products, arithmetic and copies ran while one was open for 5% -> 5% of each run, Pallas kernels for 3% -> 2%
where the time goes in v2:
time: 121 us; the launch traced here: 120 us
  starting transfers between devices  66.2 us (55%)
  Pallas kernels  21.6 us (18%)
  blocking collectives  11 us (9%)
  waiting for transfers between devices  8.83 us (7%)
  local copies, waits for them, and re-layouts  6.52 us (5%)
  between operations  3.72 us (3%)
  other arithmetic  2.34 us (2%)
    pallas_call x1, Pallas kernels, on_device(): pl.pallas_call(steps_kernel, out_shape=jax.ShapeDtypeStruct((flat_rows *...  17.5 us
    all_to_all x1, starting transfers between devices, on_device(): table = lax.all_to_all(message, 'pb', 0, 0, tiled=True)  16.3 us
    all_to_all x1, starting transfers between devices, on_device(): own = lax.all_to_all(chosen, ('pb', 'row'), 0, 0, tiled=True)  15.7 us
    all_gather x1, blocking collectives, on_device(): across = lax.all_gather(mine, 'row')  11 us
    ppermute x4, starting transfers between devices, on_device(): w_tiles = w_mine + [lax.ppermute(tile, 'col', swap) for tile in w_mine]  10.4 us
    ppermute x1, starting transfers between devices, on_device(): other = lax.ppermute(own, 'col', [(0, 1), (1, 0)])  6.51 us
    all_to_all x1, waiting for transfers between devices, on_device(): own = lax.all_to_all(chosen, ('pb', 'row'), 0, 0, tiled=True)  5.49 us
    ppermute x1, starting transfers between devices, on_device(): theirs = lax.ppermute(across, 'col', [(0, 1), (1, 0)])  5.49 us
  transfers between devices with their start and end apart: 11, of which 3 were waited for; matrix products, arithmetic and copies ran while one was open for 5% of the time, Pallas kernels for 2%

profile of v2, /device:TPU:1, one launch (start us, length us, event | category | flops | bytes accessed | tf_op | source)
XLA Modules:
  0.0 120.2 jit_solution(10721034819623480013)
XLA Ops:
  0.0 0.0 copy-start
  0.0 1.8 %shard_map.73 = bf16[64,16,128]{2,1,0:T(8,128)(2,1)} custom-call(s32[2,4]{1,0:T(2,128)} %bitcast.34, s32[1,64]{1,0:T(1,128)} %bitcast.35, bf16[1,192,256]{2,1,0:T(8,128)(2,1)} %orbitals_ref.1), custom_call_target="tpu_custom_call" | custom-call | tf_op jit(solution)/shard_map/pallas_call | solution.py:172
  1.8 5.2 %collective-permute-start.1 = (bf16[512,1024]{1,0:T(8,128)(2,1)}, bf16[512,1024]{1,0:T(8,128)(2,1)}, u32[]{:S(2)}, u32[]{:S(2)}) collective-permute-start(bf16[512,1024]{1,0:T(8,128)(2,1)} %bitcast.26), channel_id=1, source_target_pairs={{0,2},{1,7},{2,4},{3,1},{4,6},{5,3},{6,0},{7,5},{8,10},{9,15},{10,... | collective-permute-start | bytes 3145736 | tf_op jit(solution)/shard_map/ppermute | solution.py:187
  7.1 16.3 %all-to-all-start = ((bf16[64,16,128]{2,1,0:T(8,128)(2,1)}), bf16[64,16,128]{2,1,0:T(8,128)(2,1)S(1)}, u32[]{:S(2)}, u32[]{:S(2)}) async-start(bf16[64,16,128]{2,1,0:T(8,128)(2,1)} %shard_map.73), calls=%async_computation | async-start | bytes 524288 | tf_op jit(solution)/shard_map/all_to_all | solution.py:179
  23.4 1.9 %collective-permute-start.2 = (bf16[512,1024]{1,0:T(8,128)(2,1)}, bf16[512,1024]{1,0:T(8,128)(2,1)}, u32[]{:S(2)}, u32[]{:S(2)}) collective-permute-start(bf16[512,1024]{1,0:T(8,128)(2,1)} %bitcast.27), channel_id=1, source_target_pairs={{2,0},{7,1},{4,2},{1,3},{6,4},{3,5},{0,6},{5,7},{10,8},{15,9},{12,... | collective-permute-start | bytes 3145736 | tf_op jit(solution)/shard_map/ppermute | solution.py:188
  25.3 0.9 dynamic-slice_reduce_fusion.1
  26.2 0.6 fusion.10
  29.1 0.0 copy-done
  29.1 1.1 dynamic-slice_reduce_fusion
  30.3 0.0 copy-start.3
  30.3 1.0 reshape.20.start_ref
  32.4 0.1 fusion.4
  32.5 0.7 fusion.1
  33.2 0.7 broadcast_subtract_fusion.gap_ref
  33.9 0.0 collective-permute-done.1.refs_1_
  33.9 4.6 %collective-permute-start.3 = (bf16[512,1024]{1,0:T(8,128)(2,1)}, bf16[512,1024]{1,0:T(8,128)(2,1)}, u32[]{:S(2)}, u32[]{:S(2)}) collective-permute-start(bf16[512,1024]{1,0:T(8,128)(2,1)} %collective-permute-done.1.refs_1_), channel_id=1, source_target_pairs={{0,2},{1,7},{2,4},{3,1},{4,6},{5,3},{6,0},{7,5},{8,10},{9,15},{10,... | collective-permute-start | bytes 3145736 | tf_op jit(solution)/shard_map/ppermute | solution.py:189
  38.5 0.6 pad_add_fusion.place_ref
  39.1 0.0 all-to-all-done.table_ref
  39.1 0.0 copy-start.2
  39.1 0.7 slice_select_fusion.rows_ref
  39.8 0.0 copy-done.2
  39.8 2.3 %shard_map.74 = bf16[256,8,128]{2,1,0:T(8,128)(2,1)} custom-call(s32[64,4]{1,0:T(8,128)} %slice_select_fusion.rows_ref, bf16[64,16,128]{2,1,0:T(8,128)(2,1)} %copy-done.2), custom_call_target="tpu_custom_call" | custom-call | tf_op jit(solution)/shard_map/pallas_call | solution.py:211
  42.1 15.7 %all-to-all-start.1 = ((bf16[256,8,128]{2,1,0:T(8,128)(2,1)}), bf16[256,8,128]{2,1,0:T(8,128)(2,1)S(1)}, u32[]{:S(2)}, u32[]{:S(2)}) async-start(bf16[256,8,128]{2,1,0:T(8,128)(2,1)} %shard_map.74), calls=%async_computation.1 | async-start | bytes 1048576 | tf_op jit(solution)/shard_map/all_to_all | solution.py:218
  57.9 0.0 copy-done.3
  57.9 4.2 %collective-permute-start.4 = (bf16[512,1024]{1,0:T(8,128)(2,1)S(1)}, bf16[512,1024]{1,0:T(8,128)(2,1)}, u32[]{:S(2)}, u32[]{:S(2)}) collective-permute-start(bf16[512,1024]{1,0:T(8,128)(2,1)S(1)} %bitcast.29), channel_id=1, source_target_pairs={{0,1},{1,0},{2,3},{3,2},{4,5},{5,4},{6,7},{7,6},{8,9},{9,8},{10,11... | collective-permute-start | bytes 3145736 | tf_op jit(solution)/shard_map/ppermute | solution.py:191
  62.1 1.9 %collective-permute-start.5 = (bf16[512,1024]{1,0:T(8,128)(2,1)}, bf16[512,1024]{1,0:T(8,128)(2,1)}, u32[]{:S(2)}, u32[]{:S(2)}) collective-permute-start(bf16[512,1024]{1,0:T(8,128)(2,1)} %collective-permute-done.1.refs_1_), channel_id=1, source_target_pairs={{0,1},{1,0},{2,3},{3,2},{4,5},{5,4},{6,7},{7,6},{8,9},{9,8},{10,11... | collective-permute-start | bytes 3145736 | tf_op jit(solution)/shard_map/ppermute | solution.py:191
  64.0 0.0 collective-permute-done.2.refs_2_
  64.0 2.4 %collective-permute-start.6 = (bf16[512,1024]{1,0:T(8,128)(2,1)}, bf16[512,1024]{1,0:T(8,128)(2,1)}, u32[]{:S(2)}, u32[]{:S(2)}) collective-permute-start(bf16[512,1024]{1,0:T(8,128)(2,1)} %collective-permute-done.2.refs_2_), channel_id=1, source_target_pairs={{0,1},{1,0},{2,3},{3,2},{4,5},{5,4},{6,7},{7,6},{8,9},{9,8},{10,11... | collective-permute-start | bytes 3145736 | tf_op jit(solution)/shard_map/ppermute | solution.py:191
  66.4 0.0 collective-permute-done.3.refs_3_
  66.5 1.9 %collective-permute-start.7 = (bf16[512,1024]{1,0:T(8,128)(2,1)}, bf16[512,1024]{1,0:T(8,128)(2,1)}, u32[]{:S(2)}, u32[]{:S(2)}) collective-permute-start(bf16[512,1024]{1,0:T(8,128)(2,1)} %collective-permute-done.3.refs_3_), channel_id=1, source_target_pairs={{0,1},{1,0},{2,3},{3,2},{4,5},{5,4},{6,7},{7,6},{8,9},{9,8},{10,11... | collective-permute-start | bytes 3145736 | tf_op jit(solution)/shard_map/ppermute | solution.py:191
  68.4 5.5 %all-to-all-done.1.own_ref = bf16[256,8,128]{2,1,0:T(8,128)(2,1)S(1)} async-done(((bf16[256,8,128]{2,1,0:T(8,128)(2,1)}), bf16[256,8,128]{2,1,0:T(8,128)(2,1)S(1)}, u32[]{:S(2)}, u32[]{:S(2)}) %all-to-all-start.1) | async-done | bytes 524320 | tf_op jit(solution)/shard_map/all_to_all | solution.py:218
  73.9 0.0 copy-start.1
  73.9 6.5 %collective-permute-start = (bf16[256,8,128]{2,1,0:T(8,128)(2,1)S(1)}, bf16[256,8,128]{2,1,0:T(8,128)(2,1)S(1)}, u32[]{:S(2)}, u32[]{:S(2)}) collective-permute-start(bf16[256,8,128]{2,1,0:T(8,128)(2,1)S(1)} %all-to-all-done.1.own_ref), channel_id=1, source_target_pairs={{0,1},{1,0},{2,3},{3,2},{4,5},{5,4},{6,7},{7,6},{8,9},{9,8},{10,11... | collective-permute-start | bytes 1572872 | tf_op jit(solution)/shard_map/ppermute | solution.py:219
  80.4 0.0 collective-permute-done.4.refs_4_
  80.4 1.5 %collective-permute-done.other_ref = bf16[256,8,128]{2,1,0:T(8,128)(2,1)S(1)} collective-permute-done((bf16[256,8,128]{2,1,0:T(8,128)(2,1)S(1)}, bf16[256,8,128]{2,1,0:T(8,128)(2,1)S(1)}, u32[]{:S(2)}, u32[]{:S(2)}) %collective-permute-start) | collective-permute-done | bytes 524320 | tf_op jit(solution)/shard_map/ppermute | solution.py:219
  81.9 0.0 copy-start.4
  81.9 0.0 collective-permute-done.6.refs_6_
  81.9 0.0 collective-permute-done.5.refs_5_
  81.9 0.0 collective-permute-done.7.refs_7_
  81.9 0.0 copy-done.1
  81.9 0.8 copy-done.4
  82.7 17.5 %shard_map.75 = bf16[720,128]{1,0:T(8,128)(2,1)} custom-call(s32[9]{0:T(128)} %pad_add_fusion.place_ref, f32[96,96]{1,0:T(8,128)} %broadcast_subtract_fusion.gap_ref, bf16[256,8,128]{2,1,0:T(8,128)(2,1)} %copy-done.1, bf16[256,8,128]{2,1,0:T(8,128)(2,1)} %copy-done.4, bf16[960,96]{1,0:T(8,128)(2,1)} %reshape.20.start_ref, bf16[512,1024]{1,0:T(8,128)(2,1)} %bitcast.28, ...), custom_call_target="tpu_custom_call" | custom-call | tf_op jit(solution)/shard_map/pallas_call | solution.py:223
  100.2 11.0 %all_gather.3 = bf16[4,10,72,128]{3,2,1,0:T(8,128)(2,1)S(1)} all-gather(bf16[1,10,72,128]{3,2,1,0:T(8,128)(2,1)} %bitcast.31), channel_id=1, replica_groups=mesh['pb'=64,'row'=4,'col'=2] {'row'}, dimensions={0}, use_global_device_ids=true | all-gather | bytes 921600 | tf_op jit(solution)/shard_map/all_gather | solution.py:243
  111.2 5.5 %collective-permute-start.8 = (bf16[4,10,72,128]{3,2,1,0:T(8,128)(2,1)S(1)}, bf16[4,10,72,128]{3,2,1,0:T(8,128)(2,1)S(1)}, u32[]{:S(2)}, u32[]{:S(2)}) collective-permute-start(bf16[4,10,72,128]{3,2,1,0:T(8,128)(2,1)S(1)} %all_gather.3), channel_id=1, source_target_pairs={{0,1},{1,0},{2,3},{3,2},{4,5},{5,4},{6,7},{7,6},{8,9},{9,8},{10,11... | collective-permute-start | bytes 2211848 | tf_op jit(solution)/shard_map/ppermute | solution.py:244
  116.7 1.8 %collective-permute-done.8 = bf16[4,10,72,128]{3,2,1,0:T(8,128)(2,1)S(1)} collective-permute-done((bf16[4,10,72,128]{3,2,1,0:T(8,128)(2,1)S(1)}, bf16[4,10,72,128]{3,2,1,0:T(8,128)(2,1)S(1)}, u32[]{:S(2)}, u32[]{:S(2)}) %collective-permute-start.8) | collective-permute-done | bytes 737312 | tf_op jit(solution)/shard_map/ppermute | solution.py:244
  118.5 0.2 fusion
  118.8 0.1 copy.10
  118.9 1.3 %reshape.22 = bf16[1,20,4,9216]{3,2,1,0:T(4,128)(2,1)} reshape(bf16[2,10,4,72,128]{4,3,2,1,0:T(8,128)(2,1)S(1)} %copy.10) | data formatting | bytes 2949120 | tf_op jit(solution)/shard_map/reshape | solution.py:248
  (1 shorter events, 0.0 us)
Async XLA Ops:
  0.0 29.1 %copy-start = (bf16[1,20,4,9216]{3,2,1,0:T(4,128)(2,1)S(1)}, bf16[1,20,4,9216]{3,2,1,0:T(4,128)(2,1)}, u32[]{:S(2)}) copy-start(bf16[1,20,4,9216]{3,2,1,0:T(4,128)(2,1)} %param.7) | copy-start | bytes 4423684
  1.8 32.1 %collective-permute-start.1 = (bf16[512,1024]{1,0:T(8,128)(2,1)}, bf16[512,1024]{1,0:T(8,128)(2,1)}, u32[]{:S(2)}, u32[]{:S(2)}) collective-permute-start(bf16[512,1024]{1,0:T(8,128)(2,1)} %bitcast.26), channel_id=1, source_target_pairs={{0,2},{1,7},{2,4},{3,1},{4,6},{5,3},{6,0},{7,5},{8,10},{9,15},{10,... | collective-permute-start | bytes 3145736 | tf_op jit(solution)/shard_map/ppermute | solution.py:187
  7.1 32.0 %all-to-all-start = ((bf16[64,16,128]{2,1,0:T(8,128)(2,1)}), bf16[64,16,128]{2,1,0:T(8,128)(2,1)S(1)}, u32[]{:S(2)}, u32[]{:S(2)}) async-start(bf16[64,16,128]{2,1,0:T(8,128)(2,1)} %shard_map.73), calls=%async_computation | async-start | bytes 524288 | tf_op jit(solution)/shard_map/all_to_all | solution.py:179
  23.4 40.6 %collective-permute-start.2 = (bf16[512,1024]{1,0:T(8,128)(2,1)}, bf16[512,1024]{1,0:T(8,128)(2,1)}, u32[]{:S(2)}, u32[]{:S(2)}) collective-permute-start(bf16[512,1024]{1,0:T(8,128)(2,1)} %bitcast.27), channel_id=1, source_target_pairs={{2,0},{7,1},{4,2},{1,3},{6,4},{3,5},{0,6},{5,7},{10,8},{15,9},{12,... | collective-permute-start | bytes 3145736 | tf_op jit(solution)/shard_map/ppermute | solution.py:188
  30.3 27.6 %copy-start.3 = (bf16[1,512,1024]{2,1,0:T(8,128)(2,1)S(1)}, bf16[1,512,1024]{2,1,0:T(8,128)(2,1)}, u32[]{:S(2)}) copy-start(bf16[1,512,1024]{2,1,0:T(8,128)(2,1)} %param.13) | copy-start | bytes 3145732
  33.9 32.5 %collective-permute-start.3 = (bf16[512,1024]{1,0:T(8,128)(2,1)}, bf16[512,1024]{1,0:T(8,128)(2,1)}, u32[]{:S(2)}, u32[]{:S(2)}) collective-permute-start(bf16[512,1024]{1,0:T(8,128)(2,1)} %collective-permute-done.1.refs_1_), channel_id=1, source_target_pairs={{0,2},{1,7},{2,4},{3,1},{4,6},{5,3},{6,0},{7,5},{8,10},{9,15},{10,... | collective-permute-start | bytes 3145736 | tf_op jit(solution)/shard_map/ppermute | solution.py:189
  39.1 0.7 copy-start.2
  42.1 31.7 %all-to-all-start.1 = ((bf16[256,8,128]{2,1,0:T(8,128)(2,1)}), bf16[256,8,128]{2,1,0:T(8,128)(2,1)S(1)}, u32[]{:S(2)}, u32[]{:S(2)}) async-start(bf16[256,8,128]{2,1,0:T(8,128)(2,1)} %shard_map.74), calls=%async_computation.1 | async-start | bytes 1048576 | tf_op jit(solution)/shard_map/all_to_all | solution.py:218
  57.9 22.5 %collective-permute-start.4 = (bf16[512,1024]{1,0:T(8,128)(2,1)S(1)}, bf16[512,1024]{1,0:T(8,128)(2,1)}, u32[]{:S(2)}, u32[]{:S(2)}) collective-permute-start(bf16[512,1024]{1,0:T(8,128)(2,1)S(1)} %bitcast.29), channel_id=1, source_target_pairs={{0,1},{1,0},{2,3},{3,2},{4,5},{5,4},{6,7},{7,6},{8,9},{9,8},{10,11... | collective-permute-start | bytes 3145736 | tf_op jit(solution)/shard_map/ppermute | solution.py:191
  62.1 19.8 %collective-permute-start.5 = (bf16[512,1024]{1,0:T(8,128)(2,1)}, bf16[512,1024]{1,0:T(8,128)(2,1)}, u32[]{:S(2)}, u32[]{:S(2)}) collective-permute-start(bf16[512,1024]{1,0:T(8,128)(2,1)} %collective-permute-done.1.refs_1_), channel_id=1, source_target_pairs={{0,1},{1,0},{2,3},{3,2},{4,5},{5,4},{6,7},{7,6},{8,9},{9,8},{10,11... | collective-permute-start | bytes 3145736 | tf_op jit(solution)/shard_map/ppermute | solution.py:191
  64.0 17.9 %collective-permute-start.6 = (bf16[512,1024]{1,0:T(8,128)(2,1)}, bf16[512,1024]{1,0:T(8,128)(2,1)}, u32[]{:S(2)}, u32[]{:S(2)}) collective-permute-start(bf16[512,1024]{1,0:T(8,128)(2,1)} %collective-permute-done.2.refs_2_), channel_id=1, source_target_pairs={{0,1},{1,0},{2,3},{3,2},{4,5},{5,4},{6,7},{7,6},{8,9},{9,8},{10,11... | collective-permute-start | bytes 3145736 | tf_op jit(solution)/shard_map/ppermute | solution.py:191
  66.5 15.5 %collective-permute-start.7 = (bf16[512,1024]{1,0:T(8,128)(2,1)}, bf16[512,1024]{1,0:T(8,128)(2,1)}, u32[]{:S(2)}, u32[]{:S(2)}) collective-permute-start(bf16[512,1024]{1,0:T(8,128)(2,1)} %collective-permute-done.3.refs_3_), channel_id=1, source_target_pairs={{0,1},{1,0},{2,3},{3,2},{4,5},{5,4},{6,7},{7,6},{8,9},{9,8},{10,11... | collective-permute-start | bytes 3145736 | tf_op jit(solution)/shard_map/ppermute | solution.py:191
  73.9 8.1 %copy-start.1 = (bf16[256,8,128]{2,1,0:T(8,128)(2,1)}, bf16[256,8,128]{2,1,0:T(8,128)(2,1)S(1)}, u32[]{:S(2)}) copy-start(bf16[256,8,128]{2,1,0:T(8,128)(2,1)S(1)} %all-to-all-done.1.own_ref) | copy-start | bytes 1572868
  73.9 8.0 %collective-permute-start = (bf16[256,8,128]{2,1,0:T(8,128)(2,1)S(1)}, bf16[256,8,128]{2,1,0:T(8,128)(2,1)S(1)}, u32[]{:S(2)}, u32[]{:S(2)}) collective-permute-start(bf16[256,8,128]{2,1,0:T(8,128)(2,1)S(1)} %all-to-all-done.1.own_ref), channel_id=1, source_target_pairs={{0,1},{1,0},{2,3},{3,2},{4,5},{5,4},{6,7},{7,6},{8,9},{9,8},{10,11... | collective-permute-start | bytes 1572872 | tf_op jit(solution)/shard_map/ppermute | solution.py:219
  81.9 0.8 copy-start.4
  111.2 7.3 %collective-permute-start.8 = (bf16[4,10,72,128]{3,2,1,0:T(8,128)(2,1)S(1)}, bf16[4,10,72,128]{3,2,1,0:T(8,128)(2,1)S(1)}, u32[]{:S(2)}, u32[]{:S(2)}) collective-permute-start(bf16[4,10,72,128]{3,2,1,0:T(8,128)(2,1)S(1)} %all_gather.3), channel_id=1, source_target_pairs={{0,1},{1,0},{2,3},{3,2},{4,5},{5,4},{6,7},{7,6},{8,9},{9,8},{10,11... | collective-permute-start | bytes 2211848 | tf_op jit(solution)/shard_map/ppermute | solution.py:244

commit v3 on v2

--- a/solution.py
+++ b/solution.py
@@ -48,8 +48,9 @@
     lax.fori_loop(0, transfers, one, 0, unroll=8)
 
 
-def steps_kernel(place_ref, gap_ref, own_ref, other_ref, start_ref, *refs):
+def steps_kernel(pairs_ref, low_ref, high_ref, own_ref, other_ref, start_ref, *refs):
     tiles_w = len(refs) - 10
+    pair, column = lax.axis_index("row"), lax.axis_index("col")
     w_refs, out_ref = refs[:tiles_w], refs[tiles_w]
     valence, conduction, w_all, screened_in, screened_out, total, first, flat, sems = refs[tiles_w + 1 :]
     count_v = valence.shape[0]
@@ -60,13 +61,17 @@
     flat_rows = start_ref.shape[0]
     vectors = flat_rows // count_v
     padded = screened_in.shape[0]
+    turn = 1 - 2 * column
+    steps = (0, -turn, turn, 2, 0, turn, -turn, 2)
+    sides = (column,) * 4 + (1 - column,) * 4
     copies = [
-        pltpu.make_async_copy(w_refs[t], w_all.at[place_ref[1 + t]], sems.at[t]) for t in range(tiles_w)
+        pltpu.make_async_copy(w_refs[t], w_all.at[(pair + steps[t] + 4) % 4 * 2 + sides[t]], sems.at[t])
+        for t in range(tiles_w)
     ]
     for copy in copies:
         copy.start()
 
-    even = place_ref[0] == 0
+    even = column == 0
     wide = 2
     row_count = points // (2 * wide * LANES)
 
@@ -90,18 +95,11 @@
                 ).astype(jnp.bfloat16)
 
     screened_in[...] = jnp.zeros_like(screened_in)
-    chunk = 256
-    chunks = points // chunk
 
     def kernel_term(current_ref):
-        def expand(step, carry):
-            lanes = pl.ds(pl.multiple_of(step * chunk, chunk), chunk)
-            inner = jnp.dot(current_ref[...], conduction[:, lanes], preferred_element_type=jnp.float32)
-            inner = inner.reshape(vectors, count_v, chunk) * valence[:, lanes][None]
-            screened_in[:vectors, lanes] = jnp.sum(inner, axis=1).astype(jnp.bfloat16).astype(jnp.float32)
-            return carry
-
-        lax.fori_loop(0, chunks, expand, 0)
+        inner = jnp.dot(current_ref[...], conduction[...], preferred_element_type=jnp.float32)
+        inner = inner.reshape(vectors, count_v, points) * valence[...][None]
+        screened_in[:vectors, :] = jnp.sum(inner, axis=1)
         values = screened_in[...].astype(jnp.bfloat16)
         if current_ref is start_ref:
             for copy in copies:
@@ -116,23 +114,18 @@
                     preferred_element_type=jnp.float32,
                 )
             screened_out[:, row * rows_w : (row + 1) * rows_w] = summed
-        total[...] = jnp.zeros_like(total)
-
-        def project(step, carry):
-            lanes = pl.ds(pl.multiple_of(step * chunk, chunk), chunk)
-            weighted = screened_out[:vectors, lanes][:, None, :] * valence[:, lanes][None]
-            weighted = weighted.reshape(flat_rows, chunk).astype(jnp.bfloat16)
-            total[...] += lax.dot_general(
-                weighted,
-                conduction[:, lanes],
-                (((1,), (1,)), ((), ())),
-                preferred_element_type=jnp.float32,
-            )
-            return carry
-
-        lax.fori_loop(0, chunks, project, 0)
-
-    gap = gap_ref[...][None]
+        weighted = screened_out[:vectors, :][:, None, :] * valence[...][None]
+        weighted = weighted.reshape(flat_rows, points).astype(jnp.bfloat16)
+        total[...] = lax.dot_general(
+            weighted, conduction[...], (((1,), (1,)), ((), ())), preferred_element_type=jnp.float32
+        )
+
+    low = low_ref[pl.ds(pairs_ref[0, pair], 1), :]
+    high = high_ref[pl.ds(pairs_ref[1, pair], 1), :]
+    square = (count_v, count_v)
+    diagonal = lax.broadcasted_iota(jnp.int32, square, 0) == lax.broadcasted_iota(jnp.int32, square, 1)
+    low = jnp.sum(jnp.where(diagonal, low, 0.0), axis=1, keepdims=True)
+    gap = (high - low)[None]
 
     def scaled(current):
         parts = current.astype(jnp.float32).reshape(vectors, count_v, count_c)
@@ -161,49 +154,43 @@
     member = lax.axis_index("pb")
     pair = lax.axis_index("row")
     column = lax.axis_index("col")
-    cols = lax.axis_size("col")
-    devices = lax.axis_size("row") * cols
+    rows_axis, cols = lax.axis_size("row"), lax.axis_size("col")
+    devices = rows_axis * cols
     points = orbitals.shape[2] * devices
     share = vectors // cols
+    flat_rows = share * count_v
+    padded = 16
     smem = pl.BlockSpec(memory_space=pltpu.SMEM)
     vmem = pl.BlockSpec(memory_space=pltpu.VMEM)
+    anywhere = pl.BlockSpec(memory_space=pl.ANY)
     limit = pltpu.CompilerParams(vmem_limit_bytes=VMEM_LIMIT)
-
+    swap = [(0, 1), (1, 0)]
+    ring = [(r, c) for r in range(rows_axis) for c in range(cols)]
+    there = [(r * cols + c, (r + 1 - 2 * c) % rows_axis * cols + c) for r, c in ring]
+    back = [(target, source) for source, target in there]
+
+    wishes = pairs[0].T
     message = pl.pallas_call(
         pack_kernel,
         out_shape=jax.ShapeDtypeStruct((transfers, 2 * ROWS, LANES), jnp.bfloat16),
         in_specs=[smem, vmem, vmem],
         out_specs=vmem,
         compiler_params=limit,
-    )(pairs[0].T, stored_k.reshape(1, transfers), orbitals)
+    )(wishes, stored_k.reshape(1, transfers), orbitals)
     table = lax.all_to_all(message, "pb", 0, 0, tiled=True)
 
-    swap = [(0, 1), (1, 0)]
-    rows_axis = lax.axis_size("row")
-    ring = [(r, c) for r in range(rows_axis) for c in range(cols)]
-    there = [(r * cols + c, (r + 1 - 2 * c) % rows_axis * cols + c) for r, c in ring]
-    back = [(target, source) for source, target in there]
+    start = lax.dynamic_slice(
+        amplitudes[0],
+        (column * share, pair, 0),
+        (share, 1, flat_size),
+        allow_negative_indices=False,
+    ).reshape(flat_rows, count_c)
     w_own, _ = lax.optimization_barrier((screened[0], message))
     w_there = lax.ppermute(w_own, ("row", "col"), there)
     w_back = lax.ppermute(w_own, ("row", "col"), back)
+
     w_far = lax.ppermute(w_there, ("row", "col"), there)
-    w_mine = [w_own, w_there, w_back, w_far]
-    w_tiles = w_mine + [lax.ppermute(tile, "col", swap) for tile in w_mine]
-    turn = 1 - 2 * column
-    rows_mine = jnp.stack([pair, pair - turn, pair + turn, pair + 2]) % rows_axis
-    rows_theirs = jnp.stack([pair, pair + turn, pair - turn, pair + 2]) % rows_axis
-    place = jnp.concatenate(
-        [column.reshape(1), rows_mine * cols + column, rows_theirs * cols + 1 - column]
-    ).astype(jnp.int32)
-    start = lax.dynamic_slice(
-        amplitudes[0], (column * share, pair, 0), (share, 1, flat_size)
-    ).reshape(share * count_v, count_c)
-    listed = lax.dynamic_slice_in_dim(pairs[0], pair, 1, 0)
-    low = lax.dynamic_slice_in_dim(valence_energy, listed[0, 0], 1, 0)
-    high = lax.dynamic_slice_in_dim(conduction_energy, listed[0, 1], 1, 0)
-    gap = high - low.reshape(count_v, 1)
-
-    table, start, gap, place = lax.optimization_barrier((table, start, gap, place))
+    table, start = lax.optimization_barrier((table, start))
 
     wanted = table[:, ROWS, : 2 * pair_count].astype(jnp.int32)
     valence_tiles = count_v // ROWS * (orbitals.shape[2] // LANES)
@@ -216,14 +203,15 @@
         compiler_params=limit,
     )(rows, table)
     own = lax.all_to_all(chosen, ("pb", "row"), 0, 0, tiled=True)
-    other = lax.ppermute(own, "col", [(0, 1), (1, 0)])
-
-    padded = 16
-    flat_rows = share * count_v
+
+    w_core = [w_own, w_there, w_back, w_far]
+    w_tiles = w_core + [lax.ppermute(tile, "col", swap) for tile in w_core]
+    other = lax.ppermute(own, "col", swap)
+
     result = pl.pallas_call(
         steps_kernel,
         out_shape=jax.ShapeDtypeStruct((flat_rows * count_c // LANES, LANES), jnp.bfloat16),
-        in_specs=[smem, vmem, vmem, vmem, vmem] + [pl.BlockSpec(memory_space=pl.ANY)] * devices,
+        in_specs=[smem, vmem, vmem, vmem, vmem, vmem] + [anywhere] * devices,
         out_specs=vmem,
         scratch_shapes=[
             pltpu.VMEM((count_v, points), jnp.float32),
@@ -237,14 +225,12 @@
             pltpu.SemaphoreType.DMA((devices,)),
         ],
         compiler_params=limit,
-    )(place, gap, own, other, start, *w_tiles)
+    )(wishes, valence_energy, conduction_energy, own, other, start, *w_tiles)
 
     mine = result.reshape(share, flat_size // LANES, LANES)
     across = lax.all_gather(mine, "row")
-    theirs = lax.ppermute(across, "col", [(0, 1), (1, 0)])
-    both = jnp.where(
-        column == 0, jnp.stack([across, theirs]), jnp.stack([theirs, across])
-    )
+    theirs = lax.ppermute(across, "col", swap)
+    both = jnp.where(column == 0, jnp.stack([across, theirs]), jnp.stack([theirs, across]))
     return both.transpose(0, 2, 1, 3, 4).reshape(1, vectors, pair_count, flat_size)
 
 

time: 121 us -> 114 us (0.942)
  waiting for transfers between devices: 8.83 us -> 13.7 us
  starting transfers between devices: 66.2 us -> 61.4 us
  between operations: 3.72 us -> 0.21 us
  local copies, waits for them, and re-layouts: 6.52 us -> 4.33 us
  other arithmetic: 2.34 us -> 0.95 us
    all_to_all x1, waiting for transfers between devices: 0.01 us -> 5 us  [on_device(): table = lax.all_to_all(message, 'pb', 0, 0, tiled=True)]
    all_to_all x1, starting transfers between devices: 15.7 us -> 10.7 us  [on_device(): own = lax.all_to_all(chosen, ('pb', 'row'), 0, 0, tiled=True)]
  transfers between devices with their start and end apart: 11 -> 11, of which waited for: 3 -> 4; matrix products, arithmetic and copies ran while one was open for 5% -> 2% of each run, Pallas kernels for 2% -> 2%
where the time goes in v3:
time: 114 us
  starting transfers between devices  61.4 us (54%)
  Pallas kernels  22 us (19%)
  waiting for transfers between devices  13.7 us (12%)
  blocking collectives  11 us (10%)
  local copies, waits for them, and re-layouts  4.33 us (4%)
    pallas_call x1, Pallas kernels, on_device(): pl.pallas_call(steps_kernel, out_shape=jax.ShapeDtypeStruct((flat_rows *...  17.8 us
    all_to_all x1, starting transfers between devices, on_device(): table = lax.all_to_all(message, 'pb', 0, 0, tiled=True)  16.3 us
    all_gather x1, blocking collectives, on_device(): across = lax.all_gather(mine, 'row')  11 us
    all_to_all x1, starting transfers between devices, on_device(): own = lax.all_to_all(chosen, ('pb', 'row'), 0, 0, tiled=True)  10.7 us
    ppermute x4, starting transfers between devices, on_device(): w_tiles = w_core + [lax.ppermute(tile, 'col', swap) for tile in w_core]  10.4 us
    ppermute x1, starting transfers between devices, on_device(): other = lax.ppermute(own, 'col', swap)  6.7 us
    all_to_all x1, waiting for transfers between devices, on_device(): own = lax.all_to_all(chosen, ('pb', 'row'), 0, 0, tiled=True)  5.5 us
    ppermute x1, starting transfers between devices, on_device(): theirs = lax.ppermute(across, 'col', swap)  5.49 us
  transfers between devices with their start and end apart: 11, of which 4 were waited for; matrix products, arithmetic and copies ran while one was open for 2% of the time, Pallas kernels for 2%

profile of v3, /device:TPU:1, one launch (start us, length us, event | category | flops | bytes accessed | tf_op | source)
XLA Modules:
  0.0 113.5 jit_solution(7668524036936310905)
XLA Ops:
  0.0 0.0 copy-start
  0.0 1.8 %shard_map.73 = bf16[64,16,128]{2,1,0:T(8,128)(2,1)} custom-call(s32[2,4]{1,0:T(2,128)} %bitcast.21, s32[1,64]{1,0:T(1,128)} %bitcast.23, bf16[1,192,256]{2,1,0:T(8,128)(2,1)} %orbitals_ref.1), custom_call_target="tpu_custom_call" | custom-call | tf_op jit(solution)/shard_map/pallas_call | solution.py:173
  1.8 5.2 %collective-permute-start.1 = (bf16[512,1024]{1,0:T(8,128)(2,1)}, bf16[512,1024]{1,0:T(8,128)(2,1)}, u32[]{:S(2)}, u32[]{:S(2)}) collective-permute-start(bf16[512,1024]{1,0:T(8,128)(2,1)} %bitcast.14), channel_id=1, source_target_pairs={{0,2},{1,7},{2,4},{3,1},{4,6},{5,3},{6,0},{7,5},{8,10},{9,15},{10,... | collective-permute-start | bytes 3145736 | tf_op jit(solution)/shard_map/ppermute | solution.py:189
  7.1 16.3 %all-to-all-start = ((bf16[64,16,128]{2,1,0:T(8,128)(2,1)}), bf16[64,16,128]{2,1,0:T(8,128)(2,1)S(1)}, u32[]{:S(2)}, u32[]{:S(2)}) async-start(bf16[64,16,128]{2,1,0:T(8,128)(2,1)} %shard_map.73), calls=%async_computation | async-start | bytes 524288 | tf_op jit(solution)/shard_map/all_to_all | solution.py:180
  23.4 1.9 %collective-permute-start.2 = (bf16[512,1024]{1,0:T(8,128)(2,1)}, bf16[512,1024]{1,0:T(8,128)(2,1)}, u32[]{:S(2)}, u32[]{:S(2)}) collective-permute-start(bf16[512,1024]{1,0:T(8,128)(2,1)} %bitcast.15), channel_id=1, source_target_pairs={{2,0},{7,1},{4,2},{1,3},{6,4},{3,5},{0,6},{5,7},{10,8},{15,9},{12,... | collective-permute-start | bytes 3145736 | tf_op jit(solution)/shard_map/ppermute | solution.py:190
  25.3 0.0 collective-permute-done.1.refs_1_
  25.3 4.6 %collective-permute-start.3 = (bf16[512,1024]{1,0:T(8,128)(2,1)}, bf16[512,1024]{1,0:T(8,128)(2,1)}, u32[]{:S(2)}, u32[]{:S(2)}) collective-permute-start(bf16[512,1024]{1,0:T(8,128)(2,1)} %collective-permute-done.1.refs_1_), channel_id=1, source_target_pairs={{0,2},{1,7},{2,4},{3,1},{4,6},{5,3},{6,0},{7,5},{8,10},{9,15},{10,... | collective-permute-start | bytes 3145736 | tf_op jit(solution)/shard_map/ppermute | solution.py:192
  29.9 0.0 copy-done
  29.9 0.0 copy-start.3
  29.9 1.1 dynamic-slice_reduce_fusion
  31.1 1.0 reshape.14.start_ref
  32.0 5.0 %all-to-all-done.table_ref = bf16[64,16,128]{2,1,0:T(8,128)(2,1)S(1)} async-done(((bf16[64,16,128]{2,1,0:T(8,128)(2,1)}), bf16[64,16,128]{2,1,0:T(8,128)(2,1)S(1)}, u32[]{:S(2)}, u32[]{:S(2)}) %all-to-all-start) | async-done | bytes 262176 | tf_op jit(solution)/shard_map/all_to_all | solution.py:180
  37.0 0.0 copy-start.2
  37.1 0.7 slice_select_fusion.rows_ref
  37.8 0.0 copy-done.2
  37.8 2.3 %shard_map.74 = bf16[256,8,128]{2,1,0:T(8,128)(2,1)} custom-call(s32[64,4]{1,0:T(8,128)} %slice_select_fusion.rows_ref, bf16[64,16,128]{2,1,0:T(8,128)(2,1)} %copy-done.2), custom_call_target="tpu_custom_call" | custom-call | tf_op jit(solution)/shard_map/pallas_call | solution.py:198
  40.1 10.7 %all-to-all-start.1 = ((bf16[256,8,128]{2,1,0:T(8,128)(2,1)}), bf16[256,8,128]{2,1,0:T(8,128)(2,1)S(1)}, u32[]{:S(2)}, u32[]{:S(2)}) async-start(bf16[256,8,128]{2,1,0:T(8,128)(2,1)} %shard_map.74), calls=%async_computation.1 | async-start | bytes 1048576 | tf_op jit(solution)/shard_map/all_to_all | solution.py:205
  50.8 0.0 copy-done.3
  50.8 4.2 %collective-permute-start.4 = (bf16[512,1024]{1,0:T(8,128)(2,1)S(1)}, bf16[512,1024]{1,0:T(8,128)(2,1)}, u32[]{:S(2)}, u32[]{:S(2)}) collective-permute-start(bf16[512,1024]{1,0:T(8,128)(2,1)S(1)} %bitcast.17), channel_id=1, source_target_pairs={{0,1},{1,0},{2,3},{3,2},{4,5},{5,4},{6,7},{7,6},{8,9},{9,8},{10,11... | collective-permute-start | bytes 3145736 | tf_op jit(solution)/shard_map/ppermute | solution.py:208
  55.0 1.9 %collective-permute-start.5 = (bf16[512,1024]{1,0:T(8,128)(2,1)}, bf16[512,1024]{1,0:T(8,128)(2,1)}, u32[]{:S(2)}, u32[]{:S(2)}) collective-permute-start(bf16[512,1024]{1,0:T(8,128)(2,1)} %collective-permute-done.1.refs_1_), channel_id=1, source_target_pairs={{0,1},{1,0},{2,3},{3,2},{4,5},{5,4},{6,7},{7,6},{8,9},{9,8},{10,11... | collective-permute-start | bytes 3145736 | tf_op jit(solution)/shard_map/ppermute | solution.py:208
  56.9 0.0 collective-permute-done.2.refs_2_
  56.9 2.4 %collective-permute-start.6 = (bf16[512,1024]{1,0:T(8,128)(2,1)}, bf16[512,1024]{1,0:T(8,128)(2,1)}, u32[]{:S(2)}, u32[]{:S(2)}) collective-permute-start(bf16[512,1024]{1,0:T(8,128)(2,1)} %collective-permute-done.2.refs_2_), channel_id=1, source_target_pairs={{0,1},{1,0},{2,3},{3,2},{4,5},{5,4},{6,7},{7,6},{8,9},{9,8},{10,11... | collective-permute-start | bytes 3145736 | tf_op jit(solution)/shard_map/ppermute | solution.py:208
  59.4 0.0 collective-permute-done.3.refs_3_
  59.4 1.9 %collective-permute-start.7 = (bf16[512,1024]{1,0:T(8,128)(2,1)}, bf16[512,1024]{1,0:T(8,128)(2,1)}, u32[]{:S(2)}, u32[]{:S(2)}) collective-permute-start(bf16[512,1024]{1,0:T(8,128)(2,1)} %collective-permute-done.3.refs_3_), channel_id=1, source_target_pairs={{0,1},{1,0},{2,3},{3,2},{4,5},{5,4},{6,7},{7,6},{8,9},{9,8},{10,11... | collective-permute-start | bytes 3145736 | tf_op jit(solution)/shard_map/ppermute | solution.py:208
  61.3 5.5 %all-to-all-done.1.own_ref = bf16[256,8,128]{2,1,0:T(8,128)(2,1)S(1)} async-done(((bf16[256,8,128]{2,1,0:T(8,128)(2,1)}), bf16[256,8,128]{2,1,0:T(8,128)(2,1)S(1)}, u32[]{:S(2)}, u32[]{:S(2)}) %all-to-all-start.1) | async-done | bytes 524320 | tf_op jit(solution)/shard_map/all_to_all | solution.py:205
  66.8 0.0 copy-start.1
  66.8 6.7 %collective-permute-start = (bf16[256,8,128]{2,1,0:T(8,128)(2,1)S(1)}, bf16[256,8,128]{2,1,0:T(8,128)(2,1)S(1)}, u32[]{:S(2)}, u32[]{:S(2)}) collective-permute-start(bf16[256,8,128]{2,1,0:T(8,128)(2,1)S(1)} %all-to-all-done.1.own_ref), channel_id=1, source_target_pairs={{0,1},{1,0},{2,3},{3,2},{4,5},{5,4},{6,7},{7,6},{8,9},{9,8},{10,11... | collective-permute-start | bytes 1572872 | tf_op jit(solution)/shard_map/ppermute | solution.py:209
  73.5 0.0 collective-permute-done.4.refs_4_
  73.5 1.3 %collective-permute-done.other_ref = bf16[256,8,128]{2,1,0:T(8,128)(2,1)S(1)} collective-permute-done((bf16[256,8,128]{2,1,0:T(8,128)(2,1)S(1)}, bf16[256,8,128]{2,1,0:T(8,128)(2,1)S(1)}, u32[]{:S(2)}, u32[]{:S(2)}) %collective-permute-start) | collective-permute-done | bytes 524320 | tf_op jit(solution)/shard_map/ppermute | solution.py:209
  74.8 0.0 copy-start.4
  74.8 0.0 collective-permute-done.6.refs_6_
  74.8 0.0 collective-permute-done.5.refs_5_
  74.8 0.0 collective-permute-done.7.refs_7_
  74.9 0.0 copy-done.1
  74.9 0.8 copy-done.4
  75.6 17.8 %shard_map.75 = bf16[720,128]{1,0:T(8,128)(2,1)} custom-call(s32[2,4]{1,0:T(2,128)} %bitcast.22, f32[64,96]{1,0:T(8,128)} %low_ref.1, f32[64,96]{1,0:T(8,128)} %high_ref.1, bf16[256,8,128]{2,1,0:T(8,128)(2,1)} %copy-done.1, bf16[256,8,128]{2,1,0:T(8,128)(2,1)} %copy-done.4, bf16[960,96]{1,0:T(8,128)(2,1)} %reshape.14.start_ref, bf16[512,1024]{1,0:T(8,128)(2,1)} %bitcast.16, ...), custom_call_target="tpu_custom_call" | custom-call | tf_op jit(solution)/shard_map/pallas_call | solution.py:211
  93.5 11.0 %all_gather.3 = bf16[4,10,72,128]{3,2,1,0:T(8,128)(2,1)S(1)} all-gather(bf16[1,10,72,128]{3,2,1,0:T(8,128)(2,1)} %bitcast.19), channel_id=1, replica_groups=mesh['pb'=64,'row'=4,'col'=2] {'row'}, dimensions={0}, use_global_device_ids=true | all-gather | bytes 921600 | tf_op jit(solution)/shard_map/all_gather | solution.py:231
  104.5 5.5 %collective-permute-start.8 = (bf16[4,10,72,128]{3,2,1,0:T(8,128)(2,1)S(1)}, bf16[4,10,72,128]{3,2,1,0:T(8,128)(2,1)S(1)}, u32[]{:S(2)}, u32[]{:S(2)}) collective-permute-start(bf16[4,10,72,128]{3,2,1,0:T(8,128)(2,1)S(1)} %all_gather.3), channel_id=1, source_target_pairs={{0,1},{1,0},{2,3},{3,2},{4,5},{5,4},{6,7},{7,6},{8,9},{9,8},{10,11... | collective-permute-start | bytes 2211848 | tf_op jit(solution)/shard_map/ppermute | solution.py:232
  110.0 1.8 %collective-permute-done.8 = bf16[4,10,72,128]{3,2,1,0:T(8,128)(2,1)S(1)} collective-permute-done((bf16[4,10,72,128]{3,2,1,0:T(8,128)(2,1)S(1)}, bf16[4,10,72,128]{3,2,1,0:T(8,128)(2,1)S(1)}, u32[]{:S(2)}, u32[]{:S(2)}) %collective-permute-start.8) | collective-permute-done | bytes 737312 | tf_op jit(solution)/shard_map/ppermute | solution.py:232
  111.8 0.2 fusion
  112.0 0.1 copy.10
  112.2 1.3 %reshape.15 = bf16[1,20,4,9216]{3,2,1,0:T(4,128)(2,1)} reshape(bf16[2,10,4,72,128]{4,3,2,1,0:T(8,128)(2,1)S(1)} %copy.10) | data formatting | bytes 2949120 | tf_op jit(solution)/shard_map/reshape | solution.py:234
  (1 shorter events, 0.0 us)
Async XLA Ops:
  0.0 29.9 %copy-start = (bf16[1,20,4,9216]{3,2,1,0:T(4,128)(2,1)S(1)}, bf16[1,20,4,9216]{3,2,1,0:T(4,128)(2,1)}, u32[]{:S(2)}) copy-start(bf16[1,20,4,9216]{3,2,1,0:T(4,128)(2,1)} %param.7) | copy-start | bytes 4423684
  1.8 23.5 %collective-permute-start.1 = (bf16[512,1024]{1,0:T(8,128)(2,1)}, bf16[512,1024]{1,0:T(8,128)(2,1)}, u32[]{:S(2)}, u32[]{:S(2)}) collective-permute-start(bf16[512,1024]{1,0:T(8,128)(2,1)} %bitcast.14), channel_id=1, source_target_pairs={{0,2},{1,7},{2,4},{3,1},{4,6},{5,3},{6,0},{7,5},{8,10},{9,15},{10,... | collective-permute-start | bytes 3145736 | tf_op jit(solution)/shard_map/ppermute | solution.py:189
  7.1 30.0 %all-to-all-start = ((bf16[64,16,128]{2,1,0:T(8,128)(2,1)}), bf16[64,16,128]{2,1,0:T(8,128)(2,1)S(1)}, u32[]{:S(2)}, u32[]{:S(2)}) async-start(bf16[64,16,128]{2,1,0:T(8,128)(2,1)} %shard_map.73), calls=%async_computation | async-start | bytes 524288 | tf_op jit(solution)/shard_map/all_to_all | solution.py:180
  23.4 33.5 %collective-permute-start.2 = (bf16[512,1024]{1,0:T(8,128)(2,1)}, bf16[512,1024]{1,0:T(8,128)(2,1)}, u32[]{:S(2)}, u32[]{:S(2)}) collective-permute-start(bf16[512,1024]{1,0:T(8,128)(2,1)} %bitcast.15), channel_id=1, source_target_pairs={{2,0},{7,1},{4,2},{1,3},{6,4},{3,5},{0,6},{5,7},{10,8},{15,9},{12,... | collective-permute-start | bytes 3145736 | tf_op jit(solution)/shard_map/ppermute | solution.py:190
  25.3 34.0 %collective-permute-start.3 = (bf16[512,1024]{1,0:T(8,128)(2,1)}, bf16[512,1024]{1,0:T(8,128)(2,1)}, u32[]{:S(2)}, u32[]{:S(2)}) collective-permute-start(bf16[512,1024]{1,0:T(8,128)(2,1)} %collective-permute-done.1.refs_1_), channel_id=1, source_target_pairs={{0,2},{1,7},{2,4},{3,1},{4,6},{5,3},{6,0},{7,5},{8,10},{9,15},{10,... | collective-permute-start | bytes 3145736 | tf_op jit(solution)/shard_map/ppermute | solution.py:192
  29.9 20.9 %copy-start.3 = (bf16[1,512,1024]{2,1,0:T(8,128)(2,1)S(1)}, bf16[1,512,1024]{2,1,0:T(8,128)(2,1)}, u32[]{:S(2)}) copy-start(bf16[1,512,1024]{2,1,0:T(8,128)(2,1)} %param.13) | copy-start | bytes 3145732
  37.0 0.7 copy-start.2
  40.1 26.7 %all-to-all-start.1 = ((bf16[256,8,128]{2,1,0:T(8,128)(2,1)}), bf16[256,8,128]{2,1,0:T(8,128)(2,1)S(1)}, u32[]{:S(2)}, u32[]{:S(2)}) async-start(bf16[256,8,128]{2,1,0:T(8,128)(2,1)} %shard_map.74), calls=%async_computation.1 | async-start | bytes 1048576 | tf_op jit(solution)/shard_map/all_to_all | solution.py:205
  50.8 22.7 %collective-permute-start.4 = (bf16[512,1024]{1,0:T(8,128)(2,1)S(1)}, bf16[512,1024]{1,0:T(8,128)(2,1)}, u32[]{:S(2)}, u32[]{:S(2)}) collective-permute-start(bf16[512,1024]{1,0:T(8,128)(2,1)S(1)} %bitcast.17), channel_id=1, source_target_pairs={{0,1},{1,0},{2,3},{3,2},{4,5},{5,4},{6,7},{7,6},{8,9},{9,8},{10,11... | collective-permute-start | bytes 3145736 | tf_op jit(solution)/shard_map/ppermute | solution.py:208
  55.0 19.8 %collective-permute-start.5 = (bf16[512,1024]{1,0:T(8,128)(2,1)}, bf16[512,1024]{1,0:T(8,128)(2,1)}, u32[]{:S(2)}, u32[]{:S(2)}) collective-permute-start(bf16[512,1024]{1,0:T(8,128)(2,1)} %collective-permute-done.1.refs_1_), channel_id=1, source_target_pairs={{0,1},{1,0},{2,3},{3,2},{4,5},{5,4},{6,7},{7,6},{8,9},{9,8},{10,11... | collective-permute-start | bytes 3145736 | tf_op jit(solution)/shard_map/ppermute | solution.py:208
  56.9 17.9 %collective-permute-start.6 = (bf16[512,1024]{1,0:T(8,128)(2,1)}, bf16[512,1024]{1,0:T(8,128)(2,1)}, u32[]{:S(2)}, u32[]{:S(2)}) collective-permute-start(bf16[512,1024]{1,0:T(8,128)(2,1)} %collective-permute-done.2.refs_2_), channel_id=1, source_target_pairs={{0,1},{1,0},{2,3},{3,2},{4,5},{5,4},{6,7},{7,6},{8,9},{9,8},{10,11... | collective-permute-start | bytes 3145736 | tf_op jit(solution)/shard_map/ppermute | solution.py:208
  59.4 15.5 %collective-permute-start.7 = (bf16[512,1024]{1,0:T(8,128)(2,1)}, bf16[512,1024]{1,0:T(8,128)(2,1)}, u32[]{:S(2)}, u32[]{:S(2)}) collective-permute-start(bf16[512,1024]{1,0:T(8,128)(2,1)} %collective-permute-done.3.refs_3_), channel_id=1, source_target_pairs={{0,1},{1,0},{2,3},{3,2},{4,5},{5,4},{6,7},{7,6},{8,9},{9,8},{10,11... | collective-permute-start | bytes 3145736 | tf_op jit(solution)/shard_map/ppermute | solution.py:208
  66.8 8.1 %copy-start.1 = (bf16[256,8,128]{2,1,0:T(8,128)(2,1)}, bf16[256,8,128]{2,1,0:T(8,128)(2,1)S(1)}, u32[]{:S(2)}) copy-start(bf16[256,8,128]{2,1,0:T(8,128)(2,1)S(1)} %all-to-all-done.1.own_ref) | copy-start | bytes 1572868
  66.8 8.0 %collective-permute-start = (bf16[256,8,128]{2,1,0:T(8,128)(2,1)S(1)}, bf16[256,8,128]{2,1,0:T(8,128)(2,1)S(1)}, u32[]{:S(2)}, u32[]{:S(2)}) collective-permute-start(bf16[256,8,128]{2,1,0:T(8,128)(2,1)S(1)} %all-to-all-done.1.own_ref), channel_id=1, source_target_pairs={{0,1},{1,0},{2,3},{3,2},{4,5},{5,4},{6,7},{7,6},{8,9},{9,8},{10,11... | collective-permute-start | bytes 1572872 | tf_op jit(solution)/shard_map/ppermute | solution.py:209
  74.8 0.8 copy-start.4
  104.5 7.3 %collective-permute-start.8 = (bf16[4,10,72,128]{3,2,1,0:T(8,128)(2,1)S(1)}, bf16[4,10,72,128]{3,2,1,0:T(8,128)(2,1)S(1)}, u32[]{:S(2)}, u32[]{:S(2)}) collective-permute-start(bf16[4,10,72,128]{3,2,1,0:T(8,128)(2,1)S(1)} %all_gather.3), channel_id=1, source_target_pairs={{0,1},{1,0},{2,3},{3,2},{4,5},{5,4},{6,7},{7,6},{8,9},{9,8},{10,11... | collective-permute-start | bytes 2211848 | tf_op jit(solution)/shard_map/ppermute | solution.py:232

commit v4 on v3

--- a/solution.py
+++ b/solution.py
@@ -9,7 +9,7 @@
 HALF = 2.5
 LANES = 128
 ROWS = 8
-VMEM_LIMIT = 56 * 1024 * 1024
+VMEM_LIMIT = 28 * 1024 * 1024
 
 
 def pack_kernel(pairs_ref, stored_ref, orbitals_ref, out_ref):
@@ -97,9 +97,15 @@
     screened_in[...] = jnp.zeros_like(screened_in)
 
     def kernel_term(current_ref):
-        inner = jnp.dot(current_ref[...], conduction[...], preferred_element_type=jnp.float32)
-        inner = inner.reshape(vectors, count_v, points) * valence[...][None]
-        screened_in[:vectors, :] = jnp.sum(inner, axis=1)
+        chunk = 512
+        def expand(step, carry):
+            lanes = pl.ds(pl.multiple_of(step * chunk, chunk), chunk)
+            inner = jnp.dot(current_ref[...], conduction[:, lanes], preferred_element_type=jnp.float32)
+            inner = inner.reshape(vectors, count_v, chunk) * valence[:, lanes][None]
+            screened_in[:vectors, lanes] = jnp.sum(inner, axis=1)
+            return carry
+
+        lax.fori_loop(0, points // chunk, expand, 0, unroll=True)
         values = screened_in[...].astype(jnp.bfloat16)
         if current_ref is start_ref:
             for copy in copies:
@@ -114,11 +120,21 @@
                     preferred_element_type=jnp.float32,
                 )
             screened_out[:, row * rows_w : (row + 1) * rows_w] = summed
-        weighted = screened_out[:vectors, :][:, None, :] * valence[...][None]
-        weighted = weighted.reshape(flat_rows, points).astype(jnp.bfloat16)
-        total[...] = lax.dot_general(
-            weighted, conduction[...], (((1,), (1,)), ((), ())), preferred_element_type=jnp.float32
-        )
+        total[...] = jnp.zeros_like(total)
+
+        def project(step, carry):
+            lanes = pl.ds(pl.multiple_of(step * chunk, chunk), chunk)
+            weighted = screened_out[:vectors, lanes][:, None, :] * valence[:, lanes][None]
+            weighted = weighted.reshape(flat_rows, chunk).astype(jnp.bfloat16)
+            total[...] += lax.dot_general(
+                weighted,
+                conduction[:, lanes],
+                (((1,), (1,)), ((), ())),
+                preferred_element_type=jnp.float32,
+            )
+            return carry
+
+        lax.fori_loop(0, points // chunk, project, 0, unroll=True)
 
     low = low_ref[pl.ds(pairs_ref[0, pair], 1), :]
     high = high_ref[pl.ds(pairs_ref[1, pair], 1), :]

time: 114 us -> 108 us (0.947)
  Pallas kernels: 22 us -> 16.2 us
    pallas_call x1, Pallas kernels: 17.8 us -> 12.7 us  [on_device(): pl.pallas_call(steps_kernel, out_shape=jax.ShapeDtypeStruct((flat_rows *...]
    unnamed x10 -> x16, local copies, waits for them, and re-layouts: 0.79 us -> 2.37 us
  transfers between devices with their start and end apart: 11 -> 11, of which waited for: 4 -> 4; matrix products, arithmetic and copies ran while one was open for 2% -> 1% of each run, Pallas kernels for 2% -> 2%
where the time goes in v4:
time: 108 us
  starting transfers between devices  60.7 us (56%)
  Pallas kernels  16.2 us (15%)
  waiting for transfers between devices  14.3 us (13%)
  blocking collectives  10.8 us (10%)
  local copies, waits for them, and re-layouts  5.18 us (5%)
    all_to_all x1, starting transfers between devices, on_device(): table = lax.all_to_all(message, 'pb', 0, 0, tiled=True)  16.3 us
    pallas_call x1, Pallas kernels, on_device(): pl.pallas_call(steps_kernel, out_shape=jax.ShapeDtypeStruct((flat_rows *...  12.7 us
    all_gather x1, blocking collectives, on_device(): across = lax.all_gather(mine, 'row')  10.8 us
    ppermute x4, starting transfers between devices, on_device(): w_tiles = w_core + [lax.ppermute(tile, 'col', swap) for tile in w_core]  10.4 us
    all_to_all x1, starting transfers between devices, on_device(): own = lax.all_to_all(chosen, ('pb', 'row'), 0, 0, tiled=True)  10.1 us
    ppermute x1, starting transfers between devices, on_device(): other = lax.ppermute(own, 'col', swap)  6.7 us
    all_to_all x1, waiting for transfers between devices, on_device(): table = lax.all_to_all(message, 'pb', 0, 0, tiled=True)  5.68 us
    all_to_all x1, waiting for transfers between devices, on_device(): own = lax.all_to_all(chosen, ('pb', 'row'), 0, 0, tiled=True)  5.5 us
  transfers between devices with their start and end apart: 11, of which 4 were waited for; matrix products, arithmetic and copies ran while one was open for 1% of the time, Pallas kernels for 2%

profile of v4, /device:TPU:1, one launch (start us, length us, event | category | flops | bytes accessed | tf_op | source)
XLA Modules:
  0.0 107.9 jit_solution(9685471082941775029)
XLA Ops:
  0.0 0.0 copy-start
  0.0 0.0 copy-start.2
  0.0 1.0 copy-done.2
  1.0 0.0 copy-start.5
  1.0 0.7 copy-done.5
  1.7 0.0 copy-start.7
  1.7 0.7 copy-done.7
  2.3 1.4 %shard_map.73 = bf16[64,16,128]{2,1,0:T(8,128)(2,1)} custom-call(s32[2,4]{1,0:T(2,128)S(1)} %bitcast.18, s32[1,64]{1,0:T(1,128)S(1)} %bitcast.20, bf16[1,192,256]{2,1,0:T(8,128)(2,1)S(1)} %copy-done.2), custom_call_target="tpu_custom_call" | custom-call | tf_op jit(solution)/shard_map/pallas_call | solution.py:189
  3.7 5.2 %collective-permute-start.1 = (bf16[512,1024]{1,0:T(8,128)(2,1)}, bf16[512,1024]{1,0:T(8,128)(2,1)}, u32[]{:S(2)}, u32[]{:S(2)}) collective-permute-start(bf16[512,1024]{1,0:T(8,128)(2,1)} %bitcast.13), channel_id=1, source_target_pairs={{0,2},{1,7},{2,4},{3,1},{4,6},{5,3},{6,0},{7,5},{8,10},{9,15},{10,... | collective-permute-start | bytes 3145736 | tf_op jit(solution)/shard_map/ppermute | solution.py:205
  8.9 16.3 %all-to-all-start = ((bf16[64,16,128]{2,1,0:T(8,128)(2,1)}), bf16[64,16,128]{2,1,0:T(8,128)(2,1)S(1)}, u32[]{:S(2)}, u32[]{:S(2)}) async-start(bf16[64,16,128]{2,1,0:T(8,128)(2,1)} %shard_map.73), calls=%async_computation | async-start | bytes 524288 | tf_op jit(solution)/shard_map/all_to_all | solution.py:196
  25.2 1.9 %collective-permute-start.2 = (bf16[512,1024]{1,0:T(8,128)(2,1)}, bf16[512,1024]{1,0:T(8,128)(2,1)}, u32[]{:S(2)}, u32[]{:S(2)}) collective-permute-start(bf16[512,1024]{1,0:T(8,128)(2,1)} %bitcast.14), channel_id=1, source_target_pairs={{2,0},{7,1},{4,2},{1,3},{6,4},{3,5},{0,6},{5,7},{10,8},{15,9},{12,... | collective-permute-start | bytes 3145736 | tf_op jit(solution)/shard_map/ppermute | solution.py:206
  27.2 0.0 collective-permute-done.1.refs_1_
  27.2 4.6 %collective-permute-start.3 = (bf16[512,1024]{1,0:T(8,128)(2,1)}, bf16[512,1024]{1,0:T(8,128)(2,1)}, u32[]{:S(2)}, u32[]{:S(2)}) collective-permute-start(bf16[512,1024]{1,0:T(8,128)(2,1)} %collective-permute-done.1.refs_1_), channel_id=1, source_target_pairs={{0,2},{1,7},{2,4},{3,1},{4,6},{5,3},{6,0},{7,5},{8,10},{9,15},{10,... | collective-permute-start | bytes 3145736 | tf_op jit(solution)/shard_map/ppermute | solution.py:208
  31.8 0.0 copy-done
  31.8 0.0 copy-start.1
  31.8 0.0 copy-start.3
  31.8 0.0 copy-start.4
  31.8 0.0 copy-start.6
  31.8 1.1 %dynamic-slice_reduce_fusion = bf16[10,9216]{1,0:T(8,128)(2,1)S(1)} fusion(bf16[1,20,4,9216]{3,2,1,0:T(4,128)(2,1)S(1)} %copy-done, s32[]{:T(128)S(6)} %mul.3, s32[]{:T(128)S(6)} %axis_index.38), kind=kLoop, calls=%fused_computation.2 | loop fusion | bytes 368648 | tf_op jit(solution)/shard_map/dynamic_slice | solution.py:198
  33.0 0.2 reshape.14.start_ref
  33.2 5.7 %all-to-all-done.table_ref = bf16[64,16,128]{2,1,0:T(8,128)(2,1)S(1)} async-done(((bf16[64,16,128]{2,1,0:T(8,128)(2,1)}), bf16[64,16,128]{2,1,0:T(8,128)(2,1)S(1)}, u32[]{:S(2)}, u32[]{:S(2)}) %all-to-all-start) | async-done | bytes 262176 | tf_op jit(solution)/shard_map/all_to_all | solution.py:196
  38.9 0.1 slice_select_fusion.rows_ref
  39.0 2.2 %shard_map.74 = bf16[256,8,128]{2,1,0:T(8,128)(2,1)} custom-call(s32[64,4]{1,0:T(8,128)S(1)} %slice_select_fusion.rows_ref, bf16[64,16,128]{2,1,0:T(8,128)(2,1)S(1)} %all-to-all-done.table_ref), custom_call_target="tpu_custom_call" | custom-call | tf_op jit(solution)/shard_map/pallas_call | solution.py:214
  41.2 10.1 %all-to-all-start.1 = ((bf16[256,8,128]{2,1,0:T(8,128)(2,1)}), bf16[256,8,128]{2,1,0:T(8,128)(2,1)S(1)}, u32[]{:S(2)}, u32[]{:S(2)}) async-start(bf16[256,8,128]{2,1,0:T(8,128)(2,1)} %shard_map.74), calls=%async_computation.1 | async-start | bytes 1048576 | tf_op jit(solution)/shard_map/all_to_all | solution.py:221
  51.3 0.0 copy-done.1
  51.3 4.2 %collective-permute-start.4 = (bf16[512,1024]{1,0:T(8,128)(2,1)S(1)}, bf16[512,1024]{1,0:T(8,128)(2,1)}, u32[]{:S(2)}, u32[]{:S(2)}) collective-permute-start(bf16[512,1024]{1,0:T(8,128)(2,1)S(1)} %bitcast.15), channel_id=1, source_target_pairs={{0,1},{1,0},{2,3},{3,2},{4,5},{5,4},{6,7},{7,6},{8,9},{9,8},{10,11... | collective-permute-start | bytes 3145736 | tf_op jit(solution)/shard_map/ppermute | solution.py:224
  55.5 1.9 %collective-permute-start.5 = (bf16[512,1024]{1,0:T(8,128)(2,1)}, bf16[512,1024]{1,0:T(8,128)(2,1)}, u32[]{:S(2)}, u32[]{:S(2)}) collective-permute-start(bf16[512,1024]{1,0:T(8,128)(2,1)} %collective-permute-done.1.refs_1_), channel_id=1, source_target_pairs={{0,1},{1,0},{2,3},{3,2},{4,5},{5,4},{6,7},{7,6},{8,9},{9,8},{10,11... | collective-permute-start | bytes 3145736 | tf_op jit(solution)/shard_map/ppermute | solution.py:224
  57.4 0.0 collective-permute-done.2.refs_2_
  57.4 2.4 %collective-permute-start.6 = (bf16[512,1024]{1,0:T(8,128)(2,1)}, bf16[512,1024]{1,0:T(8,128)(2,1)}, u32[]{:S(2)}, u32[]{:S(2)}) collective-permute-start(bf16[512,1024]{1,0:T(8,128)(2,1)} %collective-permute-done.2.refs_2_), channel_id=1, source_target_pairs={{0,1},{1,0},{2,3},{3,2},{4,5},{5,4},{6,7},{7,6},{8,9},{9,8},{10,11... | collective-permute-start | bytes 3145736 | tf_op jit(solution)/shard_map/ppermute | solution.py:224
  59.8 0.0 collective-permute-done.3.refs_3_
  59.8 1.9 %collective-permute-start.7 = (bf16[512,1024]{1,0:T(8,128)(2,1)}, bf16[512,1024]{1,0:T(8,128)(2,1)}, u32[]{:S(2)}, u32[]{:S(2)}) collective-permute-start(bf16[512,1024]{1,0:T(8,128)(2,1)} %collective-permute-done.3.refs_3_), channel_id=1, source_target_pairs={{0,1},{1,0},{2,3},{3,2},{4,5},{5,4},{6,7},{7,6},{8,9},{9,8},{10,11... | collective-permute-start | bytes 3145736 | tf_op jit(solution)/shard_map/ppermute | solution.py:224
  61.8 5.5 %all-to-all-done.1.own_ref = bf16[256,8,128]{2,1,0:T(8,128)(2,1)S(1)} async-done(((bf16[256,8,128]{2,1,0:T(8,128)(2,1)}), bf16[256,8,128]{2,1,0:T(8,128)(2,1)S(1)}, u32[]{:S(2)}, u32[]{:S(2)}) %all-to-all-start.1) | async-done | bytes 524320 | tf_op jit(solution)/shard_map/all_to_all | solution.py:221
  67.3 6.7 %collective-permute-start = (bf16[256,8,128]{2,1,0:T(8,128)(2,1)S(1)}, bf16[256,8,128]{2,1,0:T(8,128)(2,1)S(1)}, u32[]{:S(2)}, u32[]{:S(2)}) collective-permute-start(bf16[256,8,128]{2,1,0:T(8,128)(2,1)S(1)} %all-to-all-done.1.own_ref), channel_id=1, source_target_pairs={{0,1},{1,0},{2,3},{3,2},{4,5},{5,4},{6,7},{7,6},{8,9},{9,8},{10,11... | collective-permute-start | bytes 1572872 | tf_op jit(solution)/shard_map/ppermute | solution.py:225
  74.0 0.0 collective-permute-done.4.refs_4_
  74.0 1.3 %collective-permute-done.other_ref = bf16[256,8,128]{2,1,0:T(8,128)(2,1)S(1)} collective-permute-done((bf16[256,8,128]{2,1,0:T(8,128)(2,1)S(1)}, bf16[256,8,128]{2,1,0:T(8,128)(2,1)S(1)}, u32[]{:S(2)}, u32[]{:S(2)}) %collective-permute-start) | collective-permute-done | bytes 524320 | tf_op jit(solution)/shard_map/ppermute | solution.py:225
  75.3 0.0 collective-permute-done.6.refs_6_
  75.3 0.0 collective-permute-done.5.refs_5_
  75.3 0.0 collective-permute-done.7.refs_7_
  75.3 0.0 copy-done.3
  75.3 0.0 copy-done.4
  75.3 0.0 copy-done.6
  75.3 12.7 %shard_map.75 = bf16[720,128]{1,0:T(8,128)(2,1)S(1)} custom-call(s32[2,4]{1,0:T(2,128)S(1)} %bitcast.19, f32[64,96]{1,0:T(8,128)S(1)} %copy-done.3, f32[64,96]{1,0:T(8,128)S(1)} %copy-done.4, bf16[256,8,128]{2,1,0:T(8,128)(2,1)S(1)} %all-to-all-done.1.own_ref, bf16[256,8,128]{2,1,0:T(8,128)(2,1)S(1)} %collective-permute-done.other_ref, ...), custom_call_target="tpu_custom_call" | custom-call | tf_op jit(solution)/shard_map/pallas_call | solution.py:227
  88.1 10.8 %all_gather.3 = bf16[4,10,72,128]{3,2,1,0:T(8,128)(2,1)S(1)} all-gather(bf16[1,10,72,128]{3,2,1,0:T(8,128)(2,1)S(1)} %bitcast.17), channel_id=1, replica_groups=mesh['pb'=64,'row'=4,'col'=2] {'row'}, dimensions={0}, use_global_device_ids=true | all-gather | bytes 921600 | tf_op jit(solution)/shard_map/all_gather | solution.py:247
  98.9 5.5 %collective-permute-start.8 = (bf16[4,10,72,128]{3,2,1,0:T(8,128)(2,1)S(1)}, bf16[4,10,72,128]{3,2,1,0:T(8,128)(2,1)S(1)}, u32[]{:S(2)}, u32[]{:S(2)}) collective-permute-start(bf16[4,10,72,128]{3,2,1,0:T(8,128)(2,1)S(1)} %all_gather.3), channel_id=1, source_target_pairs={{0,1},{1,0},{2,3},{3,2},{4,5},{5,4},{6,7},{7,6},{8,9},{9,8},{10,11... | collective-permute-start | bytes 2211848 | tf_op jit(solution)/shard_map/ppermute | solution.py:248
  104.4 1.8 %collective-permute-done.8 = bf16[4,10,72,128]{3,2,1,0:T(8,128)(2,1)S(1)} collective-permute-done((bf16[4,10,72,128]{3,2,1,0:T(8,128)(2,1)S(1)}, bf16[4,10,72,128]{3,2,1,0:T(8,128)(2,1)S(1)}, u32[]{:S(2)}, u32[]{:S(2)}) %collective-permute-start.8) | collective-permute-done | bytes 737312 | tf_op jit(solution)/shard_map/ppermute | solution.py:248
  106.2 0.2 fusion
  106.4 0.1 copy.10
  106.6 1.3 %reshape.15 = bf16[1,20,4,9216]{3,2,1,0:T(4,128)(2,1)} reshape(bf16[2,10,4,72,128]{4,3,2,1,0:T(8,128)(2,1)S(1)} %copy.10) | data formatting | bytes 2949120 | tf_op jit(solution)/shard_map/reshape | solution.py:250
  (1 shorter events, 0.0 us)
Async XLA Ops:
  0.0 31.8 %copy-start = (bf16[1,20,4,9216]{3,2,1,0:T(4,128)(2,1)S(1)}, bf16[1,20,4,9216]{3,2,1,0:T(4,128)(2,1)}, u32[]{:S(2)}) copy-start(bf16[1,20,4,9216]{3,2,1,0:T(4,128)(2,1)} %param.7) | copy-start | bytes 4423684
  0.0 1.0 copy-start.2
  1.0 0.7 copy-start.5
  1.7 0.7 copy-start.7
  3.7 23.5 %collective-permute-start.1 = (bf16[512,1024]{1,0:T(8,128)(2,1)}, bf16[512,1024]{1,0:T(8,128)(2,1)}, u32[]{:S(2)}, u32[]{:S(2)}) collective-permute-start(bf16[512,1024]{1,0:T(8,128)(2,1)} %bitcast.13), channel_id=1, source_target_pairs={{0,2},{1,7},{2,4},{3,1},{4,6},{5,3},{6,0},{7,5},{8,10},{9,15},{10,... | collective-permute-start | bytes 3145736 | tf_op jit(solution)/shard_map/ppermute | solution.py:205
  8.9 30.0 %all-to-all-start = ((bf16[64,16,128]{2,1,0:T(8,128)(2,1)}), bf16[64,16,128]{2,1,0:T(8,128)(2,1)S(1)}, u32[]{:S(2)}, u32[]{:S(2)}) async-start(bf16[64,16,128]{2,1,0:T(8,128)(2,1)} %shard_map.73), calls=%async_computation | async-start | bytes 524288 | tf_op jit(solution)/shard_map/all_to_all | solution.py:196
  25.2 32.1 %collective-permute-start.2 = (bf16[512,1024]{1,0:T(8,128)(2,1)}, bf16[512,1024]{1,0:T(8,128)(2,1)}, u32[]{:S(2)}, u32[]{:S(2)}) collective-permute-start(bf16[512,1024]{1,0:T(8,128)(2,1)} %bitcast.14), channel_id=1, source_target_pairs={{2,0},{7,1},{4,2},{1,3},{6,4},{3,5},{0,6},{5,7},{10,8},{15,9},{12,... | collective-permute-start | bytes 3145736 | tf_op jit(solution)/shard_map/ppermute | solution.py:206
  27.2 32.6 %collective-permute-start.3 = (bf16[512,1024]{1,0:T(8,128)(2,1)}, bf16[512,1024]{1,0:T(8,128)(2,1)}, u32[]{:S(2)}, u32[]{:S(2)}) collective-permute-start(bf16[512,1024]{1,0:T(8,128)(2,1)} %collective-permute-done.1.refs_1_), channel_id=1, source_target_pairs={{0,2},{1,7},{2,4},{3,1},{4,6},{5,3},{6,0},{7,5},{8,10},{9,15},{10,... | collective-permute-start | bytes 3145736 | tf_op jit(solution)/shard_map/ppermute | solution.py:208
  31.8 19.5 %copy-start.1 = (bf16[1,512,1024]{2,1,0:T(8,128)(2,1)S(1)}, bf16[1,512,1024]{2,1,0:T(8,128)(2,1)}, u32[]{:S(2)}) copy-start(bf16[1,512,1024]{2,1,0:T(8,128)(2,1)} %param.13) | copy-start | bytes 3145732
  31.8 43.5 %copy-start.3 = (f32[64,96]{1,0:T(8,128)S(1)}, f32[64,96]{1,0:T(8,128)}, u32[]{:S(2)}) copy-start(f32[64,96]{1,0:T(8,128)} %low_ref.1) | copy-start | bytes 73732
  31.8 43.5 %copy-start.4 = (f32[64,96]{1,0:T(8,128)S(1)}, f32[64,96]{1,0:T(8,128)}, u32[]{:S(2)}) copy-start(f32[64,96]{1,0:T(8,128)} %high_ref.1) | copy-start | bytes 73732
  31.8 43.5 %copy-start.6 = (s32[1,4,2]{1,2,0:T(2,128)S(1)}, s32[1,4,2]{1,2,0:T(2,128)}, u32[]{:S(2)}) copy-start(s32[1,4,2]{1,2,0:T(2,128)} %param.8) | copy-start | bytes 100
  41.2 26.1 %all-to-all-start.1 = ((bf16[256,8,128]{2,1,0:T(8,128)(2,1)}), bf16[256,8,128]{2,1,0:T(8,128)(2,1)S(1)}, u32[]{:S(2)}, u32[]{:S(2)}) async-start(bf16[256,8,128]{2,1,0:T(8,128)(2,1)} %shard_map.74), calls=%async_computation.1 | async-start | bytes 1048576 | tf_op jit(solution)/shard_map/all_to_all | solution.py:221
  51.3 22.7 %collective-permute-start.4 = (bf16[512,1024]{1,0:T(8,128)(2,1)S(1)}, bf16[512,1024]{1,0:T(8,128)(2,1)}, u32[]{:S(2)}, u32[]{:S(2)}) collective-permute-start(bf16[512,1024]{1,0:T(8,128)(2,1)S(1)} %bitcast.15), channel_id=1, source_target_pairs={{0,1},{1,0},{2,3},{3,2},{4,5},{5,4},{6,7},{7,6},{8,9},{9,8},{10,11... | collective-permute-start | bytes 3145736 | tf_op jit(solution)/shard_map/ppermute | solution.py:224
  55.5 19.8 %collective-permute-start.5 = (bf16[512,1024]{1,0:T(8,128)(2,1)}, bf16[512,1024]{1,0:T(8,128)(2,1)}, u32[]{:S(2)}, u32[]{:S(2)}) collective-permute-start(bf16[512,1024]{1,0:T(8,128)(2,1)} %collective-permute-done.1.refs_1_), channel_id=1, source_target_pairs={{0,1},{1,0},{2,3},{3,2},{4,5},{5,4},{6,7},{7,6},{8,9},{9,8},{10,11... | collective-permute-start | bytes 3145736 | tf_op jit(solution)/shard_map/ppermute | solution.py:224
  57.4 17.9 %collective-permute-start.6 = (bf16[512,1024]{1,0:T(8,128)(2,1)}, bf16[512,1024]{1,0:T(8,128)(2,1)}, u32[]{:S(2)}, u32[]{:S(2)}) collective-permute-start(bf16[512,1024]{1,0:T(8,128)(2,1)} %collective-permute-done.2.refs_2_), channel_id=1, source_target_pairs={{0,1},{1,0},{2,3},{3,2},{4,5},{5,4},{6,7},{7,6},{8,9},{9,8},{10,11... | collective-permute-start | bytes 3145736 | tf_op jit(solution)/shard_map/ppermute | solution.py:224
  59.8 15.5 %collective-permute-start.7 = (bf16[512,1024]{1,0:T(8,128)(2,1)}, bf16[512,1024]{1,0:T(8,128)(2,1)}, u32[]{:S(2)}, u32[]{:S(2)}) collective-permute-start(bf16[512,1024]{1,0:T(8,128)(2,1)} %collective-permute-done.3.refs_3_), channel_id=1, source_target_pairs={{0,1},{1,0},{2,3},{3,2},{4,5},{5,4},{6,7},{7,6},{8,9},{9,8},{10,11... | collective-permute-start | bytes 3145736 | tf_op jit(solution)/shard_map/ppermute | solution.py:224
  67.3 8.0 %collective-permute-start = (bf16[256,8,128]{2,1,0:T(8,128)(2,1)S(1)}, bf16[256,8,128]{2,1,0:T(8,128)(2,1)S(1)}, u32[]{:S(2)}, u32[]{:S(2)}) collective-permute-start(bf16[256,8,128]{2,1,0:T(8,128)(2,1)S(1)} %all-to-all-done.1.own_ref), channel_id=1, source_target_pairs={{0,1},{1,0},{2,3},{3,2},{4,5},{5,4},{6,7},{7,6},{8,9},{9,8},{10,11... | collective-permute-start | bytes 1572872 | tf_op jit(solution)/shard_map/ppermute | solution.py:225
  98.9 7.3 %collective-permute-start.8 = (bf16[4,10,72,128]{3,2,1,0:T(8,128)(2,1)S(1)}, bf16[4,10,72,128]{3,2,1,0:T(8,128)(2,1)S(1)}, u32[]{:S(2)}, u32[]{:S(2)}) collective-permute-start(bf16[4,10,72,128]{3,2,1,0:T(8,128)(2,1)S(1)} %all_gather.3), channel_id=1, source_target_pairs={{0,1},{1,0},{2,3},{3,2},{4,5},{5,4},{6,7},{7,6},{8,9},{9,8},{10,11... | collective-permute-start | bytes 2211848 | tf_op jit(solution)/shard_map/ppermute | solution.py:248

commit v5 on v4

--- a/solution.py
+++ b/solution.py
@@ -9,7 +9,14 @@
 HALF = 2.5
 LANES = 128
 ROWS = 8
+QUAD = 4
+PARTS = 3
 VMEM_LIMIT = 28 * 1024 * 1024
+
+
+def piece_of(slot, part):
+    tile = slot // QUAD * PARTS + part
+    return tile, slot % QUAD
 
 
 def pack_kernel(pairs_ref, stored_ref, orbitals_ref, out_ref):
@@ -17,8 +24,8 @@
     count = pairs_ref.shape[1]
     stored = stored_ref[...]
     place = lax.broadcasted_iota(jnp.int32, stored.shape, 1).astype(jnp.float32)
-    lane = lax.broadcasted_iota(jnp.int32, (ROWS, LANES), 1)
-    wanted = jnp.zeros((ROWS, LANES), jnp.float32)
+    lane = lax.broadcasted_iota(jnp.int32, (2, LANES), 1)
+    wanted = jnp.zeros((2, LANES), jnp.float32)
     for half in range(2):
         for pair in range(count):
             hit = stored == pairs_ref[half, pair]
@@ -26,23 +33,25 @@
             wanted = jnp.where(lane == half * count + pair, row, wanted)
     bands = orbitals_ref.shape[1]
     wide = orbitals_ref.shape[2] // LANES
-    tiles = bands // ROWS * wide
+    own = orbitals_ref[0].astype(jnp.float32)
     for target in range(targets):
-        if target < tiles:
-            group, side = target // wide, target % wide
-            tile = orbitals_ref[0, group * ROWS : (group + 1) * ROWS, side * LANES : (side + 1) * LANES]
-            tile = tile.astype(jnp.float32)
-        else:
-            tile = jnp.zeros((ROWS, LANES), jnp.float32)
-        out_ref[target] = jnp.concatenate([tile, wanted], axis=0).astype(jnp.bfloat16)
+        half, slot = divmod(target, targets // 2)
+        parts = []
+        for part in range(PARTS):
+            tile, quarter = piece_of(slot, part)
+            row = half * (bands // 2) + tile // wide * ROWS + 2 * quarter
+            side = tile % wide
+            parts.append(own[row : row + 2, side * LANES : (side + 1) * LANES])
+        out_ref[target] = jnp.concatenate(parts + [wanted], axis=1).astype(jnp.bfloat16)
 
 
 def select_kernel(rows_ref, table_ref, out_ref):
     transfers, count = rows_ref.shape
+    width = out_ref.shape[2]
 
     def one(transfer, carry):
         for pair in range(count):
-            out_ref[transfer * count + pair] = table_ref[rows_ref[transfer, pair], :ROWS, :]
+            out_ref[transfer * count + pair] = table_ref[rows_ref[transfer, pair], :, :width]
         return carry
 
     lax.fori_loop(0, transfers, one, 0, unroll=8)
@@ -71,28 +80,40 @@
     for copy in copies:
         copy.start()
 
-    even = column == 0
     wide = 2
     row_count = points // (2 * wide * LANES)
-
-    def fetch(tile, block):
-        row, core = block // 2, block % 2
-        mine = own_ref[tile * row_count + row].astype(jnp.float32)
-        theirs = other_ref[tile * row_count + row].astype(jnp.float32)
-        return jnp.where(even, mine, theirs) if core == 0 else jnp.where(even, theirs, mine)
-
-    for block in range(2 * row_count):
-        for side in range(wide):
-            lanes = slice((block * wide + side) * LANES, (block * wide + side + 1) * LANES)
-            for pack in range(count_v // (2 * ROWS)):
-                tile = [fetch((2 * pack + k) * wide + side, block) for k in range(2)]
-                valence[2 * pack * ROWS : 2 * (pack + 1) * ROWS, lanes] = jnp.concatenate(tile, axis=0)
-            base = count_v // ROWS
-            for pack in range(count_c // (2 * ROWS)):
-                tile = [fetch((base + 2 * pack + k) * wide + side, block) for k in range(2)]
-                conduction[2 * pack * ROWS : 2 * (pack + 1) * ROWS, lanes] = jnp.concatenate(
-                    tile, axis=0
-                ).astype(jnp.bfloat16)
+    tiles = count_v // ROWS * wide
+    slots = tiles // PARTS * QUAD
+
+    def assemble(cores):
+        def fetch(tile, block):
+            half, tile = divmod(tile, tiles)
+            part = tile % PARTS
+            first = half * slots + tile // PARTS * QUAD
+            lanes = slice(part * LANES, (part + 1) * LANES)
+            rows = [cores[block % 2][(first + k) * row_count + block // 2, :, lanes] for k in range(QUAD)]
+            return jnp.concatenate([row.astype(jnp.float32) for row in rows], axis=0)
+
+        for block in range(2 * row_count):
+            for side in range(wide):
+                lanes = slice((block * wide + side) * LANES, (block * wide + side + 1) * LANES)
+                for pack in range(count_v // (2 * ROWS)):
+                    pair_of = [fetch((2 * pack + k) * wide + side, block) for k in range(2)]
+                    valence[2 * pack * ROWS : 2 * (pack + 1) * ROWS, lanes] = jnp.concatenate(pair_of, axis=0)
+                base = count_v // ROWS
+                for pack in range(count_c // (2 * ROWS)):
+                    pair_of = [fetch((base + 2 * pack + k) * wide + side, block) for k in range(2)]
+                    conduction[2 * pack * ROWS : 2 * (pack + 1) * ROWS, lanes] = jnp.concatenate(
+                        pair_of, axis=0
+                    ).astype(jnp.bfloat16)
+
+    @pl.when(column == 0)
+    def _():
+        assemble((own_ref, other_ref))
+
+    @pl.when(column == 1)
+    def _():
+        assemble((other_ref, own_ref))
 
     screened_in[...] = jnp.zeros_like(screened_in)
 
@@ -180,6 +201,7 @@
     vmem = pl.BlockSpec(memory_space=pltpu.VMEM)
     anywhere = pl.BlockSpec(memory_space=pl.ANY)
     limit = pltpu.CompilerParams(vmem_limit_bytes=VMEM_LIMIT)
+    width = PARTS * LANES
     swap = [(0, 1), (1, 0)]
     ring = [(r, c) for r in range(rows_axis) for c in range(cols)]
     there = [(r * cols + c, (r + 1 - 2 * c) % rows_axis * cols + c) for r, c in ring]
@@ -188,10 +210,10 @@
     wishes = pairs[0].T
     message = pl.pallas_call(
         pack_kernel,
-        out_shape=jax.ShapeDtypeStruct((transfers, 2 * ROWS, LANES), jnp.bfloat16),
+        out_shape=jax.ShapeDtypeStruct((transfers, 2, width + LANES), jnp.bfloat16),
         in_specs=[smem, vmem, vmem],
         out_specs=vmem,
-        compiler_params=limit,
+        compiler_params=pltpu.CompilerParams(vmem_limit_bytes=2 * VMEM_LIMIT),
     )(wishes, stored_k.reshape(1, transfers), orbitals)
     table = lax.all_to_all(message, "pb", 0, 0, tiled=True)
 
@@ -205,15 +227,15 @@
     w_there = lax.ppermute(w_own, ("row", "col"), there)
     w_back = lax.ppermute(w_own, ("row", "col"), back)
 
-    w_far = lax.ppermute(w_there, ("row", "col"), there)
     table, start = lax.optimization_barrier((table, start))
-
-    wanted = table[:, ROWS, : 2 * pair_count].astype(jnp.int32)
-    valence_tiles = count_v // ROWS * (orbitals.shape[2] // LANES)
-    rows = jnp.where(member < valence_tiles, wanted[:, :pair_count], wanted[:, pair_count:])
+    w_next, _ = lax.optimization_barrier((w_there, table))
+    w_far = lax.ppermute(w_next, ("row", "col"), there)
+
+    wanted = table[:, 0, width : width + 2 * pair_count].astype(jnp.int32)
+    rows = jnp.where(member < transfers // 2, wanted[:, :pair_count], wanted[:, pair_count:])
     chosen = pl.pallas_call(
         select_kernel,
-        out_shape=jax.ShapeDtypeStruct((transfers * pair_count, ROWS, LANES), jnp.bfloat16),
+        out_shape=jax.ShapeDtypeStruct((transfers * pair_count, 2, width), jnp.bfloat16),
         in_specs=[smem, vmem],
         out_specs=vmem,
         compiler_params=limit,

time: 108 us -> 103 us (0.954)
  starting transfers between devices: 60.7 us -> 58.3 us
  local copies, waits for them, and re-layouts: 5.18 us -> 2.83 us
    all_to_all x1, waiting for transfers between devices: 5.68 us -> 8.52 us  [on_device(): table = lax.all_to_all(message, 'pb', 0, 0, tiled=True)]
    all_to_all x1, waiting for transfers between devices: 5.5 us -> 2.85 us  [on_device(): own = lax.all_to_all(chosen, ('pb', 'row'), 0, 0, tiled=True)]
    ppermute x1, starting transfers between devices: 4.57 us -> 2.1 us  [on_device(): w_far = lax.ppermute(w_next, ('row', 'col'), there)]
    unnamed x16 -> x10, local copies, waits for them, and re-layouts: 2.37 us -> 0.02 us
where the time goes in v5:
time: 103 us
  starting transfers between devices  58.3 us (57%)
  Pallas kernels  15.6 us (15%)
  waiting for transfers between devices  14.5 us (14%)
  blocking collectives  10.8 us (10%)
  local copies, waits for them, and re-layouts  2.83 us (3%)
    all_to_all x1, starting transfers between devices, on_device(): table = lax.all_to_all(message, 'pb', 0, 0, tiled=True)  16.3 us
    pallas_call x1, Pallas kernels, on_device(): pl.pallas_call(steps_kernel, out_shape=jax.ShapeDtypeStruct((flat_rows *...  11.7 us
    all_gather x1, blocking collectives, on_device(): across = lax.all_gather(mine, 'row')  10.8 us
    ppermute x4, starting transfers between devices, on_device(): w_tiles = w_core + [lax.ppermute(tile, 'col', swap) for tile in w_core]  10.4 us
    all_to_all x1, starting transfers between devices, on_device(): own = lax.all_to_all(chosen, ('pb', 'row'), 0, 0, tiled=True)  9.71 us
    all_to_all x1, waiting for transfers between devices, on_device(): table = lax.all_to_all(message, 'pb', 0, 0, tiled=True)  8.52 us
    ppermute x1, starting transfers between devices, on_device(): other = lax.ppermute(own, 'col', swap)  7 us
    ppermute x1, starting transfers between devices, on_device(): theirs = lax.ppermute(across, 'col', swap)  5.48 us
  transfers between devices with their start and end apart: 11, of which 4 were waited for; matrix products, arithmetic and copies ran while one was open for 1% of the time, Pallas kernels for 2%

profile of v5, /device:TPU:1, one launch (start us, length us, event | category | flops | bytes accessed | tf_op | source)
XLA Modules:
  0.0 102.6 jit_solution(8669281411926195050)
XLA Ops:
  0.0 0.0 copy-start
  0.0 1.8 %shard_map.73 = bf16[64,2,512]{2,1,0:T(2,128)(2,1)} custom-call(s32[2,4]{1,0:T(2,128)} %bitcast.18, s32[1,64]{1,0:T(1,128)} %bitcast.23, bf16[1,192,256]{2,1,0:T(8,128)(2,1)} %orbitals_ref.1), custom_call_target="tpu_custom_call" | custom-call | tf_op jit(solution)/shard_map/pallas_call | solution.py:211
  1.8 0.0 copy-start.1
  1.8 0.0 copy-start.2
  1.8 0.0 copy-start.3
  1.8 0.0 copy-start.4
  1.8 5.4 %collective-permute-start.1 = (bf16[512,1024]{1,0:T(8,128)(2,1)}, bf16[512,1024]{1,0:T(8,128)(2,1)}, u32[]{:S(2)}, u32[]{:S(2)}) collective-permute-start(bf16[512,1024]{1,0:T(8,128)(2,1)} %bitcast.13), channel_id=1, source_target_pairs={{0,2},{1,7},{2,4},{3,1},{4,6},{5,3},{6,0},{7,5},{8,10},{9,15},{10,... | collective-permute-start | bytes 3145736 | tf_op jit(solution)/shard_map/ppermute | solution.py:227
  7.2 16.3 %all-to-all-start = ((bf16[64,2,512]{2,1,0:T(2,128)(2,1)}), bf16[64,2,512]{2,1,0:T(2,128)(2,1)S(1)}, u32[]{:S(2)}, u32[]{:S(2)}) async-start(bf16[64,2,512]{2,1,0:T(2,128)(2,1)} %shard_map.73), calls=%async_computation | async-start | bytes 262144 | tf_op jit(solution)/shard_map/all_to_all | solution.py:218
  23.5 1.9 %collective-permute-start.2 = (bf16[512,1024]{1,0:T(8,128)(2,1)}, bf16[512,1024]{1,0:T(8,128)(2,1)}, u32[]{:S(2)}, u32[]{:S(2)}) collective-permute-start(bf16[512,1024]{1,0:T(8,128)(2,1)} %bitcast.14), channel_id=1, source_target_pairs={{2,0},{7,1},{4,2},{1,3},{6,4},{3,5},{0,6},{5,7},{10,8},{15,9},{12,... | collective-permute-start | bytes 3145736 | tf_op jit(solution)/shard_map/ppermute | solution.py:228
  25.4 0.0 copy-done
  25.4 1.1 %dynamic-slice_reduce_fusion = bf16[10,9216]{1,0:T(8,128)(2,1)S(1)} fusion(bf16[1,20,4,9216]{3,2,1,0:T(4,128)(2,1)S(1)} %copy-done, s32[]{:T(128)S(6)} %mul.3, s32[]{:T(128)S(6)} %axis_index.38), kind=kLoop, calls=%fused_computation.2 | loop fusion | bytes 368648 | tf_op jit(solution)/shard_map/dynamic_slice | solution.py:220
  26.6 0.2 reshape.14.start_ref
  26.8 8.5 %all-to-all-done.table_ref = bf16[64,2,512]{2,1,0:T(2,128)(2,1)S(1)} async-done(((bf16[64,2,512]{2,1,0:T(2,128)(2,1)}), bf16[64,2,512]{2,1,0:T(2,128)(2,1)S(1)}, u32[]{:S(2)}, u32[]{:S(2)}) %all-to-all-start) | async-done | bytes 131104 | tf_op jit(solution)/shard_map/all_to_all | solution.py:218
  35.4 0.0 collective-permute-done.1.refs_1_
  35.4 2.1 %collective-permute-start.3 = (bf16[512,1024]{1,0:T(8,128)(2,1)}, bf16[512,1024]{1,0:T(8,128)(2,1)}, u32[]{:S(2)}, u32[]{:S(2)}) collective-permute-start(bf16[512,1024]{1,0:T(8,128)(2,1)} %collective-permute-done.1.refs_1_), channel_id=1, source_target_pairs={{0,2},{1,7},{2,4},{3,1},{4,6},{5,3},{6,0},{7,5},{8,10},{9,15},{10,... | collective-permute-start | bytes 3145736 | tf_op jit(solution)/shard_map/ppermute | solution.py:232
  37.5 0.1 slice_select_fusion.rows_ref
  37.6 2.1 %shard_map.74 = bf16[256,2,384]{2,1,0:T(2,128)(2,1)} custom-call(s32[64,4]{1,0:T(8,128)S(1)} %slice_select_fusion.rows_ref, bf16[64,2,512]{2,1,0:T(2,128)(2,1)S(1)} %all-to-all-done.table_ref), custom_call_target="tpu_custom_call" | custom-call | tf_op jit(solution)/shard_map/pallas_call | solution.py:236
  39.7 9.7 %all-to-all-start.1 = ((bf16[256,2,384]{2,1,0:T(2,128)(2,1)}), bf16[256,2,384]{2,1,0:T(2,128)(2,1)S(1)}, u32[]{:S(2)}, u32[]{:S(2)}) async-start(bf16[256,2,384]{2,1,0:T(2,128)(2,1)} %shard_map.74), calls=%async_computation.1 | async-start | bytes 786432 | tf_op jit(solution)/shard_map/all_to_all | solution.py:243
  49.4 0.0 copy-done.1
  49.4 4.2 %collective-permute-start.4 = (bf16[512,1024]{1,0:T(8,128)(2,1)S(1)}, bf16[512,1024]{1,0:T(8,128)(2,1)}, u32[]{:S(2)}, u32[]{:S(2)}) collective-permute-start(bf16[512,1024]{1,0:T(8,128)(2,1)S(1)} %bitcast.15), channel_id=1, source_target_pairs={{0,1},{1,0},{2,3},{3,2},{4,5},{5,4},{6,7},{7,6},{8,9},{9,8},{10,11... | collective-permute-start | bytes 3145736 | tf_op jit(solution)/shard_map/ppermute | solution.py:246
  53.6 1.9 %collective-permute-start.5 = (bf16[512,1024]{1,0:T(8,128)(2,1)}, bf16[512,1024]{1,0:T(8,128)(2,1)}, u32[]{:S(2)}, u32[]{:S(2)}) collective-permute-start(bf16[512,1024]{1,0:T(8,128)(2,1)} %collective-permute-done.1.refs_1_), channel_id=1, source_target_pairs={{0,1},{1,0},{2,3},{3,2},{4,5},{5,4},{6,7},{7,6},{8,9},{9,8},{10,11... | collective-permute-start | bytes 3145736 | tf_op jit(solution)/shard_map/ppermute | solution.py:246
  55.6 0.0 collective-permute-done.2.refs_2_
  55.6 2.4 %collective-permute-start.6 = (bf16[512,1024]{1,0:T(8,128)(2,1)}, bf16[512,1024]{1,0:T(8,128)(2,1)}, u32[]{:S(2)}, u32[]{:S(2)}) collective-permute-start(bf16[512,1024]{1,0:T(8,128)(2,1)} %collective-permute-done.2.refs_2_), channel_id=1, source_target_pairs={{0,1},{1,0},{2,3},{3,2},{4,5},{5,4},{6,7},{7,6},{8,9},{9,8},{10,11... | collective-permute-start | bytes 3145736 | tf_op jit(solution)/shard_map/ppermute | solution.py:246
  58.0 0.0 collective-permute-done.3.refs_3_
  58.0 1.9 %collective-permute-start.7 = (bf16[512,1024]{1,0:T(8,128)(2,1)}, bf16[512,1024]{1,0:T(8,128)(2,1)}, u32[]{:S(2)}, u32[]{:S(2)}) collective-permute-start(bf16[512,1024]{1,0:T(8,128)(2,1)} %collective-permute-done.3.refs_3_), channel_id=1, source_target_pairs={{0,1},{1,0},{2,3},{3,2},{4,5},{5,4},{6,7},{7,6},{8,9},{9,8},{10,11... | collective-permute-start | bytes 3145736 | tf_op jit(solution)/shard_map/ppermute | solution.py:246
  59.9 2.9 %all-to-all-done.1.own_ref = bf16[256,2,384]{2,1,0:T(2,128)(2,1)S(1)} async-done(((bf16[256,2,384]{2,1,0:T(2,128)(2,1)}), bf16[256,2,384]{2,1,0:T(2,128)(2,1)S(1)}, u32[]{:S(2)}, u32[]{:S(2)}) %all-to-all-start.1) | async-done | bytes 393248 | tf_op jit(solution)/shard_map/all_to_all | solution.py:243
  62.8 7.0 %collective-permute-start = (bf16[256,2,384]{2,1,0:T(2,128)(2,1)S(1)}, bf16[256,2,384]{2,1,0:T(2,128)(2,1)S(1)}, u32[]{:S(2)}, u32[]{:S(2)}) collective-permute-start(bf16[256,2,384]{2,1,0:T(2,128)(2,1)S(1)} %all-to-all-done.1.own_ref), channel_id=1, source_target_pairs={{0,1},{1,0},{2,3},{3,2},{4,5},{5,4},{6,7},{7,6},{8,9},{9,8},{10,11... | collective-permute-start | bytes 1179656 | tf_op jit(solution)/shard_map/ppermute | solution.py:247
  69.8 0.0 collective-permute-done.4.refs_4_
  69.8 1.3 %collective-permute-done.other_ref = bf16[256,2,384]{2,1,0:T(2,128)(2,1)S(1)} collective-permute-done((bf16[256,2,384]{2,1,0:T(2,128)(2,1)S(1)}, bf16[256,2,384]{2,1,0:T(2,128)(2,1)S(1)}, u32[]{:S(2)}, u32[]{:S(2)}) %collective-permute-start) | collective-permute-done | bytes 393248 | tf_op jit(solution)/shard_map/ppermute | solution.py:247
  71.1 0.0 collective-permute-done.6.refs_6_
  71.1 0.0 collective-permute-done.5.refs_5_
  71.1 0.0 collective-permute-done.7.refs_7_
  71.1 0.0 copy-done.2
  71.1 0.0 copy-done.3
  71.1 0.0 copy-done.4
  71.1 11.7 %shard_map.75 = bf16[720,128]{1,0:T(8,128)(2,1)S(1)} custom-call(s32[2,4]{1,0:T(2,128)S(1)} %bitcast.19, f32[64,96]{1,0:T(8,128)S(1)} %copy-done.2, f32[64,96]{1,0:T(8,128)S(1)} %copy-done.3, bf16[256,2,384]{2,1,0:T(2,128)(2,1)S(1)} %all-to-all-done.1.own_ref, bf16[256,2,384]{2,1,0:T(2,128)(2,1)S(1)} %collective-permute-done.other_ref, ...), custom_call_target="tpu_custom_call" | custom-call | tf_op jit(solution)/shard_map/pallas_call | solution.py:249
  82.8 10.8 %all_gather.3 = bf16[4,10,72,128]{3,2,1,0:T(8,128)(2,1)S(1)} all-gather(bf16[1,10,72,128]{3,2,1,0:T(8,128)(2,1)S(1)} %bitcast.17), channel_id=1, replica_groups=mesh['pb'=64,'row'=4,'col'=2] {'row'}, dimensions={0}, use_global_device_ids=true | all-gather | bytes 921600 | tf_op jit(solution)/shard_map/all_gather | solution.py:269
  93.6 5.5 %collective-permute-start.8 = (bf16[4,10,72,128]{3,2,1,0:T(8,128)(2,1)S(1)}, bf16[4,10,72,128]{3,2,1,0:T(8,128)(2,1)S(1)}, u32[]{:S(2)}, u32[]{:S(2)}) collective-permute-start(bf16[4,10,72,128]{3,2,1,0:T(8,128)(2,1)S(1)} %all_gather.3), channel_id=1, source_target_pairs={{0,1},{1,0},{2,3},{3,2},{4,5},{5,4},{6,7},{7,6},{8,9},{9,8},{10,11... | collective-permute-start | bytes 2211848 | tf_op jit(solution)/shard_map/ppermute | solution.py:270
  99.1 1.8 %collective-permute-done.8 = bf16[4,10,72,128]{3,2,1,0:T(8,128)(2,1)S(1)} collective-permute-done((bf16[4,10,72,128]{3,2,1,0:T(8,128)(2,1)S(1)}, bf16[4,10,72,128]{3,2,1,0:T(8,128)(2,1)S(1)}, u32[]{:S(2)}, u32[]{:S(2)}) %collective-permute-start.8) | collective-permute-done | bytes 737312 | tf_op jit(solution)/shard_map/ppermute | solution.py:270
  100.9 0.2 fusion
  101.2 0.1 copy.10
  101.3 1.3 %reshape.15 = bf16[1,20,4,9216]{3,2,1,0:T(4,128)(2,1)} reshape(bf16[2,10,4,72,128]{4,3,2,1,0:T(8,128)(2,1)S(1)} %copy.10) | data formatting | bytes 2949120 | tf_op jit(solution)/shard_map/reshape | solution.py:272
  (1 shorter events, 0.0 us)
Async XLA Ops:
  0.0 25.4 %copy-start = (bf16[1,20,4,9216]{3,2,1,0:T(4,128)(2,1)S(1)}, bf16[1,20,4,9216]{3,2,1,0:T(4,128)(2,1)}, u32[]{:S(2)}) copy-start(bf16[1,20,4,9216]{3,2,1,0:T(4,128)(2,1)} %param.7) | copy-start | bytes 4423684
  1.8 47.6 %copy-start.1 = (bf16[1,512,1024]{2,1,0:T(8,128)(2,1)S(1)}, bf16[1,512,1024]{2,1,0:T(8,128)(2,1)}, u32[]{:S(2)}) copy-start(bf16[1,512,1024]{2,1,0:T(8,128)(2,1)} %param.13) | copy-start | bytes 3145732
  1.8 69.3 %copy-start.2 = (f32[64,96]{1,0:T(8,128)S(1)}, f32[64,96]{1,0:T(8,128)}, u32[]{:S(2)}) copy-start(f32[64,96]{1,0:T(8,128)} %low_ref.1) | copy-start | bytes 73732
  1.8 69.3 %copy-start.3 = (f32[64,96]{1,0:T(8,128)S(1)}, f32[64,96]{1,0:T(8,128)}, u32[]{:S(2)}) copy-start(f32[64,96]{1,0:T(8,128)} %high_ref.1) | copy-start | bytes 73732
  1.8 69.3 %copy-start.4 = (s32[1,4,2]{1,2,0:T(2,128)S(1)}, s32[1,4,2]{1,2,0:T(2,128)}, u32[]{:S(2)}) copy-start(s32[1,4,2]{1,2,0:T(2,128)} %param.8) | copy-start | bytes 100
  1.8 33.5 %collective-permute-start.1 = (bf16[512,1024]{1,0:T(8,128)(2,1)}, bf16[512,1024]{1,0:T(8,128)(2,1)}, u32[]{:S(2)}, u32[]{:S(2)}) collective-permute-start(bf16[512,1024]{1,0:T(8,128)(2,1)} %bitcast.13), channel_id=1, source_target_pairs={{0,2},{1,7},{2,4},{3,1},{4,6},{5,3},{6,0},{7,5},{8,10},{9,15},{10,... | collective-permute-start | bytes 3145736 | tf_op jit(solution)/shard_map/ppermute | solution.py:227
  7.2 28.2 %all-to-all-start = ((bf16[64,2,512]{2,1,0:T(2,128)(2,1)}), bf16[64,2,512]{2,1,0:T(2,128)(2,1)S(1)}, u32[]{:S(2)}, u32[]{:S(2)}) async-start(bf16[64,2,512]{2,1,0:T(2,128)(2,1)} %shard_map.73), calls=%async_computation | async-start | bytes 262144 | tf_op jit(solution)/shard_map/all_to_all | solution.py:218
  23.5 32.1 %collective-permute-start.2 = (bf16[512,1024]{1,0:T(8,128)(2,1)}, bf16[512,1024]{1,0:T(8,128)(2,1)}, u32[]{:S(2)}, u32[]{:S(2)}) collective-permute-start(bf16[512,1024]{1,0:T(8,128)(2,1)} %bitcast.14), channel_id=1, source_target_pairs={{2,0},{7,1},{4,2},{1,3},{6,4},{3,5},{0,6},{5,7},{10,8},{15,9},{12,... | collective-permute-start | bytes 3145736 | tf_op jit(solution)/shard_map/ppermute | solution.py:228
  35.4 22.6 %collective-permute-start.3 = (bf16[512,1024]{1,0:T(8,128)(2,1)}, bf16[512,1024]{1,0:T(8,128)(2,1)}, u32[]{:S(2)}, u32[]{:S(2)}) collective-permute-start(bf16[512,1024]{1,0:T(8,128)(2,1)} %collective-permute-done.1.refs_1_), channel_id=1, source_target_pairs={{0,2},{1,7},{2,4},{3,1},{4,6},{5,3},{6,0},{7,5},{8,10},{9,15},{10,... | collective-permute-start | bytes 3145736 | tf_op jit(solution)/shard_map/ppermute | solution.py:232
  39.7 23.1 %all-to-all-start.1 = ((bf16[256,2,384]{2,1,0:T(2,128)(2,1)}), bf16[256,2,384]{2,1,0:T(2,128)(2,1)S(1)}, u32[]{:S(2)}, u32[]{:S(2)}) async-start(bf16[256,2,384]{2,1,0:T(2,128)(2,1)} %shard_map.74), calls=%async_computation.1 | async-start | bytes 786432 | tf_op jit(solution)/shard_map/all_to_all | solution.py:243
  49.4 20.3 %collective-permute-start.4 = (bf16[512,1024]{1,0:T(8,128)(2,1)S(1)}, bf16[512,1024]{1,0:T(8,128)(2,1)}, u32[]{:S(2)}, u32[]{:S(2)}) collective-permute-start(bf16[512,1024]{1,0:T(8,128)(2,1)S(1)} %bitcast.15), channel_id=1, source_target_pairs={{0,1},{1,0},{2,3},{3,2},{4,5},{5,4},{6,7},{7,6},{8,9},{9,8},{10,11... | collective-permute-start | bytes 3145736 | tf_op jit(solution)/shard_map/ppermute | solution.py:246
  53.6 17.5 %collective-permute-start.5 = (bf16[512,1024]{1,0:T(8,128)(2,1)}, bf16[512,1024]{1,0:T(8,128)(2,1)}, u32[]{:S(2)}, u32[]{:S(2)}) collective-permute-start(bf16[512,1024]{1,0:T(8,128)(2,1)} %collective-permute-done.1.refs_1_), channel_id=1, source_target_pairs={{0,1},{1,0},{2,3},{3,2},{4,5},{5,4},{6,7},{7,6},{8,9},{9,8},{10,11... | collective-permute-start | bytes 3145736 | tf_op jit(solution)/shard_map/ppermute | solution.py:246
  55.6 15.5 %collective-permute-start.6 = (bf16[512,1024]{1,0:T(8,128)(2,1)}, bf16[512,1024]{1,0:T(8,128)(2,1)}, u32[]{:S(2)}, u32[]{:S(2)}) collective-permute-start(bf16[512,1024]{1,0:T(8,128)(2,1)} %collective-permute-done.2.refs_2_), channel_id=1, source_target_pairs={{0,1},{1,0},{2,3},{3,2},{4,5},{5,4},{6,7},{7,6},{8,9},{9,8},{10,11... | collective-permute-start | bytes 3145736 | tf_op jit(solution)/shard_map/ppermute | solution.py:246
  58.0 13.1 %collective-permute-start.7 = (bf16[512,1024]{1,0:T(8,128)(2,1)}, bf16[512,1024]{1,0:T(8,128)(2,1)}, u32[]{:S(2)}, u32[]{:S(2)}) collective-permute-start(bf16[512,1024]{1,0:T(8,128)(2,1)} %collective-permute-done.3.refs_3_), channel_id=1, source_target_pairs={{0,1},{1,0},{2,3},{3,2},{4,5},{5,4},{6,7},{7,6},{8,9},{9,8},{10,11... | collective-permute-start | bytes 3145736 | tf_op jit(solution)/shard_map/ppermute | solution.py:246
  62.8 8.3 %collective-permute-start = (bf16[256,2,384]{2,1,0:T(2,128)(2,1)S(1)}, bf16[256,2,384]{2,1,0:T(2,128)(2,1)S(1)}, u32[]{:S(2)}, u32[]{:S(2)}) collective-permute-start(bf16[256,2,384]{2,1,0:T(2,128)(2,1)S(1)} %all-to-all-done.1.own_ref), channel_id=1, source_target_pairs={{0,1},{1,0},{2,3},{3,2},{4,5},{5,4},{6,7},{7,6},{8,9},{9,8},{10,11... | collective-permute-start | bytes 1179656 | tf_op jit(solution)/shard_map/ppermute | solution.py:247
  93.6 7.3 %collective-permute-start.8 = (bf16[4,10,72,128]{3,2,1,0:T(8,128)(2,1)S(1)}, bf16[4,10,72,128]{3,2,1,0:T(8,128)(2,1)S(1)}, u32[]{:S(2)}, u32[]{:S(2)}) collective-permute-start(bf16[4,10,72,128]{3,2,1,0:T(8,128)(2,1)S(1)} %all_gather.3), channel_id=1, source_target_pairs={{0,1},{1,0},{2,3},{3,2},{4,5},{5,4},{6,7},{7,6},{8,9},{9,8},{10,11... | collective-permute-start | bytes 2211848 | tf_op jit(solution)/shard_map/ppermute | solution.py:270

commit v6 on v5

--- a/solution.py
+++ b/solution.py
@@ -46,12 +46,14 @@
 
 
 def select_kernel(rows_ref, table_ref, out_ref):
-    transfers, count = rows_ref.shape
+    transfers = rows_ref.shape[0]
+    count = rows_ref.shape[1] // 2
     width = out_ref.shape[2]
+    first = jnp.where(lax.axis_index("pb") < transfers // 2, 0, count)
 
     def one(transfer, carry):
         for pair in range(count):
-            out_ref[transfer * count + pair] = table_ref[rows_ref[transfer, pair], :, :width]
+            out_ref[transfer * count + pair] = table_ref[rows_ref[transfer, first + pair], :, :width]
         return carry
 
     lax.fori_loop(0, transfers, one, 0, unroll=8)
@@ -188,7 +190,6 @@
     count_v = valence_energy.shape[1]
     count_c = conduction_energy.shape[1]
     vectors, pair_count, flat_size = amplitudes.shape[1:]
-    member = lax.axis_index("pb")
     pair = lax.axis_index("row")
     column = lax.axis_index("col")
     rows_axis, cols = lax.axis_size("row"), lax.axis_size("col")
@@ -227,24 +228,23 @@
     w_there = lax.ppermute(w_own, ("row", "col"), there)
     w_back = lax.ppermute(w_own, ("row", "col"), back)
 
+    w_far = lax.ppermute(w_there, ("row", "col"), there)
     table, start = lax.optimization_barrier((table, start))
-    w_next, _ = lax.optimization_barrier((w_there, table))
-    w_far = lax.ppermute(w_next, ("row", "col"), there)
 
     wanted = table[:, 0, width : width + 2 * pair_count].astype(jnp.int32)
-    rows = jnp.where(member < transfers // 2, wanted[:, :pair_count], wanted[:, pair_count:])
     chosen = pl.pallas_call(
         select_kernel,
         out_shape=jax.ShapeDtypeStruct((transfers * pair_count, 2, width), jnp.bfloat16),
         in_specs=[smem, vmem],
         out_specs=vmem,
         compiler_params=limit,
-    )(rows, table)
+    )(wanted, table)
     own = lax.all_to_all(chosen, ("pb", "row"), 0, 0, tiled=True)
 
-    w_core = [w_own, w_there, w_back, w_far]
+    other = lax.ppermute(own, "col", swap)
+    w_last, _ = lax.optimization_barrier((w_far, own))
+    w_core = [w_own, w_there, w_back, w_last]
     w_tiles = w_core + [lax.ppermute(tile, "col", swap) for tile in w_core]
-    other = lax.ppermute(own, "col", swap)
 
     result = pl.pallas_call(
         steps_kernel,

time: 103 us -> 105 us (1.019)
  starting transfers between devices: 58.3 us -> 62.3 us
  waiting for transfers between devices: 14.5 us -> 12.2 us
    ppermute x1, starting transfers between devices: 7 us -> 1.92 us  [on_device(): other = lax.ppermute(own, 'col', swap)]
    ppermute x4, starting transfers between devices: 10.4 us -> 15.5 us  [on_device(): w_tiles = w_core + [lax.ppermute(tile, 'col', swap) for tile in w_core]]
    all_to_all x1, waiting for transfers between devices: 8.52 us -> 3.93 us  [on_device(): table = lax.all_to_all(message, 'pb', 0, 0, tiled=True)]
    ppermute x1, starting transfers between devices: 2.1 us -> 4.57 us  [on_device(): w_far = lax.ppermute(w_there, ('row', 'col'), there)]
    all_to_all x1, starting transfers between devices: 9.71 us -> 11.8 us  [on_device(): own = lax.all_to_all(chosen, ('pb', 'row'), 0, 0, tiled=True)]
    all_to_all x1, waiting for transfers between devices: 2.85 us -> 4.79 us  [on_device(): own = lax.all_to_all(chosen, ('pb', 'row'), 0, 0, tiled=True)]
where the time goes in v6:
time: 105 us
  starting transfers between devices  62.3 us (59%)
  Pallas kernels  15.5 us (15%)
  waiting for transfers between devices  12.2 us (12%)
  blocking collectives  11.4 us (11%)
  local copies, waits for them, and re-layouts  2.83 us (3%)
    all_to_all x1, starting transfers between devices, on_device(): table = lax.all_to_all(message, 'pb', 0, 0, tiled=True)  16.3 us
    ppermute x4, starting transfers between devices, on_device(): w_tiles = w_core + [lax.ppermute(tile, 'col', swap) for tile in w_core]  15.5 us
    all_to_all x1, starting transfers between devices, on_device(): own = lax.all_to_all(chosen, ('pb', 'row'), 0, 0, tiled=True)  11.8 us
    all_gather x1, blocking collectives, on_device(): across = lax.all_gather(mine, 'row')  11.4 us
    pallas_call x1, Pallas kernels, on_device(): pl.pallas_call(steps_kernel, out_shape=jax.ShapeDtypeStruct((flat_rows *...  11.4 us
    ppermute x1, starting transfers between devices, on_device(): w_there = lax.ppermute(w_own, ('row', 'col'), there)  5.35 us
    ppermute x1, starting transfers between devices, on_device(): theirs = lax.ppermute(across, 'col', swap)  4.92 us
    all_to_all x1, waiting for transfers between devices, on_device(): own = lax.all_to_all(chosen, ('pb', 'row'), 0, 0, tiled=True)  4.79 us
  transfers between devices with their start and end apart: 11, of which 4 were waited for; matrix products, arithmetic and copies ran while one was open for 1% of the time, Pallas kernels for 2%

profile of v6, /device:TPU:1, one launch (start us, length us, event | category | flops | bytes accessed | tf_op | source)
XLA Modules:
  0.0 104.8 jit_solution(9774151868426720985)
XLA Ops:
  0.0 0.0 copy-start
  0.0 1.8 %shard_map.73 = bf16[64,2,512]{2,1,0:T(2,128)(2,1)} custom-call(s32[2,4]{1,0:T(2,128)} %bitcast.19, s32[1,64]{1,0:T(1,128)} %bitcast.23, bf16[1,192,256]{2,1,0:T(8,128)(2,1)} %orbitals_ref.1), custom_call_target="tpu_custom_call" | custom-call | tf_op jit(solution)/shard_map/pallas_call | solution.py:212
  1.8 0.0 copy-start.1
  1.8 0.0 copy-start.2
  1.8 0.0 copy-start.3
  1.8 0.0 copy-start.4
  1.8 5.4 %collective-permute-start.1 = (bf16[512,1024]{1,0:T(8,128)(2,1)}, bf16[512,1024]{1,0:T(8,128)(2,1)}, u32[]{:S(2)}, u32[]{:S(2)}) collective-permute-start(bf16[512,1024]{1,0:T(8,128)(2,1)} %bitcast.13), channel_id=1, source_target_pairs={{0,2},{1,7},{2,4},{3,1},{4,6},{5,3},{6,0},{7,5},{8,10},{9,15},{10,... | collective-permute-start | bytes 3145736 | tf_op jit(solution)/shard_map/ppermute | solution.py:228
  7.2 16.3 %all-to-all-start = ((bf16[64,2,512]{2,1,0:T(2,128)(2,1)}), bf16[64,2,512]{2,1,0:T(2,128)(2,1)S(1)}, u32[]{:S(2)}, u32[]{:S(2)}) async-start(bf16[64,2,512]{2,1,0:T(2,128)(2,1)} %shard_map.73), calls=%async_computation | async-start | bytes 262144 | tf_op jit(solution)/shard_map/all_to_all | solution.py:219
  23.5 1.9 %collective-permute-start.2 = (bf16[512,1024]{1,0:T(8,128)(2,1)}, bf16[512,1024]{1,0:T(8,128)(2,1)}, u32[]{:S(2)}, u32[]{:S(2)}) collective-permute-start(bf16[512,1024]{1,0:T(8,128)(2,1)} %bitcast.14), channel_id=1, source_target_pairs={{2,0},{7,1},{4,2},{1,3},{6,4},{3,5},{0,6},{5,7},{10,8},{15,9},{12,... | collective-permute-start | bytes 3145736 | tf_op jit(solution)/shard_map/ppermute | solution.py:229
  25.4 0.0 collective-permute-done.1.refs_1_
  25.4 4.6 %collective-permute-start.3 = (bf16[512,1024]{1,0:T(8,128)(2,1)}, bf16[512,1024]{1,0:T(8,128)(2,1)}, u32[]{:S(2)}, u32[]{:S(2)}) collective-permute-start(bf16[512,1024]{1,0:T(8,128)(2,1)} %collective-permute-done.1.refs_1_), channel_id=1, source_target_pairs={{0,2},{1,7},{2,4},{3,1},{4,6},{5,3},{6,0},{7,5},{8,10},{9,15},{10,... | collective-permute-start | bytes 3145736 | tf_op jit(solution)/shard_map/ppermute | solution.py:231
  30.0 0.0 copy-done
  30.0 1.1 %dynamic-slice_reduce_fusion = bf16[10,9216]{1,0:T(8,128)(2,1)S(1)} fusion(bf16[1,20,4,9216]{3,2,1,0:T(4,128)(2,1)S(1)} %copy-done, s32[]{:T(128)S(6)} %mul.3, s32[]{:T(128)S(6)} %axis_index.25), kind=kLoop, calls=%fused_computation.2 | loop fusion | bytes 368648 | tf_op jit(solution)/shard_map/dynamic_slice | solution.py:221
  31.2 0.2 reshape.14.start_ref
  31.4 3.9 %all-to-all-done.table_ref = bf16[64,2,512]{2,1,0:T(2,128)(2,1)S(1)} async-done(((bf16[64,2,512]{2,1,0:T(2,128)(2,1)}), bf16[64,2,512]{2,1,0:T(2,128)(2,1)S(1)}, u32[]{:S(2)}, u32[]{:S(2)}) %all-to-all-start) | async-done | bytes 131104 | tf_op jit(solution)/shard_map/all_to_all | solution.py:219
  35.4 2.3 %shard_map.74 = bf16[256,2,384]{2,1,0:T(2,128)(2,1)} custom-call(s32[64,8]{1,0:T(8,128)S(1)} %bitcast.18, bf16[64,2,512]{2,1,0:T(2,128)(2,1)S(1)} %all-to-all-done.table_ref), custom_call_target="tpu_custom_call" | custom-call | tf_op jit(solution)/shard_map/pallas_call | solution.py:235
  37.7 11.8 %all-to-all-start.1 = ((bf16[256,2,384]{2,1,0:T(2,128)(2,1)}), bf16[256,2,384]{2,1,0:T(2,128)(2,1)S(1)}, u32[]{:S(2)}, u32[]{:S(2)}) async-start(bf16[256,2,384]{2,1,0:T(2,128)(2,1)} %shard_map.74), calls=%async_computation.1 | async-start | bytes 786432 | tf_op jit(solution)/shard_map/all_to_all | solution.py:242
  49.5 0.0 copy-done.1
  49.5 4.2 %collective-permute-start.4 = (bf16[512,1024]{1,0:T(8,128)(2,1)S(1)}, bf16[512,1024]{1,0:T(8,128)(2,1)}, u32[]{:S(2)}, u32[]{:S(2)}) collective-permute-start(bf16[512,1024]{1,0:T(8,128)(2,1)S(1)} %bitcast.15), channel_id=1, source_target_pairs={{0,1},{1,0},{2,3},{3,2},{4,5},{5,4},{6,7},{7,6},{8,9},{9,8},{10,11... | collective-permute-start | bytes 3145736 | tf_op jit(solution)/shard_map/ppermute | solution.py:247
  53.7 1.9 %collective-permute-start.5 = (bf16[512,1024]{1,0:T(8,128)(2,1)}, bf16[512,1024]{1,0:T(8,128)(2,1)}, u32[]{:S(2)}, u32[]{:S(2)}) collective-permute-start(bf16[512,1024]{1,0:T(8,128)(2,1)} %collective-permute-done.1.refs_1_), channel_id=1, source_target_pairs={{0,1},{1,0},{2,3},{3,2},{4,5},{5,4},{6,7},{7,6},{8,9},{9,8},{10,11... | collective-permute-start | bytes 3145736 | tf_op jit(solution)/shard_map/ppermute | solution.py:247
  55.6 0.0 collective-permute-done.2.refs_2_
  55.7 2.4 %collective-permute-start.6 = (bf16[512,1024]{1,0:T(8,128)(2,1)}, bf16[512,1024]{1,0:T(8,128)(2,1)}, u32[]{:S(2)}, u32[]{:S(2)}) collective-permute-start(bf16[512,1024]{1,0:T(8,128)(2,1)} %collective-permute-done.2.refs_2_), channel_id=1, source_target_pairs={{0,1},{1,0},{2,3},{3,2},{4,5},{5,4},{6,7},{7,6},{8,9},{9,8},{10,11... | collective-permute-start | bytes 3145736 | tf_op jit(solution)/shard_map/ppermute | solution.py:247
  58.1 4.8 %all-to-all-done.1.own_ref = bf16[256,2,384]{2,1,0:T(2,128)(2,1)S(1)} async-done(((bf16[256,2,384]{2,1,0:T(2,128)(2,1)}), bf16[256,2,384]{2,1,0:T(2,128)(2,1)S(1)}, u32[]{:S(2)}, u32[]{:S(2)}) %all-to-all-start.1) | async-done | bytes 393248 | tf_op jit(solution)/shard_map/all_to_all | solution.py:242
  62.9 0.0 collective-permute-done.3.refs_3_
  62.9 7.0 %collective-permute-start.7 = (bf16[512,1024]{1,0:T(8,128)(2,1)}, bf16[512,1024]{1,0:T(8,128)(2,1)S(1)}, u32[]{:S(2)}, u32[]{:S(2)}) collective-permute-start(bf16[512,1024]{1,0:T(8,128)(2,1)} %collective-permute-done.3.refs_3_), channel_id=1, source_target_pairs={{0,1},{1,0},{2,3},{3,2},{4,5},{5,4},{6,7},{7,6},{8,9},{9,8},{10,11... | collective-permute-start | bytes 3145736 | tf_op jit(solution)/shard_map/ppermute | solution.py:247
  69.9 1.9 %collective-permute-start = (bf16[256,2,384]{2,1,0:T(2,128)(2,1)S(1)}, bf16[256,2,384]{2,1,0:T(2,128)(2,1)S(1)}, u32[]{:S(2)}, u32[]{:S(2)}) collective-permute-start(bf16[256,2,384]{2,1,0:T(2,128)(2,1)S(1)} %all-to-all-done.1.own_ref), channel_id=1, source_target_pairs={{0,1},{1,0},{2,3},{3,2},{4,5},{5,4},{6,7},{7,6},{8,9},{9,8},{10,11... | collective-permute-start | bytes 1179656 | tf_op jit(solution)/shard_map/ppermute | solution.py:244
  71.8 0.0 collective-permute-done.4.refs_4_
  71.8 1.7 %collective-permute-done.other_ref = bf16[256,2,384]{2,1,0:T(2,128)(2,1)S(1)} collective-permute-done((bf16[256,2,384]{2,1,0:T(2,128)(2,1)S(1)}, bf16[256,2,384]{2,1,0:T(2,128)(2,1)S(1)}, u32[]{:S(2)}, u32[]{:S(2)}) %collective-permute-start) | collective-permute-done | bytes 393248 | tf_op jit(solution)/shard_map/ppermute | solution.py:244
  73.5 0.0 collective-permute-done.6.refs_6_
  73.5 0.0 collective-permute-done.5.refs_5_
  73.5 0.0 collective-permute-done.7.refs_7_
  73.5 0.0 copy-done.2
  73.5 0.0 copy-done.3
  73.5 0.0 copy-done.4
  73.5 11.4 %shard_map.75 = bf16[720,128]{1,0:T(8,128)(2,1)S(1)} custom-call(s32[2,4]{1,0:T(2,128)S(1)} %bitcast.20, f32[64,96]{1,0:T(8,128)S(1)} %copy-done.2, f32[64,96]{1,0:T(8,128)S(1)} %copy-done.3, bf16[256,2,384]{2,1,0:T(2,128)(2,1)S(1)} %all-to-all-done.1.own_ref, bf16[256,2,384]{2,1,0:T(2,128)(2,1)S(1)} %collective-permute-done.other_ref, ...), custom_call_target="tpu_custom_call" | custom-call | tf_op jit(solution)/shard_map/pallas_call | solution.py:249
  84.9 11.4 %all_gather.3 = bf16[4,10,72,128]{3,2,1,0:T(8,128)(2,1)S(1)} all-gather(bf16[1,10,72,128]{3,2,1,0:T(8,128)(2,1)S(1)} %bitcast.17), channel_id=1, replica_groups=mesh['pb'=64,'row'=4,'col'=2] {'row'}, dimensions={0}, use_global_device_ids=true | all-gather | bytes 921600 | tf_op jit(solution)/shard_map/all_gather | solution.py:269
  96.3 4.9 %collective-permute-start.8 = (bf16[4,10,72,128]{3,2,1,0:T(8,128)(2,1)S(1)}, bf16[4,10,72,128]{3,2,1,0:T(8,128)(2,1)S(1)}, u32[]{:S(2)}, u32[]{:S(2)}) collective-permute-start(bf16[4,10,72,128]{3,2,1,0:T(8,128)(2,1)S(1)} %all_gather.3), channel_id=1, source_target_pairs={{0,1},{1,0},{2,3},{3,2},{4,5},{5,4},{6,7},{7,6},{8,9},{9,8},{10,11... | collective-permute-start | bytes 2211848 | tf_op jit(solution)/shard_map/ppermute | solution.py:270
  101.3 1.8 %collective-permute-done.8 = bf16[4,10,72,128]{3,2,1,0:T(8,128)(2,1)S(1)} collective-permute-done((bf16[4,10,72,128]{3,2,1,0:T(8,128)(2,1)S(1)}, bf16[4,10,72,128]{3,2,1,0:T(8,128)(2,1)S(1)}, u32[]{:S(2)}, u32[]{:S(2)}) %collective-permute-start.8) | collective-permute-done | bytes 737312 | tf_op jit(solution)/shard_map/ppermute | solution.py:270
  103.1 0.2 fusion
  103.3 0.1 copy.10
  103.5 1.3 %reshape.15 = bf16[1,20,4,9216]{3,2,1,0:T(4,128)(2,1)} reshape(bf16[2,10,4,72,128]{4,3,2,1,0:T(8,128)(2,1)S(1)} %copy.10) | data formatting | bytes 2949120 | tf_op jit(solution)/shard_map/reshape | solution.py:272
  (1 shorter events, 0.0 us)
Async XLA Ops:
  0.0 30.0 %copy-start = (bf16[1,20,4,9216]{3,2,1,0:T(4,128)(2,1)S(1)}, bf16[1,20,4,9216]{3,2,1,0:T(4,128)(2,1)}, u32[]{:S(2)}) copy-start(bf16[1,20,4,9216]{3,2,1,0:T(4,128)(2,1)} %param.7) | copy-start | bytes 4423684
  1.8 47.7 %copy-start.1 = (bf16[1,512,1024]{2,1,0:T(8,128)(2,1)S(1)}, bf16[1,512,1024]{2,1,0:T(8,128)(2,1)}, u32[]{:S(2)}) copy-start(bf16[1,512,1024]{2,1,0:T(8,128)(2,1)} %param.13) | copy-start | bytes 3145732
  1.8 71.7 %copy-start.2 = (f32[64,96]{1,0:T(8,128)S(1)}, f32[64,96]{1,0:T(8,128)}, u32[]{:S(2)}) copy-start(f32[64,96]{1,0:T(8,128)} %low_ref.1) | copy-start | bytes 73732
  1.8 71.7 %copy-start.3 = (f32[64,96]{1,0:T(8,128)S(1)}, f32[64,96]{1,0:T(8,128)}, u32[]{:S(2)}) copy-start(f32[64,96]{1,0:T(8,128)} %high_ref.1) | copy-start | bytes 73732
  1.8 71.7 %copy-start.4 = (s32[1,4,2]{1,2,0:T(2,128)S(1)}, s32[1,4,2]{1,2,0:T(2,128)}, u32[]{:S(2)}) copy-start(s32[1,4,2]{1,2,0:T(2,128)} %param.8) | copy-start | bytes 100
  1.8 23.6 %collective-permute-start.1 = (bf16[512,1024]{1,0:T(8,128)(2,1)}, bf16[512,1024]{1,0:T(8,128)(2,1)}, u32[]{:S(2)}, u32[]{:S(2)}) collective-permute-start(bf16[512,1024]{1,0:T(8,128)(2,1)} %bitcast.13), channel_id=1, source_target_pairs={{0,2},{1,7},{2,4},{3,1},{4,6},{5,3},{6,0},{7,5},{8,10},{9,15},{10,... | collective-permute-start | bytes 3145736 | tf_op jit(solution)/shard_map/ppermute | solution.py:228
  7.2 28.2 %all-to-all-start = ((bf16[64,2,512]{2,1,0:T(2,128)(2,1)}), bf16[64,2,512]{2,1,0:T(2,128)(2,1)S(1)}, u32[]{:S(2)}, u32[]{:S(2)}) async-start(bf16[64,2,512]{2,1,0:T(2,128)(2,1)} %shard_map.73), calls=%async_computation | async-start | bytes 262144 | tf_op jit(solution)/shard_map/all_to_all | solution.py:219
  23.5 32.2 %collective-permute-start.2 = (bf16[512,1024]{1,0:T(8,128)(2,1)}, bf16[512,1024]{1,0:T(8,128)(2,1)}, u32[]{:S(2)}, u32[]{:S(2)}) collective-permute-start(bf16[512,1024]{1,0:T(8,128)(2,1)} %bitcast.14), channel_id=1, source_target_pairs={{2,0},{7,1},{4,2},{1,3},{6,4},{3,5},{0,6},{5,7},{10,8},{15,9},{12,... | collective-permute-start | bytes 3145736 | tf_op jit(solution)/shard_map/ppermute | solution.py:229
  25.4 37.4 %collective-permute-start.3 = (bf16[512,1024]{1,0:T(8,128)(2,1)}, bf16[512,1024]{1,0:T(8,128)(2,1)}, u32[]{:S(2)}, u32[]{:S(2)}) collective-permute-start(bf16[512,1024]{1,0:T(8,128)(2,1)} %collective-permute-done.1.refs_1_), channel_id=1, source_target_pairs={{0,2},{1,7},{2,4},{3,1},{4,6},{5,3},{6,0},{7,5},{8,10},{9,15},{10,... | collective-permute-start | bytes 3145736 | tf_op jit(solution)/shard_map/ppermute | solution.py:231
  37.7 25.2 %all-to-all-start.1 = ((bf16[256,2,384]{2,1,0:T(2,128)(2,1)}), bf16[256,2,384]{2,1,0:T(2,128)(2,1)S(1)}, u32[]{:S(2)}, u32[]{:S(2)}) async-start(bf16[256,2,384]{2,1,0:T(2,128)(2,1)} %shard_map.74), calls=%async_computation.1 | async-start | bytes 786432 | tf_op jit(solution)/shard_map/all_to_all | solution.py:242
  49.5 22.3 %collective-permute-start.4 = (bf16[512,1024]{1,0:T(8,128)(2,1)S(1)}, bf16[512,1024]{1,0:T(8,128)(2,1)}, u32[]{:S(2)}, u32[]{:S(2)}) collective-permute-start(bf16[512,1024]{1,0:T(8,128)(2,1)S(1)} %bitcast.15), channel_id=1, source_target_pairs={{0,1},{1,0},{2,3},{3,2},{4,5},{5,4},{6,7},{7,6},{8,9},{9,8},{10,11... | collective-permute-start | bytes 3145736 | tf_op jit(solution)/shard_map/ppermute | solution.py:247
  53.7 19.8 %collective-permute-start.5 = (bf16[512,1024]{1,0:T(8,128)(2,1)}, bf16[512,1024]{1,0:T(8,128)(2,1)}, u32[]{:S(2)}, u32[]{:S(2)}) collective-permute-start(bf16[512,1024]{1,0:T(8,128)(2,1)} %collective-permute-done.1.refs_1_), channel_id=1, source_target_pairs={{0,1},{1,0},{2,3},{3,2},{4,5},{5,4},{6,7},{7,6},{8,9},{9,8},{10,11... | collective-permute-start | bytes 3145736 | tf_op jit(solution)/shard_map/ppermute | solution.py:247
  55.7 17.8 %collective-permute-start.6 = (bf16[512,1024]{1,0:T(8,128)(2,1)}, bf16[512,1024]{1,0:T(8,128)(2,1)}, u32[]{:S(2)}, u32[]{:S(2)}) collective-permute-start(bf16[512,1024]{1,0:T(8,128)(2,1)} %collective-permute-done.2.refs_2_), channel_id=1, source_target_pairs={{0,1},{1,0},{2,3},{3,2},{4,5},{5,4},{6,7},{7,6},{8,9},{9,8},{10,11... | collective-permute-start | bytes 3145736 | tf_op jit(solution)/shard_map/ppermute | solution.py:247
  62.9 10.6 %collective-permute-start.7 = (bf16[512,1024]{1,0:T(8,128)(2,1)}, bf16[512,1024]{1,0:T(8,128)(2,1)S(1)}, u32[]{:S(2)}, u32[]{:S(2)}) collective-permute-start(bf16[512,1024]{1,0:T(8,128)(2,1)} %collective-permute-done.3.refs_3_), channel_id=1, source_target_pairs={{0,1},{1,0},{2,3},{3,2},{4,5},{5,4},{6,7},{7,6},{8,9},{9,8},{10,11... | collective-permute-start | bytes 3145736 | tf_op jit(solution)/shard_map/ppermute | solution.py:247
  69.9 3.6 %collective-permute-start = (bf16[256,2,384]{2,1,0:T(2,128)(2,1)S(1)}, bf16[256,2,384]{2,1,0:T(2,128)(2,1)S(1)}, u32[]{:S(2)}, u32[]{:S(2)}) collective-permute-start(bf16[256,2,384]{2,1,0:T(2,128)(2,1)S(1)} %all-to-all-done.1.own_ref), channel_id=1, source_target_pairs={{0,1},{1,0},{2,3},{3,2},{4,5},{5,4},{6,7},{7,6},{8,9},{9,8},{10,11... | collective-permute-start | bytes 1179656 | tf_op jit(solution)/shard_map/ppermute | solution.py:244
  96.3 6.7 %collective-permute-start.8 = (bf16[4,10,72,128]{3,2,1,0:T(8,128)(2,1)S(1)}, bf16[4,10,72,128]{3,2,1,0:T(8,128)(2,1)S(1)}, u32[]{:S(2)}, u32[]{:S(2)}) collective-permute-start(bf16[4,10,72,128]{3,2,1,0:T(8,128)(2,1)S(1)} %all_gather.3), channel_id=1, source_target_pairs={{0,1},{1,0},{2,3},{3,2},{4,5},{5,4},{6,7},{7,6},{8,9},{9,8},{10,11... | collective-permute-start | bytes 2211848 | tf_op jit(solution)/shard_map/ppermute | solution.py:270

commit v7 on v6

--- a/solution.py
+++ b/solution.py
@@ -228,8 +228,9 @@
     w_there = lax.ppermute(w_own, ("row", "col"), there)
     w_back = lax.ppermute(w_own, ("row", "col"), back)
 
-    w_far = lax.ppermute(w_there, ("row", "col"), there)
     table, start = lax.optimization_barrier((table, start))
+    w_next, _ = lax.optimization_barrier((w_there, table))
+    w_far = lax.ppermute(w_next, ("row", "col"), there)
 
     wanted = table[:, 0, width : width + 2 * pair_count].astype(jnp.int32)
     chosen = pl.pallas_call(
@@ -241,10 +242,9 @@
     )(wanted, table)
     own = lax.all_to_all(chosen, ("pb", "row"), 0, 0, tiled=True)
 
+    w_core = [w_own, w_there, w_back, w_far]
+    w_tiles = w_core + [lax.ppermute(tile, "col", swap) for tile in w_core]
     other = lax.ppermute(own, "col", swap)
-    w_last, _ = lax.optimization_barrier((w_far, own))
-    w_core = [w_own, w_there, w_back, w_last]
-    w_tiles = w_core + [lax.ppermute(tile, "col", swap) for tile in w_core]
 
     result = pl.pallas_call(
         steps_kernel,

time: 105 us -> 103 us (0.981)
  starting transfers between devices: 62.3 us -> 58.3 us
  waiting for transfers between devices: 12.2 us -> 14.5 us
    ppermute x1, starting transfers between devices: 1.92 us -> 7 us  [on_device(): other = lax.ppermute(own, 'col', swap)]
    ppermute x4, starting transfers between devices: 15.5 us -> 10.4 us  [on_device(): w_tiles = w_core + [lax.ppermute(tile, 'col', swap) for tile in w_core]]
    all_to_all x1, waiting for transfers between devices: 3.93 us -> 8.52 us  [on_device(): table = lax.all_to_all(message, 'pb', 0, 0, tiled=True)]
    ppermute x1, starting transfers between devices: 4.57 us -> 2.1 us  [on_device(): w_far = lax.ppermute(w_next, ('row', 'col'), there)]
    all_to_all x1, starting transfers between devices: 11.8 us -> 9.71 us  [on_device(): own = lax.all_to_all(chosen, ('pb', 'row'), 0, 0, tiled=True)]
    all_to_all x1, waiting for transfers between devices: 4.79 us -> 2.85 us  [on_device(): own = lax.all_to_all(chosen, ('pb', 'row'), 0, 0, tiled=True)]
where the time goes in v7:
time: 103 us
  starting transfers between devices  58.3 us (57%)
  Pallas kernels  15.8 us (15%)
  waiting for transfers between devices  14.5 us (14%)
  blocking collectives  10.8 us (10%)
  local copies, waits for them, and re-layouts  2.83 us (3%)
    all_to_all x1, starting transfers between devices, on_device(): table = lax.all_to_all(message, 'pb', 0, 0, tiled=True)  16.3 us
    pallas_call x1, Pallas kernels, on_device(): pl.pallas_call(steps_kernel, out_shape=jax.ShapeDtypeStruct((flat_rows *...  11.7 us
    all_gather x1, blocking collectives, on_device(): across = lax.all_gather(mine, 'row')  10.8 us
    ppermute x4, starting transfers between devices, on_device(): w_tiles = w_core + [lax.ppermute(tile, 'col', swap) for tile in w_core]  10.4 us
    all_to_all x1, starting transfers between devices, on_device(): own = lax.all_to_all(chosen, ('pb', 'row'), 0, 0, tiled=True)  9.71 us
    all_to_all x1, waiting for transfers between devices, on_device(): table = lax.all_to_all(message, 'pb', 0, 0, tiled=True)  8.52 us
    ppermute x1, starting transfers between devices, on_device(): other = lax.ppermute(own, 'col', swap)  7 us
    ppermute x1, starting transfers between devices, on_device(): theirs = lax.ppermute(across, 'col', swap)  5.5 us
  transfers between devices with their start and end apart: 11, of which 4 were waited for; matrix products, arithmetic and copies ran while one was open for 1% of the time, Pallas kernels for 2%

profile of v7, /device:TPU:1, one launch (start us, length us, event | category | flops | bytes accessed | tf_op | source)
XLA Modules:
  0.0 102.7 jit_solution(14913719244142166757)
XLA Ops:
  0.0 0.0 copy-start
  0.0 1.8 %shard_map.73 = bf16[64,2,512]{2,1,0:T(2,128)(2,1)} custom-call(s32[2,4]{1,0:T(2,128)} %bitcast.19, s32[1,64]{1,0:T(1,128)} %bitcast.23, bf16[1,192,256]{2,1,0:T(8,128)(2,1)} %orbitals_ref.1), custom_call_target="tpu_custom_call" | custom-call | tf_op jit(solution)/shard_map/pallas_call | solution.py:212
  1.8 0.0 copy-start.1
  1.8 0.0 copy-start.2
  1.8 0.0 copy-start.3
  1.8 0.0 copy-start.4
  1.8 5.4 %collective-permute-start.1 = (bf16[512,1024]{1,0:T(8,128)(2,1)}, bf16[512,1024]{1,0:T(8,128)(2,1)}, u32[]{:S(2)}, u32[]{:S(2)}) collective-permute-start(bf16[512,1024]{1,0:T(8,128)(2,1)} %bitcast.13), channel_id=1, source_target_pairs={{0,2},{1,7},{2,4},{3,1},{4,6},{5,3},{6,0},{7,5},{8,10},{9,15},{10,... | collective-permute-start | bytes 3145736 | tf_op jit(solution)/shard_map/ppermute | solution.py:228
  7.2 16.3 %all-to-all-start = ((bf16[64,2,512]{2,1,0:T(2,128)(2,1)}), bf16[64,2,512]{2,1,0:T(2,128)(2,1)S(1)}, u32[]{:S(2)}, u32[]{:S(2)}) async-start(bf16[64,2,512]{2,1,0:T(2,128)(2,1)} %shard_map.73), calls=%async_computation | async-start | bytes 262144 | tf_op jit(solution)/shard_map/all_to_all | solution.py:219
  23.5 1.9 %collective-permute-start.2 = (bf16[512,1024]{1,0:T(8,128)(2,1)}, bf16[512,1024]{1,0:T(8,128)(2,1)}, u32[]{:S(2)}, u32[]{:S(2)}) collective-permute-start(bf16[512,1024]{1,0:T(8,128)(2,1)} %bitcast.14), channel_id=1, source_target_pairs={{2,0},{7,1},{4,2},{1,3},{6,4},{3,5},{0,6},{5,7},{10,8},{15,9},{12,... | collective-permute-start | bytes 3145736 | tf_op jit(solution)/shard_map/ppermute | solution.py:229
  25.4 0.0 copy-done
  25.4 1.1 %dynamic-slice_reduce_fusion = bf16[10,9216]{1,0:T(8,128)(2,1)S(1)} fusion(bf16[1,20,4,9216]{3,2,1,0:T(4,128)(2,1)S(1)} %copy-done, s32[]{:T(128)S(6)} %mul.3, s32[]{:T(128)S(6)} %axis_index.25), kind=kLoop, calls=%fused_computation.2 | loop fusion | bytes 368648 | tf_op jit(solution)/shard_map/dynamic_slice | solution.py:221
  26.6 0.2 reshape.14.start_ref
  26.8 8.5 %all-to-all-done.table_ref = bf16[64,2,512]{2,1,0:T(2,128)(2,1)S(1)} async-done(((bf16[64,2,512]{2,1,0:T(2,128)(2,1)}), bf16[64,2,512]{2,1,0:T(2,128)(2,1)S(1)}, u32[]{:S(2)}, u32[]{:S(2)}) %all-to-all-start) | async-done | bytes 131104 | tf_op jit(solution)/shard_map/all_to_all | solution.py:219
  35.4 0.0 collective-permute-done.1.refs_1_
  35.4 2.1 %collective-permute-start.3 = (bf16[512,1024]{1,0:T(8,128)(2,1)}, bf16[512,1024]{1,0:T(8,128)(2,1)}, u32[]{:S(2)}, u32[]{:S(2)}) collective-permute-start(bf16[512,1024]{1,0:T(8,128)(2,1)} %collective-permute-done.1.refs_1_), channel_id=1, source_target_pairs={{0,2},{1,7},{2,4},{3,1},{4,6},{5,3},{6,0},{7,5},{8,10},{9,15},{10,... | collective-permute-start | bytes 3145736 | tf_op jit(solution)/shard_map/ppermute | solution.py:233
  37.5 2.3 %shard_map.74 = bf16[256,2,384]{2,1,0:T(2,128)(2,1)} custom-call(s32[64,8]{1,0:T(8,128)S(1)} %bitcast.18, bf16[64,2,512]{2,1,0:T(2,128)(2,1)S(1)} %all-to-all-done.table_ref), custom_call_target="tpu_custom_call" | custom-call | tf_op jit(solution)/shard_map/pallas_call | solution.py:236
  39.8 9.7 %all-to-all-start.1 = ((bf16[256,2,384]{2,1,0:T(2,128)(2,1)}), bf16[256,2,384]{2,1,0:T(2,128)(2,1)S(1)}, u32[]{:S(2)}, u32[]{:S(2)}) async-start(bf16[256,2,384]{2,1,0:T(2,128)(2,1)} %shard_map.74), calls=%async_computation.1 | async-start | bytes 786432 | tf_op jit(solution)/shard_map/all_to_all | solution.py:243
  49.5 0.0 copy-done.1
  49.5 4.2 %collective-permute-start.4 = (bf16[512,1024]{1,0:T(8,128)(2,1)S(1)}, bf16[512,1024]{1,0:T(8,128)(2,1)}, u32[]{:S(2)}, u32[]{:S(2)}) collective-permute-start(bf16[512,1024]{1,0:T(8,128)(2,1)S(1)} %bitcast.15), channel_id=1, source_target_pairs={{0,1},{1,0},{2,3},{3,2},{4,5},{5,4},{6,7},{7,6},{8,9},{9,8},{10,11... | collective-permute-start | bytes 3145736 | tf_op jit(solution)/shard_map/ppermute | solution.py:246
  53.7 1.9 %collective-permute-start.5 = (bf16[512,1024]{1,0:T(8,128)(2,1)}, bf16[512,1024]{1,0:T(8,128)(2,1)}, u32[]{:S(2)}, u32[]{:S(2)}) collective-permute-start(bf16[512,1024]{1,0:T(8,128)(2,1)} %collective-permute-done.1.refs_1_), channel_id=1, source_target_pairs={{0,1},{1,0},{2,3},{3,2},{4,5},{5,4},{6,7},{7,6},{8,9},{9,8},{10,11... | collective-permute-start | bytes 3145736 | tf_op jit(solution)/shard_map/ppermute | solution.py:246
  55.6 0.0 collective-permute-done.2.refs_2_
  55.7 2.4 %collective-permute-start.6 = (bf16[512,1024]{1,0:T(8,128)(2,1)}, bf16[512,1024]{1,0:T(8,128)(2,1)}, u32[]{:S(2)}, u32[]{:S(2)}) collective-permute-start(bf16[512,1024]{1,0:T(8,128)(2,1)} %collective-permute-done.2.refs_2_), channel_id=1, source_target_pairs={{0,1},{1,0},{2,3},{3,2},{4,5},{5,4},{6,7},{7,6},{8,9},{9,8},{10,11... | collective-permute-start | bytes 3145736 | tf_op jit(solution)/shard_map/ppermute | solution.py:246
  58.1 0.0 collective-permute-done.3.refs_3_
  58.1 1.9 %collective-permute-start.7 = (bf16[512,1024]{1,0:T(8,128)(2,1)}, bf16[512,1024]{1,0:T(8,128)(2,1)}, u32[]{:S(2)}, u32[]{:S(2)}) collective-permute-start(bf16[512,1024]{1,0:T(8,128)(2,1)} %collective-permute-done.3.refs_3_), channel_id=1, source_target_pairs={{0,1},{1,0},{2,3},{3,2},{4,5},{5,4},{6,7},{7,6},{8,9},{9,8},{10,11... | collective-permute-start | bytes 3145736 | tf_op jit(solution)/shard_map/ppermute | solution.py:246
  60.0 2.9 %all-to-all-done.1.own_ref = bf16[256,2,384]{2,1,0:T(2,128)(2,1)S(1)} async-done(((bf16[256,2,384]{2,1,0:T(2,128)(2,1)}), bf16[256,2,384]{2,1,0:T(2,128)(2,1)S(1)}, u32[]{:S(2)}, u32[]{:S(2)}) %all-to-all-start.1) | async-done | bytes 393248 | tf_op jit(solution)/shard_map/all_to_all | solution.py:243
  62.9 7.0 %collective-permute-start = (bf16[256,2,384]{2,1,0:T(2,128)(2,1)S(1)}, bf16[256,2,384]{2,1,0:T(2,128)(2,1)S(1)}, u32[]{:S(2)}, u32[]{:S(2)}) collective-permute-start(bf16[256,2,384]{2,1,0:T(2,128)(2,1)S(1)} %all-to-all-done.1.own_ref), channel_id=1, source_target_pairs={{0,1},{1,0},{2,3},{3,2},{4,5},{5,4},{6,7},{7,6},{8,9},{9,8},{10,11... | collective-permute-start | bytes 1179656 | tf_op jit(solution)/shard_map/ppermute | solution.py:247
  69.9 0.0 collective-permute-done.4.refs_4_
  69.9 1.3 %collective-permute-done.other_ref = bf16[256,2,384]{2,1,0:T(2,128)(2,1)S(1)} collective-permute-done((bf16[256,2,384]{2,1,0:T(2,128)(2,1)S(1)}, bf16[256,2,384]{2,1,0:T(2,128)(2,1)S(1)}, u32[]{:S(2)}, u32[]{:S(2)}) %collective-permute-start) | collective-permute-done | bytes 393248 | tf_op jit(solution)/shard_map/ppermute | solution.py:247
  71.2 0.0 collective-permute-done.6.refs_6_
  71.2 0.0 collective-permute-done.5.refs_5_
  71.2 0.0 collective-permute-done.7.refs_7_
  71.2 0.0 copy-done.2
  71.2 0.0 copy-done.3
  71.2 0.0 copy-done.4
  71.2 11.7 %shard_map.75 = bf16[720,128]{1,0:T(8,128)(2,1)S(1)} custom-call(s32[2,4]{1,0:T(2,128)S(1)} %bitcast.20, f32[64,96]{1,0:T(8,128)S(1)} %copy-done.2, f32[64,96]{1,0:T(8,128)S(1)} %copy-done.3, bf16[256,2,384]{2,1,0:T(2,128)(2,1)S(1)} %all-to-all-done.1.own_ref, bf16[256,2,384]{2,1,0:T(2,128)(2,1)S(1)} %collective-permute-done.other_ref, ...), custom_call_target="tpu_custom_call" | custom-call | tf_op jit(solution)/shard_map/pallas_call | solution.py:249
  82.9 10.8 %all_gather.3 = bf16[4,10,72,128]{3,2,1,0:T(8,128)(2,1)S(1)} all-gather(bf16[1,10,72,128]{3,2,1,0:T(8,128)(2,1)S(1)} %bitcast.17), channel_id=1, replica_groups=mesh['pb'=64,'row'=4,'col'=2] {'row'}, dimensions={0}, use_global_device_ids=true | all-gather | bytes 921600 | tf_op jit(solution)/shard_map/all_gather | solution.py:269
  93.7 5.5 %collective-permute-start.8 = (bf16[4,10,72,128]{3,2,1,0:T(8,128)(2,1)S(1)}, bf16[4,10,72,128]{3,2,1,0:T(8,128)(2,1)S(1)}, u32[]{:S(2)}, u32[]{:S(2)}) collective-permute-start(bf16[4,10,72,128]{3,2,1,0:T(8,128)(2,1)S(1)} %all_gather.3), channel_id=1, source_target_pairs={{0,1},{1,0},{2,3},{3,2},{4,5},{5,4},{6,7},{7,6},{8,9},{9,8},{10,11... | collective-permute-start | bytes 2211848 | tf_op jit(solution)/shard_map/ppermute | solution.py:270
  99.2 1.8 %collective-permute-done.8 = bf16[4,10,72,128]{3,2,1,0:T(8,128)(2,1)S(1)} collective-permute-done((bf16[4,10,72,128]{3,2,1,0:T(8,128)(2,1)S(1)}, bf16[4,10,72,128]{3,2,1,0:T(8,128)(2,1)S(1)}, u32[]{:S(2)}, u32[]{:S(2)}) %collective-permute-start.8) | collective-permute-done | bytes 737312 | tf_op jit(solution)/shard_map/ppermute | solution.py:270
  101.0 0.2 fusion
  101.3 0.1 copy.10
  101.4 1.3 %reshape.15 = bf16[1,20,4,9216]{3,2,1,0:T(4,128)(2,1)} reshape(bf16[2,10,4,72,128]{4,3,2,1,0:T(8,128)(2,1)S(1)} %copy.10) | data formatting | bytes 2949120 | tf_op jit(solution)/shard_map/reshape | solution.py:272
  (1 shorter events, 0.0 us)
Async XLA Ops:
  0.0 25.4 %copy-start = (bf16[1,20,4,9216]{3,2,1,0:T(4,128)(2,1)S(1)}, bf16[1,20,4,9216]{3,2,1,0:T(4,128)(2,1)}, u32[]{:S(2)}) copy-start(bf16[1,20,4,9216]{3,2,1,0:T(4,128)(2,1)} %param.7) | copy-start | bytes 4423684
  1.8 47.7 %copy-start.1 = (bf16[1,512,1024]{2,1,0:T(8,128)(2,1)S(1)}, bf16[1,512,1024]{2,1,0:T(8,128)(2,1)}, u32[]{:S(2)}) copy-start(bf16[1,512,1024]{2,1,0:T(8,128)(2,1)} %param.13) | copy-start | bytes 3145732
  1.8 69.4 %copy-start.2 = (f32[64,96]{1,0:T(8,128)S(1)}, f32[64,96]{1,0:T(8,128)}, u32[]{:S(2)}) copy-start(f32[64,96]{1,0:T(8,128)} %low_ref.1) | copy-start | bytes 73732
  1.8 69.4 %copy-start.3 = (f32[64,96]{1,0:T(8,128)S(1)}, f32[64,96]{1,0:T(8,128)}, u32[]{:S(2)}) copy-start(f32[64,96]{1,0:T(8,128)} %high_ref.1) | copy-start | bytes 73732
  1.8 69.4 %copy-start.4 = (s32[1,4,2]{1,2,0:T(2,128)S(1)}, s32[1,4,2]{1,2,0:T(2,128)}, u32[]{:S(2)}) copy-start(s32[1,4,2]{1,2,0:T(2,128)} %param.8) | copy-start | bytes 100
  1.8 33.5 %collective-permute-start.1 = (bf16[512,1024]{1,0:T(8,128)(2,1)}, bf16[512,1024]{1,0:T(8,128)(2,1)}, u32[]{:S(2)}, u32[]{:S(2)}) collective-permute-start(bf16[512,1024]{1,0:T(8,128)(2,1)} %bitcast.13), channel_id=1, source_target_pairs={{0,2},{1,7},{2,4},{3,1},{4,6},{5,3},{6,0},{7,5},{8,10},{9,15},{10,... | collective-permute-start | bytes 3145736 | tf_op jit(solution)/shard_map/ppermute | solution.py:228
  7.2 28.2 %all-to-all-start = ((bf16[64,2,512]{2,1,0:T(2,128)(2,1)}), bf16[64,2,512]{2,1,0:T(2,128)(2,1)S(1)}, u32[]{:S(2)}, u32[]{:S(2)}) async-start(bf16[64,2,512]{2,1,0:T(2,128)(2,1)} %shard_map.73), calls=%async_computation | async-start | bytes 262144 | tf_op jit(solution)/shard_map/all_to_all | solution.py:219
  23.5 32.2 %collective-permute-start.2 = (bf16[512,1024]{1,0:T(8,128)(2,1)}, bf16[512,1024]{1,0:T(8,128)(2,1)}, u32[]{:S(2)}, u32[]{:S(2)}) collective-permute-start(bf16[512,1024]{1,0:T(8,128)(2,1)} %bitcast.14), channel_id=1, source_target_pairs={{2,0},{7,1},{4,2},{1,3},{6,4},{3,5},{0,6},{5,7},{10,8},{15,9},{12,... | collective-permute-start | bytes 3145736 | tf_op jit(solution)/shard_map/ppermute | solution.py:229
  35.4 22.7 %collective-permute-start.3 = (bf16[512,1024]{1,0:T(8,128)(2,1)}, bf16[512,1024]{1,0:T(8,128)(2,1)}, u32[]{:S(2)}, u32[]{:S(2)}) collective-permute-start(bf16[512,1024]{1,0:T(8,128)(2,1)} %collective-permute-done.1.refs_1_), channel_id=1, source_target_pairs={{0,2},{1,7},{2,4},{3,1},{4,6},{5,3},{6,0},{7,5},{8,10},{9,15},{10,... | collective-permute-start | bytes 3145736 | tf_op jit(solution)/shard_map/ppermute | solution.py:233
  39.8 23.1 %all-to-all-start.1 = ((bf16[256,2,384]{2,1,0:T(2,128)(2,1)}), bf16[256,2,384]{2,1,0:T(2,128)(2,1)S(1)}, u32[]{:S(2)}, u32[]{:S(2)}) async-start(bf16[256,2,384]{2,1,0:T(2,128)(2,1)} %shard_map.74), calls=%async_computation.1 | async-start | bytes 786432 | tf_op jit(solution)/shard_map/all_to_all | solution.py:243
  49.5 20.3 %collective-permute-start.4 = (bf16[512,1024]{1,0:T(8,128)(2,1)S(1)}, bf16[512,1024]{1,0:T(8,128)(2,1)}, u32[]{:S(2)}, u32[]{:S(2)}) collective-permute-start(bf16[512,1024]{1,0:T(8,128)(2,1)S(1)} %bitcast.15), channel_id=1, source_target_pairs={{0,1},{1,0},{2,3},{3,2},{4,5},{5,4},{6,7},{7,6},{8,9},{9,8},{10,11... | collective-permute-start | bytes 3145736 | tf_op jit(solution)/shard_map/ppermute | solution.py:246
  53.7 17.5 %collective-permute-start.5 = (bf16[512,1024]{1,0:T(8,128)(2,1)}, bf16[512,1024]{1,0:T(8,128)(2,1)}, u32[]{:S(2)}, u32[]{:S(2)}) collective-permute-start(bf16[512,1024]{1,0:T(8,128)(2,1)} %collective-permute-done.1.refs_1_), channel_id=1, source_target_pairs={{0,1},{1,0},{2,3},{3,2},{4,5},{5,4},{6,7},{7,6},{8,9},{9,8},{10,11... | collective-permute-start | bytes 3145736 | tf_op jit(solution)/shard_map/ppermute | solution.py:246
  55.7 15.5 %collective-permute-start.6 = (bf16[512,1024]{1,0:T(8,128)(2,1)}, bf16[512,1024]{1,0:T(8,128)(2,1)}, u32[]{:S(2)}, u32[]{:S(2)}) collective-permute-start(bf16[512,1024]{1,0:T(8,128)(2,1)} %collective-permute-done.2.refs_2_), channel_id=1, source_target_pairs={{0,1},{1,0},{2,3},{3,2},{4,5},{5,4},{6,7},{7,6},{8,9},{9,8},{10,11... | collective-permute-start | bytes 3145736 | tf_op jit(solution)/shard_map/ppermute | solution.py:246
  58.1 13.1 %collective-permute-start.7 = (bf16[512,1024]{1,0:T(8,128)(2,1)}, bf16[512,1024]{1,0:T(8,128)(2,1)}, u32[]{:S(2)}, u32[]{:S(2)}) collective-permute-start(bf16[512,1024]{1,0:T(8,128)(2,1)} %collective-permute-done.3.refs_3_), channel_id=1, source_target_pairs={{0,1},{1,0},{2,3},{3,2},{4,5},{5,4},{6,7},{7,6},{8,9},{9,8},{10,11... | collective-permute-start | bytes 3145736 | tf_op jit(solution)/shard_map/ppermute | solution.py:246
  62.9 8.3 %collective-permute-start = (bf16[256,2,384]{2,1,0:T(2,128)(2,1)S(1)}, bf16[256,2,384]{2,1,0:T(2,128)(2,1)S(1)}, u32[]{:S(2)}, u32[]{:S(2)}) collective-permute-start(bf16[256,2,384]{2,1,0:T(2,128)(2,1)S(1)} %all-to-all-done.1.own_ref), channel_id=1, source_target_pairs={{0,1},{1,0},{2,3},{3,2},{4,5},{5,4},{6,7},{7,6},{8,9},{9,8},{10,11... | collective-permute-start | bytes 1179656 | tf_op jit(solution)/shard_map/ppermute | solution.py:247
  93.7 7.3 %collective-permute-start.8 = (bf16[4,10,72,128]{3,2,1,0:T(8,128)(2,1)S(1)}, bf16[4,10,72,128]{3,2,1,0:T(8,128)(2,1)S(1)}, u32[]{:S(2)}, u32[]{:S(2)}) collective-permute-start(bf16[4,10,72,128]{3,2,1,0:T(8,128)(2,1)S(1)} %all_gather.3), channel_id=1, source_target_pairs={{0,1},{1,0},{2,3},{3,2},{4,5},{5,4},{6,7},{7,6},{8,9},{9,8},{10,11... | collective-permute-start | bytes 2211848 | tf_op jit(solution)/shard_map/ppermute | solution.py:270
